TPU v7x, 128 devices: a whole 4x4x4 slice. The times are simulated.
128 devices in a mesh: stream: 4 (over z), tile: 32 (over y, x, core).
Axes of the slice: x: 4, y: 4, z: 4, core: 2. Of those that a mesh axis runs over, the one named last changes fastest.
Arguments:
- enthalpy: float32 [64, 64, 4096], P('stream', None, 'tile'), may hold values from -6 to 6
- velocity: float32 [64, 64, 4096], P('stream', None, 'tile'), may hold values from 0.05 to 0.35
- diffusivity: float32 [64, 64, 4096], P('stream', None, 'tile'), may hold values from 0.02 to 0.1
- wall_flux: float32 [64, 4096], P('stream', 'tile'), may hold values from 0.05 to 0.5
- profiles: float32 [64, 2097152], P(None, ('stream', 'tile')), may hold values from -6 to 6
- counts: int32 [128], P(('stream', 'tile')), may hold values from 1 to 16384, as said below
- owners: int32 [2097152], P(('stream', 'tile')), may hold values from 0 to 196607, as said below
- cells: int32 [2097152], P(('stream', 'tile')), may hold values from 0 to 131071, as said below
- radial_step: float32 [64, 64], replicated, may hold values from -1 to 1
- far_weights: float32 [64], replicated, may hold values from 0.05 to 0.3
- flux_weights: float32 [64], replicated, may hold values from -0.75 to 0.75
Outputs:
- new_enthalpy: float32 [64, 64, 4096], P('stream', None, 'tile')
- new_profiles: float32 [64, 786432], P(None, ('stream', 'tile'))
Inputs may be any that keep to these rules, and one draw needn't show every extreme that they name: A tile's live bubbles fill its first counts slots; the counts of one group sum to 196608. `owners`: over the live slots of one group the entries are distinct and cover all 196608 balanced slots; entry // 6144 is the tile index of the device that holds the balanced slot, entry % 6144 the slot there. No tile has more than 512 live bubbles whose entries lie on one device. Entries of slots that are not live are arbitrary. `cells`: the cell's index (x * 64 + w) * 128 + s inside the home tile.
All inputs are finite; a program needn't handle non-finite values.
Results may differ from a plain program's by a relative error of at most 0.0001.
Values sent between devices are 32-bit elements; how exact they have to be, the bound alone decides.
No kernel may reach another device: no remote copies, remote signals or barrier semaphores. Data moves between devices by JAX's collectives and lax.ppermute only.
A program may use at most 128 MiB of HBM per device.

v0:
```python
import jax
import jax.numpy as jnp
from jax import lax
from jax.sharding import PartitionSpec as P

SUB = 16


latent_share = 0.5


def with_halo(cells, sides, width, closed):
    for axis, dim in sides:
        count = lax.axis_size(axis)
        ends = count if closed else count - 1
        head = lax.slice_in_dim(cells, 0, width, axis=dim)
        tail = lax.slice_in_dim(cells, cells.shape[dim] - width, cells.shape[dim], axis=dim)
        cells = jnp.concatenate(
            [
                lax.ppermute(tail, axis, [(i, (i + 1) % count) for i in range(ends)]),
                cells,
                lax.ppermute(head, axis, [((i + 1) % count, i) for i in range(ends)]),
            ],
            axis=dim,
        )
    return cells


def advance(radial_step, far_weights, flux_weights, profile_state, far_temp):

    def substep(substep_index, carried):
        current, heat_rate = carried
        current = (
            jnp.dot(
                radial_step,
                current,
                precision=lax.Precision.HIGHEST,
                preferred_element_type=jnp.float32,
            )
            + far_weights[:, None] * far_temp[None, :]
            + 0.25 * jnp.tanh(current)
        )
        heat_rate = heat_rate + jnp.dot(
            flux_weights,
            current,
            precision=lax.Precision.HIGHEST,
            preferred_element_type=jnp.float32,
        )
        return (current, heat_rate)

    start_heat = jnp.zeros(far_temp.shape, jnp.float32)
    current, heat_rate = lax.fori_loop(0, SUB, substep, (profile_state, start_heat))
    return (current, heat_rate / SUB)


def stencil(enthalpy, x_lower, x_upper, s_lower, s_upper, velocity, diffusivity, wall_flux):
    wall_low = jnp.concatenate([enthalpy[:, :1], enthalpy[:, :-1]], axis=1)
    wall_high = jnp.concatenate([enthalpy[:, 1:], enthalpy[:, -1:]], axis=1)
    laplace = x_lower + x_upper + (wall_low + wall_high) + (s_lower + s_upper) - 6.0 * enthalpy
    stepped = enthalpy + diffusivity * laplace - velocity * (enthalpy - x_lower)
    return stepped.at[:, 0, :].add(wall_flux)


def on_device(
    enthalpy,
    velocity,
    diffusivity,
    wall_flux,
    profiles,
    counts,
    owners,
    cells,
    radial_step,
    far_weights,
    flux_weights,
):
    peer_count = lax.axis_size("tile")
    capacity = owners.shape[0]
    message = capacity // peer_count
    owned_slots = 3 * capacity // 8
    slot_total = peer_count * message
    points = profiles.shape[0]
    is_live = jnp.arange(capacity, dtype=jnp.int32) < counts[0]
    far_home = enthalpy.reshape(-1)[cells]
    target = jnp.where(is_live, owners // owned_slots, peer_count)
    within = owners % owned_slots
    onehot = (target[:, None] == jnp.arange(peer_count, dtype=jnp.int32)[None, :]).astype(jnp.int32)
    before = jnp.cumsum(onehot, axis=0) - onehot
    message_rank = jnp.sum(before * onehot, axis=1)
    send_place = jnp.where(is_live, target * message + message_rank, slot_total)
    slot_row = (
        jnp.full((slot_total,), -1.0, jnp.float32)
        .at[send_place]
        .set(within.astype(jnp.float32), mode="drop")
    )
    send_rows = (
        jnp.zeros((points, slot_total), jnp.float32).at[:, send_place].set(profiles, mode="drop")
    )
    send_far = jnp.zeros((slot_total,), jnp.float32).at[send_place].set(far_home, mode="drop")
    side_rows = jnp.stack([send_far, slot_row])
    got_rows, got_side = (
        lax.all_to_all(send_rows, "tile", split_axis=1, concat_axis=1, tiled=True),
        lax.all_to_all(side_rows, "tile", split_axis=1, concat_axis=1, tiled=True),
    )
    arrived = got_side[1].astype(jnp.int32)
    landing = jnp.where(arrived >= 0, arrived, owned_slots)
    start_rows = (
        jnp.zeros((points, owned_slots), jnp.float32).at[:, landing].set(got_rows, mode="drop")
    )
    start_far = jnp.zeros((owned_slots,), jnp.float32).at[landing].set(got_side[0], mode="drop")
    final_state, heat_rate = advance(radial_step, far_weights, flux_weights, start_rows, start_far)
    reply_heat = jnp.where(arrived >= 0, heat_rate[jnp.minimum(landing, owned_slots - 1)], 0.0)
    returned = lax.all_to_all(reply_heat, "tile", split_axis=0, concat_axis=0, tiled=True)
    heat_home = jnp.where(is_live, returned[jnp.minimum(send_place, slot_total - 1)], 0.0)
    x_padded = with_halo(enthalpy, (("stream", 0),), 1, False)
    s_padded = with_halo(enthalpy, (("tile", 2),), 1, True)
    stepped = stencil(
        enthalpy,
        x_padded[:-2],
        x_padded[2:],
        s_padded[..., :-2],
        s_padded[..., 2:],
        velocity,
        diffusivity,
        wall_flux,
    )
    new_enthalpy = (
        stepped.reshape(-1).at[cells].add(latent_share * heat_home).reshape(stepped.shape)
    )
    return (new_enthalpy, final_state)


def solution(mesh):
    return jax.shard_map(
        on_device,
        mesh=mesh,
        in_specs=(
            P("stream", None, "tile"),
            P("stream", None, "tile"),
            P("stream", None, "tile"),
            P("stream", "tile"),
            P(None, ("stream", "tile")),
            P(("stream", "tile")),
            P(("stream", "tile")),
            P(("stream", "tile")),
            P(),
            P(),
            P(),
        ),
        out_specs=(P("stream", None, "tile"), P(None, ("stream", "tile"))),
        check_vma=False,
    )
```

profile of v0, /device:TPU:35, one launch (start us, length us, event | category | flops | bytes accessed | tf_op | source)
XLA Modules:
  0.0 752.8 jit_solution(3607493439665662514)
XLA Ops:
  4.5 2.0 copy.43
  9.0 90.5 %gather_fusion = f32[16384]{0:T(1024)S(1)} fusion(f32[131072]{0:T(1024)S(1)} %bitcast.64, s32[16384]{0:T(1024)S(1)} %get-tuple-element.134), kind=kCustom, calls=%fused_computation | custom fusion | bytes 196608 | tf_op jit(solution)/shard_map/gather | solution.py:84
  99.5 60.3 %scatter_custom_fusion.1 = f32[16384]{0:T(1024)S(1)} fusion(s32[16384]{0:T(1024)S(1)} %get-tuple-element.129, f32[16384]{0:T(1024)S(1)} %get-tuple-element.136, f32[]{:T(128)} %constant.82.clone.1), kind=kCustom, calls=%fused_computation.66 | custom fusion | bytes 65540 | tf_op jit(solution)/shard_map/scatter | solution.py:94
  159.9 60.3 %scatter_custom_fusion = f32[16384]{0:T(1024)S(1)} fusion(s32[16384]{0:T(1024)S(1)} %get-tuple-element.129, f32[16384]{0:T(1024)S(1)} %gather_fusion, f32[]{:T(128)} %constant.75.clone.1), kind=kCustom, calls=%fused_computation.68 | custom fusion | bytes 65540 | tf_op jit(solution)/shard_map/scatter | solution.py:99
  221.0 7.9 %all-to-all-start = ((f32[2,32,512]{2,0,1:T(2,128)}), f32[2,32,512]{2,0,1:T(2,128)S(1)}, u32[]{:S(2)}, u32[]{:S(2)}) async-start(f32[2,32,512]{2,0,1:T(2,128)} %pad_maximum_fusion.4), calls=%async_computation | async-start | bytes 262144 | tf_op jit(solution)/shard_map/all_to_all | solution.py:103
  230.7 3.5 collective-permute-start
  234.2 1.9 collective-permute-start.1
  236.3 6.9 copy.45
  243.1 44.4 %scatter_custom_fusion.2 = f32[64,16384]{0,1:T(8,128)} fusion(s32[16384]{0:T(1024)S(1)} %get-tuple-element.129, f32[16384,64]{1,0:T(8,128)} %copy.45, f32[]{:T(128)} %constant.75.clone.1), kind=kCustom, calls=%fused_computation.14 | custom fusion | bytes 4194816 | tf_op jit(solution)/shard_map/scatter | solution.py:97
  287.5 6.9 copy.46
  294.4 1.9 fusion.18
  296.3 8.7 %all-to-all-start.1 = ((f32[64,32,512]{2,0,1:T(8,128)}), f32[64,32,512]{2,0,1:T(8,128)}, u32[]{:S(2)}, u32[]{:S(2)}) async-start(f32[64,32,512]{2,0,1:T(8,128)} %copy.46), calls=%async_computation.1 | async-start | bytes 8388608 | tf_op jit(solution)/shard_map/all_to_all | solution.py:102
  305.4 60.4 %scatter_custom_fusion.4 = f32[6144]{0:T(1024)S(1)} fusion(s32[16384]{0:T(1024)S(1)} %bitcast.77, f32[16384]{0:T(1024)S(1)} %bitcast.79, f32[]{:T(128)} %constant.75.clone.1), kind=kCustom, calls=%fused_computation.72 | custom fusion | bytes 24580 | tf_op jit(solution)/shard_map/scatter | solution.py:110
  365.8 4.8 copy.52
  370.5 6.9 copy.48
  377.4 42.6 %scatter_custom_fusion.3 = f32[64,6144]{0,1:T(8,128)} fusion(s32[16384]{0:T(1024)S(1)} %bitcast.78, f32[16384,64]{1,0:T(8,128)} %copy.48, f32[]{:T(128)} %constant.75.clone.1), kind=kCustom, calls=%fused_computation.24 | custom fusion | bytes 1573376 | tf_op jit(solution)/shard_map/scatter | solution.py:108
  420.1 2.4 copy.49
  422.5 45.8 %while.14 = (s32[]{:T(128)}, f32[64,6144]{1,0:T(8,128)S(1)}, f32[6144]{0:T(1024)S(1)}, f32[64,64]{1,0:T(8,128)S(1)}, f32[64]{0:T(128)S(1)}, /*index=5*/f32[6144]{0:T(1024)S(1)}, f32[64]{0:T(128)S(1)}, s32[]{:T(128)}, s32[]{:T(128)}) while((s32[]{:T(128)}, f32[64,6144]{1,0:T(8,128)S(1)}, f32[6144]{0:T(1024)S(1)}, ...), condition=%wide.region_9.10_spmd.clone, body=%wide.region_8.9_spmd.clone.sunk | while | flops 308293632 | bytes 8004199 | solution.py:52
  428.3 1.8 fusion.52
  431.2 1.8 fusion.52
  439.8 1.8 fusion.52
  442.7 1.8 fusion.52
  445.5 1.8 fusion.52
  448.4 1.8 fusion.52
  451.2 1.8 fusion.52
  454.1 1.8 fusion.52
  465.6 1.8 fusion.52
  468.4 90.5 %gather_fusion.1 = f32[16384]{0:T(1024)S(1)} fusion(f32[6144]{0:T(1024)S(1)} %broadcast_multiply_fusion, s32[16384]{0:T(1024)S(1)} %broadcast_clamp_fusion), kind=kCustom, calls=%fused_computation.1 | custom fusion | bytes 196608 | tf_op jit(solution)/shard_map/gather | solution.py:112
  559.6 7.5 all-to-all-start.2
  567.2 6.2 all-to-all-done.2
  573.4 90.5 %gather_fusion.2 = f32[16384]{0:T(1024)S(1)} fusion(f32[16384]{0:T(1024)S(1)} %bitcast.63, s32[16384]{0:T(1024)S(1)} %copy-done.5), kind=kCustom, calls=%fused_computation.2 | custom fusion | bytes 196608 | tf_op jit(solution)/shard_map/gather | solution.py:114
  664.0 88.0 %scatter_fusion = f32[131072]{0:T(1024)S(1)} fusion(f32[131072]{0:T(1024)S(1)} %bitcast.65, s32[16384]{0:T(1024)S(1)} %get-tuple-element.135, f32[16384]{0:T(1024)S(1)} %select_multiply_fusion), kind=kCustom, calls=%fused_computation.8 | custom fusion | flops 16384 | bytes 262144 | tf_op jit(solution)/shard_map/scatter-add | solution.py:128
  (111 shorter events, 39.2 us)
Async XLA Ops:
  6.5 1.8 copy-start.6
  6.5 2.5 copy-start
  221.0 75.3 %all-to-all-start = ((f32[2,32,512]{2,0,1:T(2,128)}), f32[2,32,512]{2,0,1:T(2,128)S(1)}, u32[]{:S(2)}, u32[]{:S(2)}) async-start(f32[2,32,512]{2,0,1:T(2,128)} %pad_maximum_fusion.4), calls=%async_computation | async-start | bytes 262144 | tf_op jit(solution)/shard_map/all_to_all | solution.py:103
  229.1 65.2 %collective-permute-start.2 = (f32[16,64,1]{2,1,0:T(8,128)S(1)}, f32[16,64,1]{2,1,0:T(8,128)}, u32[]{:S(2)}, u32[]{:S(2)}) collective-permute-start(f32[16,64,1]{2,1,0:T(8,128)S(1)} %get-tuple-element.126), channel_id=1, source_target_pairs={{0,1},{1,2},{2,3},{3,4},{4,5},{5,6},{6,7},{7,8},{8,9},{9,10},{10,1... | collective-permute-start | bytes 12296 | tf_op jit(solution)/shard_map/ppermute | solution.py:20
  230.6 63.7 %collective-permute-start.3 = (f32[16,64,1]{2,1,0:T(8,128)S(1)}, f32[16,64,1]{2,1,0:T(8,128)}, u32[]{:S(2)}, u32[]{:S(2)}) collective-permute-start(f32[16,64,1]{2,1,0:T(8,128)S(1)} %get-tuple-element.127), channel_id=1, source_target_pairs={{1,0},{2,1},{3,2},{4,3},{5,4},{6,5},{7,6},{8,7},{9,8},{10,9},{11,1... | collective-permute-start | bytes 12296 | tf_op jit(solution)/shard_map/ppermute | solution.py:22
  230.7 63.7 %collective-permute-start = (f32[1,64,128]{2,1,0:T(8,128)S(1)}, f32[1,64,128]{2,1,0:T(8,128)S(1)}, u32[]{:S(2)}, u32[]{:S(2)}) collective-permute-start(f32[1,64,128]{2,1,0:T(8,128)S(1)} %get-tuple-element.124), channel_id=1, source_target_pairs={{0,32},{32,64},{64,96},{1,33},{33,65},{65,97},{2,34},{34,66},{66,9... | collective-permute-start | bytes 98312 | tf_op jit(solution)/shard_map/ppermute | solution.py:20
  234.2 60.2 %collective-permute-start.1 = (f32[1,64,128]{2,1,0:T(8,128)S(1)}, f32[1,64,128]{2,1,0:T(8,128)S(1)}, u32[]{:S(2)}, u32[]{:S(2)}) collective-permute-start(f32[1,64,128]{2,1,0:T(8,128)S(1)} %get-tuple-element.125), channel_id=1, source_target_pairs={{32,0},{64,32},{96,64},{33,1},{65,33},{97,65},{34,2},{66,34},{98,6... | collective-permute-start | bytes 98312 | tf_op jit(solution)/shard_map/ppermute | solution.py:22
  287.5 6.9 copy-start.4
  296.3 69.5 %all-to-all-start.1 = ((f32[64,32,512]{2,0,1:T(8,128)}), f32[64,32,512]{2,0,1:T(8,128)}, u32[]{:S(2)}, u32[]{:S(2)}) async-start(f32[64,32,512]{2,0,1:T(8,128)} %copy.46), calls=%async_computation.1 | async-start | bytes 8388608 | tf_op jit(solution)/shard_map/all_to_all | solution.py:102
  420.1 2.4 copy-start.3
  420.1 2.4 copy-start.7
  420.1 2.4 copy-start.8
  468.3 90.6 %copy-start.2 = (f32[64,6144]{1,0:T(8,128)}, f32[64,6144]{1,0:T(8,128)S(1)}, u32[]{:S(2)}) copy-start(f32[64,6144]{1,0:T(8,128)S(1)} %get-tuple-element.51) | copy-start | bytes 4718596
  468.3 98.8 %copy-start.9 = (f32[16,128]{1,0:T(8,128)S(1)}, f32[16,128]{1,0:T(8,128)}, u32[]{:S(2)}) copy-start(f32[16,128]{1,0:T(8,128)} %param.18) | copy-start | bytes 24580
  468.3 105.1 %copy-start.5 = (s32[16384]{0:T(1024)S(1)}, s32[16384]{0:T(1024)}, u32[]{:S(2)}) copy-start(s32[16384]{0:T(1024)} %get-tuple-element.128) | copy-start | bytes 196612
  559.6 13.7 %all-to-all-start.2 = ((f32[32,512,1]{1,2,0:T(1,128)}), f32[32,512,1]{1,2,0:T(1,128)S(1)}, u32[]{:S(2)}, u32[]{:S(2)}) async-start(f32[32,512,1]{1,2,0:T(1,128)} %copy.50), calls=%async_computation.2 | async-start | bytes 131072 | tf_op jit(solution)/shard_map/all_to_all | solution.py:113
  752.0 0.8 copy-start.1
where the time goes:
time: 755 us; the launch traced here: 753 us
  local copies, waits for them, and re-layouts  573 us (76%)
  other arithmetic  96.5 us (13%)
  matrix products  43.3 us (6%)
  starting transfers between devices  31.1 us (4%)
    gather x2, local copies, waits for them, and re-layouts, on_device(): heat_rate[jnp.minimum(landing, owned_slots - 1)]  90.5 us
    gather x1, local copies, waits for them, and re-layouts, on_device(): returned[jnp.minimum(send_place, slot_total - 1)]  90.5 us
    gather x1, local copies, waits for them, and re-layouts, on_device(): far_home = enthalpy.reshape(-1)[cells]  90.5 us
    scatter-add x1, other arithmetic, on_device(): stepped.reshape(-1).at[cells].add(latent_share * heat_home)  88 us
    scatter x1, local copies, waits for them, and re-layouts, on_device(): jnp.zeros((owned_slots,), jnp.float32).at[landing]  60.4 us
    scatter x1, local copies, waits for them, and re-layouts, on_device(): slot_row = jnp.full((slot_total,), -1.0, jnp.float32).at[send_place].set(...  60.3 us
    scatter x1, local copies, waits for them, and re-layouts, on_device(): jnp.zeros((slot_total,), jnp.float32).at[send_place]  60.3 us
    scatter x1, local copies, waits for them, and re-layouts, on_device(): jnp.zeros((points, slot_total), jnp.float32).at[:, send_place]  44.4 us
  transfers between devices with their start and end apart: 7, of which 1 were waited for; matrix products, arithmetic and copies ran while one was open for 16% of the time, Pallas kernels for 0%

commit v1 on v0

v1 whole, which is shorter than its diff:
```python
import jax
import jax.numpy as jnp
from jax import lax
from jax.experimental import pallas as pl
from jax.experimental.pallas import tpu as pltpu
from jax.sharding import PartitionSpec as P

SUB = 16
PTS = 64
NT = 32
CAP = 16384
OWN = 6144
MSG = 512
HALF = MSG // 2
BLK = 256
NBLK = CAP // BLK
STRIDE = MSG + 16
ROWS = 1024
OWN2 = OWN // 2

F32, BF16, I32 = jnp.float32, jnp.bfloat16, jnp.int32
NTD = (((1,), (1,)), ((), ()))


def iota(shape, dim):
    return lax.broadcasted_iota(I32, shape, dim)


def split(x):
    high = x.astype(BF16)
    return high, (x - high.astype(F32)).astype(BF16)


def dot(a, b):
    return jnp.dot(a, b, preferred_element_type=F32)


def dot_nt(a, b):
    return lax.dot_general(a, b, NTD, preferred_element_type=F32)


def route_kernel(
    count_ref, owners_ref, cells_ref, prof_ref,
    rows_ref, meta_ref, lanes_ref,
    pos_s, m0_s, m1_s, m2_s, m3_s, m4_s, sorted_a, sorted_b, bucket, tab_v, tab_s, sem,
):
    count = count_ref[0]
    slot = iota((NBLK, BLK), 0) * BLK + iota((NBLK, BLK), 1)
    owners = owners_ref[...]
    dest = jnp.floor((owners.astype(F32) + 0.5) * (1.0 / OWN)).astype(I32)
    within = owners - dest * OWN
    live = slot < count
    dest = jnp.where(live, dest, NT)
    cells = cells_ref[...]
    m0_s[...] = (cells & 127).astype(F32)
    m1_s[...] = ((cells >> 7) & 255).astype(F32)
    m2_s[...] = (cells >> 15).astype(F32)
    m3_s[...] = (within & 255).astype(F32)
    m4_s[...] = (within >> 8).astype(F32)

    sub, lane = iota((BLK, BLK), 0), iota((BLK, BLK), 1)
    one, nil = jnp.ones((), F32), jnp.zeros((), F32)
    before = jnp.where(sub < lane, one, nil).astype(BF16)
    same_block = (sub >> 5) == (lane >> 5)
    same_dest = (sub & 31) == (lane & 31)
    seg_left = jnp.where(same_block & (lane < sub), one, nil).astype(BF16)
    seg_right = jnp.where(same_block & (sub < lane), one, nil).astype(BF16)
    base_right = jnp.where(same_dest & ((sub >> 5) < (lane >> 5)), one, nil).astype(BF16)
    all_right = jnp.where(same_dest, one, nil).astype(BF16)
    ones_a = jnp.ones((8, BLK), BF16)
    ones_b = jnp.ones((BLK, 128), BF16)
    run = jnp.zeros((8, BLK), F32)
    for c in range(8):
        part = dest[8 * c : 8 * c + 8]
        hot = jnp.where(part[:, None, :] == iota((8, NT, BLK), 1), one, nil).reshape(BLK, BLK)
        hot_b = hot.astype(BF16)
        prefix = dot(hot_b, before)
        amount = dot(hot_b, ones_b)
        seg = dot(seg_left, amount.astype(BF16))
        seg2 = jnp.concatenate([seg, seg], axis=1)
        pos = jnp.sum((hot * (prefix + seg2)).reshape(8, NT, BLK), axis=1)
        pos_s[8 * c : 8 * c + 8] = jnp.where(live[8 * c : 8 * c + 8], pos, 511.0)
        amount_l = dot_nt(ones_a, hot_b)
        amount_lb = amount_l.astype(BF16)
        src = dot(amount_lb, seg_right)
        base = dot(amount_lb, base_right) + run
        run = run + dot(amount_lb, all_right)
        most = amount_l
        for shift in (1, 2, 4, 8, 16):
            most = jnp.maximum(most, pltpu.roll(most, BLK - shift, 1))
        first = iota((8, BLK), 1) & 31
        row8 = iota((8, BLK), 0)
        packed = jnp.where(row8 == 0, src, nil)
        packed = jnp.where(row8 == 1, base + (first * STRIDE).astype(F32), packed)
        packed = jnp.where(row8 == 2, amount_l, packed)
        packed = jnp.where(row8 == 3, most, packed)
        tab_v[8 * c : 8 * c + 8] = packed.astype(I32)
    copy = pltpu.make_async_copy(tab_v, tab_s, sem)
    copy.start()
    total = run

    zero8 = jnp.zeros((STRIDE, 128), F32)

    @pl.loop(0, NT)
    def _(d):
        bucket[pl.ds(pl.multiple_of(d * STRIDE, 8), STRIDE)] = zero8

    copy.wait()

    meta_rest = jnp.zeros((56, BLK), BF16)
    low_rest = jnp.zeros((64, BLK), BF16)
    row8 = iota((8, BLK), 0)

    def sort_block(j, out):
        x = prof_ref[:, pl.ds(pl.multiple_of(j * BLK, BLK), BLK)]
        high, low = split(x)
        meta = jnp.zeros((8, BLK), F32)
        for k, ref in enumerate((m0_s, m1_s, m2_s, m3_s, m4_s)):
            meta = jnp.where(row8 == k, ref[pl.ds(j, 1), :], meta)
        data = jnp.concatenate([high, meta.astype(BF16), meta_rest, low, low_rest], axis=0)
        place = pos_s[pl.ds(j, 1), :].astype(I32)
        perm = jnp.where(place == sub, one, nil).astype(BF16)
        got = dot_nt(perm, data)
        out[0:BLK] = got[:, :128] + got[:, 128:]

    def copy_block(j, inp):
        chunk = (j >> 3) * 8
        at = (j & 7) * NT
        most = tab_s[chunk + 3, at]

        @pl.when(most <= 8)
        def _():
            for d in range(NT):
                src = tab_s[chunk, at + d]
                dst = tab_s[chunk + 1, at + d]
                bucket[pl.ds(dst, 8)] = inp[pl.ds(src, 8)]

        @pl.when((most > 8) & (most <= 16))
        def _():
            for d in range(NT):
                src = tab_s[chunk, at + d]
                dst = tab_s[chunk + 1, at + d]
                bucket[pl.ds(dst, 16)] = inp[pl.ds(src, 16)]

        @pl.when(most > 16)
        def _():
            @pl.loop(0, NT)
            def _(d):
                src = tab_s[chunk, at + d]
                dst = tab_s[chunk + 1, at + d]

                @pl.loop(0, (tab_s[chunk + 2, at + d] + 7) >> 3)
                def _(k):
                    bucket[pl.ds(dst + 8 * k, 8)] = inp[pl.ds(src + 8 * k, 8)]

    sorted_a[BLK:] = jnp.zeros((16, 128), F32)
    sorted_b[BLK:] = jnp.zeros((16, 128), F32)
    pairs = (count + 2 * BLK - 1) // (2 * BLK)
    sort_block(0, sorted_a)

    @pl.loop(0, pairs)
    def _(p):
        sort_block(2 * p + 1, sorted_b)
        copy_block(2 * p, sorted_a)
        sort_block(jnp.minimum(2 * p + 2, NBLK - 1), sorted_a)
        copy_block(2 * p + 1, sorted_b)

    low_lanes = iota((HALF, 128), 1) < 64
    r8, l8 = iota((8, 128), 0), iota((8, 128), 1)
    pick = jnp.where((r8 == 0) & (l8 == 64), one, nil)
    pick = jnp.where((r8 == 1) & (l8 == 65), one, pick)
    pick = jnp.where((r8 == 1) & (l8 == 66), 256.0 * one, pick)
    pick = jnp.where((r8 == 2) & (l8 == 67), one, pick)
    pick = jnp.where((r8 == 2) & (l8 == 68), 256.0 * one, pick)
    pick = pick.astype(BF16)
    rank = iota((8, MSG), 1)
    rank_row = iota((8, MSG), 0)
    lane_dest = iota((8, BLK), 1)

    @pl.loop(0, NT)
    def _(d):
        at = pl.multiple_of(d * STRIDE, 8)
        lo = bucket[pl.ds(at, HALF)]
        hi = bucket[pl.ds(pl.multiple_of(at + HALF, 8), HALF)]
        rows_ref[d] = jnp.where(low_lanes, lo, pltpu.roll(hi, 64, 1))
        meta_ref[d] = jnp.where(low_lanes, pltpu.roll(lo, 64, 1), hi).astype(BF16)
        both = jnp.concatenate([lo, hi], axis=0).astype(BF16)
        nums = dot_nt(pick, both)
        mine = jnp.max(jnp.where(lane_dest == d, total, nil), axis=1, keepdims=True)
        valid = rank.astype(F32) < mine
        nums = jnp.where((rank_row == 2) & ~valid, float(OWN), nums)
        nums = jnp.where(rank_row == 3, jnp.where(valid, one, nil), nums)
        lanes_ref[d] = nums


def route(counts, owners, cells, profiles):
    vmem = pl.BlockSpec(memory_space=pltpu.VMEM)
    return pl.pallas_call(
        route_kernel,
        out_shape=(
            jax.ShapeDtypeStruct((NT, HALF, 128), F32),
            jax.ShapeDtypeStruct((NT, HALF, 128), BF16),
            jax.ShapeDtypeStruct((NT, 8, MSG), F32),
        ),
        in_specs=[pl.BlockSpec(memory_space=pltpu.SMEM), vmem, vmem, vmem],
        out_specs=(vmem, vmem, vmem),
        scratch_shapes=[pltpu.VMEM((NBLK, BLK), F32)] * 6
        + [pltpu.VMEM((BLK + 16, 128), F32)] * 2
        + [
            pltpu.VMEM((NT * STRIDE, 128), F32),
            pltpu.VMEM((64, BLK), I32),
            pltpu.SMEM((64, BLK), I32),
            pltpu.SemaphoreType.DMA,
        ],
        compiler_params=pltpu.CompilerParams(vmem_limit_bytes=40 * 2**20),
        name="route",
    )(counts, owners.reshape(NBLK, BLK), cells.reshape(NBLK, BLK), profiles)


def far_kernel(meta_ref, cells_ref, fw_ref, far_ref, add_ref):
    table = cells_ref[...]
    t0, t1 = split(table)
    table2 = jnp.concatenate([t0, t1], axis=1)
    one, nil = jnp.ones((), F32), jnp.zeros((), F32)
    fw = fw_ref[...]
    fw0, fw1 = split(fw)
    shape = (128, 128)
    sub, lane = iota(shape, 0), iota(shape, 1)
    ones8 = jnp.ones((8, 256), BF16)
    cell_lane = iota((HALF, 128), 1)

    def half(h):
        first = 64 if h else 0
        meta = meta_ref[0]
        s128 = jnp.where(sub == first, one, nil)
        r128 = jnp.where(sub == first + 1, one, nil) + jnp.where(sub == first + 2, 256.0 * one, nil)
        pick = jnp.concatenate([s128, r128], axis=1).astype(BF16)
        got = dot(meta, pick)
        s_b = got[:, :128].astype(I32)
        r_b = got[:, 128:].astype(I32)
        hot = jnp.concatenate(
            [jnp.where(r_b == cell_lane + 128 * k, one, nil).astype(BF16) for k in range(ROWS // 128)],
            axis=1,
        )
        val = dot(hot, table2)
        val = val[:, :128] + val[:, 128:]
        v0, v1 = split(jnp.where(s_b == cell_lane, val, nil))
        v = jnp.concatenate([v0, v1], axis=1)
        far = dot_nt(ones8, v)
        mask = (lane >= 64) if h else (lane < 64)
        w0 = jnp.where(mask, fw0.astype(F32), nil).astype(BF16)
        w1 = jnp.where(mask, fw1.astype(F32), nil).astype(BF16)
        return far, v, w0, w1

    far_a, va, a0, a1 = half(0)
    far_b, vb, b0, b1 = half(1)
    far_ref[0] = jnp.concatenate([far_a, far_b], axis=1)
    w = jnp.concatenate([jnp.concatenate([a0, a1], axis=1)] * 2, axis=0)
    u = jnp.concatenate([jnp.concatenate([b0, b1], axis=1)] * 2, axis=0)
    got = dot(va, w) + dot(vb, u)
    add_ref[0] = got[:, :128] + got[:, 128:]


def far_gather(meta, table, fw):
    return pl.pallas_call(
        far_kernel,
        grid=(NT,),
        out_shape=(
            jax.ShapeDtypeStruct((NT, 8, MSG), F32),
            jax.ShapeDtypeStruct((NT, HALF, 128), F32),
        ),
        in_specs=[
            pl.BlockSpec((1, HALF, 128), lambda d: (d, 0, 0)),
            pl.BlockSpec((ROWS, 128), lambda d: (0, 0)),
            pl.BlockSpec((1, 128), lambda d: (0, 0)),
        ],
        out_specs=(
            pl.BlockSpec((1, 8, MSG), lambda d: (d, 0, 0)),
            pl.BlockSpec((1, HALF, 128), lambda d: (d, 0, 0)),
        ),
        compiler_params=pltpu.CompilerParams(vmem_limit_bytes=24 * 2**20),
        cost_estimate=pl.CostEstimate(flops=16384 * 1024 * 512, bytes_accessed=8 << 20, transcendentals=0),
        name="far_gather",
    )(meta, table, fw)


def step_weights(radial_step):
    zero = jnp.zeros((PTS, PTS), F32)
    w = jnp.concatenate(
        [
            jnp.concatenate([radial_step.T, zero], axis=1),
            jnp.concatenate([zero, radial_step.T], axis=1),
        ],
        axis=0,
    )
    high = lax.reduce_precision(w, 8, 7)
    w0, w1 = high.astype(BF16), (w - high).astype(BF16)
    row = jnp.concatenate([w0, w1], axis=1)
    return jnp.concatenate([row, row], axis=0)


def flux_rows(flux_weights):
    zero = jnp.zeros((PTS,), F32)
    f = jnp.stack(
        [jnp.concatenate([flux_weights, zero]), jnp.concatenate([zero, flux_weights])]
        + [jnp.zeros((128,), F32)] * 6
    )
    return f / SUB


def substep(state, add, weights):
    s0, s1 = split(state)
    got = dot(jnp.concatenate([s0, s1], axis=1), weights)
    return (got[:, :128] + got[:, 128:]) + (add + 0.25 * jnp.tanh(state))


def heat_kernel(rows_ref, add_ref, weights_ref, flux_ref, heat_ref):
    weights = weights_ref[...]
    state = rows_ref[0]
    total = jnp.zeros_like(state)
    for _ in range(SUB):
        state = substep(state, add_ref[0], weights)
        total = total + state
    t0, t1 = split(total)
    f0, f1 = split(flux_ref[...])
    heat_ref[0] = dot_nt(f0, t0) + dot_nt(f0, t1) + dot_nt(f1, t0)


def home_heat(rows, add, weights, flux):
    return pl.pallas_call(
        heat_kernel,
        grid=(NT,),
        out_shape=jax.ShapeDtypeStruct((NT, 8, HALF), F32),
        in_specs=[
            pl.BlockSpec((1, HALF, 128), lambda d: (d, 0, 0)),
            pl.BlockSpec((1, HALF, 128), lambda d: (d, 0, 0)),
            pl.BlockSpec((256, 256), lambda d: (0, 0)),
            pl.BlockSpec((8, 128), lambda d: (0, 0)),
        ],
        out_specs=pl.BlockSpec((1, 8, HALF), lambda d: (d, 0, 0)),
        compiler_params=pltpu.CompilerParams(vmem_limit_bytes=24 * 2**20),
        cost_estimate=pl.CostEstimate(
            flops=SUB * 8192 * 256 * 512, bytes_accessed=8 << 20, transcendentals=SUB << 20
        ),
        name="home_heat",
    )(rows, add, weights, flux)


def deposit_kernel(lanes_ref, heat_ref, stepped_ref, out_ref, acc):
    d = pl.program_id(0)

    @pl.when(d == 0)
    def _():
        acc[...] = jnp.zeros_like(acc)

    one, nil = jnp.ones((), F32), jnp.zeros((), F32)
    nums = lanes_ref[0]
    s, r, valid = nums[0:1].astype(I32), nums[1:2].astype(I32), nums[3:4]
    heat = jnp.concatenate([heat_ref[0, 0:1], heat_ref[0, 1:2]], axis=1)
    heat = jnp.where(valid > 0.5, 0.5 * heat, nil)
    spread = jnp.where(s == iota((128, MSG), 0), heat, nil)
    h0, h1 = split(spread)
    hot = jnp.where(r == iota((ROWS, MSG), 0), one, nil).astype(BF16)
    acc[...] += dot_nt(hot, jnp.concatenate([h0, h1], axis=0))

    @pl.when(d == NT - 1)
    def _():
        out_ref[...] = stepped_ref[...] + acc[:, :128] + acc[:, 128:]


def deposit(lanes, heat, stepped):
    return pl.pallas_call(
        deposit_kernel,
        grid=(NT,),
        out_shape=jax.ShapeDtypeStruct((ROWS, 128), F32),
        in_specs=[
            pl.BlockSpec((1, 8, MSG), lambda d: (d, 0, 0)),
            pl.BlockSpec((1, 8, HALF), lambda d: (d, 0, 0)),
            pl.BlockSpec((ROWS, 128), lambda d: (0, 0)),
        ],
        out_specs=pl.BlockSpec((ROWS, 128), lambda d: (0, 0)),
        scratch_shapes=[pltpu.VMEM((ROWS, 256), F32)],
        compiler_params=pltpu.CompilerParams(vmem_limit_bytes=24 * 2**20),
        cost_estimate=pl.CostEstimate(flops=16384 * 1024 * 512, bytes_accessed=2 << 20, transcendentals=0),
        name="deposit",
    )(lanes, heat, stepped)


def settle_kernel(amount_ref, slot_ref, rows_ref, far_ref, fw_ref, weights_ref, out_ref, stage, low_s, high_s):
    low_lanes = iota((HALF, 128), 1) < 64
    pick = jnp.where(iota((8, 128), 0) == 0, 1.0, 0.0).astype(F32)
    tn = (((0,), (0,)), ((), ()))

    @pl.loop(0, NT)
    def _(t):
        rows = rows_ref[t]
        far = far_ref[t]
        f0, f1 = split(far)
        col = lax.dot_general(f0, pick.astype(BF16), tn, preferred_element_type=F32)
        col = col + lax.dot_general(f1, pick.astype(BF16), tn, preferred_element_type=F32)
        low_s[...] = jnp.where(low_lanes, rows, col[:HALF])
        high_s[...] = jnp.where(low_lanes, pltpu.roll(rows, 64, 1), col[HALF:])
        amount = amount_ref[t]

        @pl.loop(0, (jnp.minimum(amount, HALF) + 7) >> 3)
        def _(k):
            at = pl.multiple_of(8 * k, 8)
            for i in range(8):
                stage[pl.ds(slot_ref[t, at + i], 1)] = low_s[pl.ds(at + i, 1)]

        @pl.loop(0, (jnp.maximum(amount - HALF, 0) + 7) >> 3)
        def _(k):
            at = pl.multiple_of(8 * k, 8)
            for i in range(8):
                stage[pl.ds(slot_ref[t, HALF + at + i], 1)] = high_s[pl.ds(at + i, 1)]

    weights = weights_ref[...]
    fw = fw_ref[...]

    @pl.loop(0, OWN2 // HALF)
    def _(c):
        at = pl.multiple_of(c * HALF, HALF)
        a = stage[pl.ds(at, HALF)]
        b = stage[pl.ds(pl.multiple_of(at + OWN2, HALF), HALF)]
        state = jnp.where(low_lanes, a, pltpu.roll(b, 64, 1))
        add = fw * jnp.where(low_lanes, pltpu.roll(a, 64, 1), b)
        for _ in range(SUB):
            state = substep(state, add, weights)
        for k in range(HALF // 128):
            turned = state[128 * k : 128 * k + 128].T
            out_ref[:, pl.ds(pl.multiple_of(at + 128 * k, 128), 128)] = turned[:64]
            out_ref[:, pl.ds(pl.multiple_of(at + OWN2 + 128 * k, 128), 128)] = turned[64:]


def settle(amount, slots, rows, far, fw, weights):
    vmem, smem = pl.BlockSpec(memory_space=pltpu.VMEM), pl.BlockSpec(memory_space=pltpu.SMEM)
    return pl.pallas_call(
        settle_kernel,
        out_shape=jax.ShapeDtypeStruct((PTS, OWN), F32),
        in_specs=[smem, smem, vmem, vmem, vmem, vmem],
        out_specs=vmem,
        scratch_shapes=[
            pltpu.VMEM((OWN + 8, 128), F32),
            pltpu.VMEM((HALF, 128), F32),
            pltpu.VMEM((HALF, 128), F32),
        ],
        compiler_params=pltpu.CompilerParams(vmem_limit_bytes=32 * 2**20),
        name="settle",
    )(amount, slots, rows, far, fw, weights)


def halo(cells):
    n_x, n_s = lax.axis_size("stream"), lax.axis_size("tile")
    up_x = [(i, i + 1) for i in range(n_x - 1)]
    down_x = [(i + 1, i) for i in range(n_x - 1)]
    up_s = [(i, (i + 1) % n_s) for i in range(n_s)]
    down_s = [((i + 1) % n_s, i) for i in range(n_s)]
    before_x = lax.ppermute(cells[-1:], "stream", up_x)
    after_x = lax.ppermute(cells[:1], "stream", down_x)
    before_s = lax.ppermute(cells[:, :, -1], "tile", up_s)[:, :, None]
    after_s = lax.ppermute(cells[:, :, 0], "tile", down_s)[:, :, None]
    return (
        jnp.concatenate([before_x, cells[:-1]], axis=0),
        jnp.concatenate([cells[1:], after_x], axis=0),
        jnp.concatenate([before_s, cells[..., :-1]], axis=2),
        jnp.concatenate([cells[..., 1:], after_s], axis=2),
    )


def stencil(enthalpy, x_lower, x_upper, s_lower, s_upper, velocity, diffusivity, wall_flux):
    wall_low = jnp.concatenate([enthalpy[:, :1], enthalpy[:, :-1]], axis=1)
    wall_high = jnp.concatenate([enthalpy[:, 1:], enthalpy[:, -1:]], axis=1)
    laplace = x_lower + x_upper + (wall_low + wall_high) + (s_lower + s_upper) - 6.0 * enthalpy
    stepped = enthalpy + diffusivity * laplace - velocity * (enthalpy - x_lower)
    at_wall = lax.broadcasted_iota(I32, stepped.shape, 1) == 0
    return stepped + jnp.where(at_wall, wall_flux[:, None, :], 0.0)


def on_device(
    enthalpy, velocity, diffusivity, wall_flux, profiles, counts, owners, cells,
    radial_step, far_weights, flux_weights,
):
    weights = step_weights(radial_step)
    fw = jnp.concatenate([far_weights, far_weights])[None, :]
    flux = flux_rows(flux_weights)
    rows, meta, lanes = route(counts, owners, cells, profiles)
    got_rows = lax.all_to_all(rows, "tile", split_axis=0, concat_axis=0, tiled=True)
    far, add = far_gather(meta, enthalpy.reshape(ROWS, 128), fw)
    side = jnp.concatenate(
        [lanes[:, 2].reshape(NT, 4, 128), far[:, 0].reshape(NT, 4, 128)], axis=1
    )
    got_side = lax.all_to_all(side, "tile", split_axis=0, concat_axis=0, tiled=True)
    heat = home_heat(rows, add, weights, flux)
    stepped = stencil(enthalpy, *halo(enthalpy), velocity, diffusivity, wall_flux)
    new_enthalpy = deposit(lanes, heat, stepped.reshape(ROWS, 128)).reshape(enthalpy.shape)
    slots = got_side[:, :4].reshape(NT, MSG).astype(I32)
    amount = jnp.sum((slots < OWN).astype(I32), axis=1)
    got_far = jnp.broadcast_to(got_side[:, 4:].reshape(NT, 1, MSG), (NT, 8, MSG))
    new_profiles = settle(amount, slots, got_rows, got_far, fw, weights)
    return new_enthalpy, new_profiles


def solution(mesh):
    return jax.shard_map(
        on_device,
        mesh=mesh,
        in_specs=(
            P("stream", None, "tile"),
            P("stream", None, "tile"),
            P("stream", None, "tile"),
            P("stream", "tile"),
            P(None, ("stream", "tile")),
            P(("stream", "tile")),
            P(("stream", "tile")),
            P(("stream", "tile")),
            P(),
            P(),
            P(),
        ),
        out_specs=(P("stream", None, "tile"), P(None, ("stream", "tile"))),
        check_vma=False,
    )
```

time: 755 us -> 273 us (0.36)
  local copies, waits for them, and re-layouts: 573 us -> 17.6 us
  Pallas kernels: 0 us -> 205 us
  other arithmetic: 96.5 us -> 4.78 us
  matrix products: 43.3 us -> 0 us
    gather x4 -> x0, local copies, waits for them, and re-layouts: 272 us -> none  [the longest x2 90.5 us: on_device(): heat_rate[jnp.minimum(landing, owned_slots - 1)]]
    scatter x5 -> x0, local copies, waits for them, and re-layouts: 268 us -> none  [the longest x1 60.4 us: on_device(): jnp.zeros((owned_slots,), jnp.float32).at[landing]]
    pallas_call x0 -> x5, Pallas kernels: none -> 205 us  [the longest x1 72.5 us: home_heat(): pl.pallas_call(heat_kernel, grid=(NT,), out_shape=jax.ShapeDtypeStruct((N...]
    scatter-add x1 -> x0, other arithmetic: 88 us -> none  [on_device(): stepped.reshape(-1).at[cells].add(latent_share * heat_home)]
    dot_general x32 -> x0, matrix products: 43.3 us -> none  [the longest x16 28.7 us: substep(): jnp.dot(radial_step, current, precision=lax.Precision.HIGHEST, preferred_...]
    all_to_all x3 -> x0, local copies, waits for them, and re-layouts: 18.6 us -> none  [on_device(): lax.all_to_all(send_rows, 'tile', split_axis=1, concat_axis=1, tiled=True)]
    all_to_all x3 -> x2, starting transfers between devices: 24.1 us -> 30.3 us  [the longest x1 24.4 us: on_device(): lax.all_to_all(side, 'tile', split_axis=0, concat_axis=0, tiled=True)]
  transfers between devices with their start and end apart: 7 -> 6, of which waited for: 1 -> 1; matrix products, arithmetic and copies ran while one was open for 16% -> 5% of each run, Pallas kernels for 0% -> 54%
where the time goes in v1:
time: 273 us; the launch traced here: 272 us
  Pallas kernels  205 us (75%)
  starting transfers between devices  37.7 us (14%)
  local copies, waits for them, and re-layouts  17.6 us (6%)
  waiting for transfers between devices  5.63 us (2%)
  other arithmetic  4.78 us (2%)
    pallas_call x1, Pallas kernels, home_heat(): pl.pallas_call(heat_kernel, grid=(NT,), out_shape=jax.ShapeDtypeStruct((N...  72.5 us
    pallas_call x1, Pallas kernels, settle(): pl.pallas_call(settle_kernel, out_shape=jax.ShapeDtypeStruct((PTS, OWN),...  57.7 us
    pallas_call x1, Pallas kernels, far_gather(): pl.pallas_call(far_kernel, grid=(NT,), out_shape=(jax.ShapeDtypeStruct((N...  43 us
    all_to_all x1, starting transfers between devices, on_device(): lax.all_to_all(side, 'tile', split_axis=0, concat_axis=0, tiled=True)  24.4 us
    pallas_call x1, Pallas kernels, deposit(): pl.pallas_call(deposit_kernel, grid=(NT,), out_shape=jax.ShapeDtypeStruct...  17.1 us
    pallas_call x1, Pallas kernels, route(): pl.pallas_call(route_kernel, out_shape=(jax.ShapeDtypeStruct((NT, HALF, 1...  14.8 us
    unnamed x27, local copies, waits for them, and re-layouts  8.47 us
    all_to_all x1, starting transfers between devices, on_device(): lax.all_to_all(rows, 'tile', split_axis=0, concat_axis=0, tiled=True)  5.87 us
  transfers between devices with their start and end apart: 6, of which 1 were waited for; matrix products, arithmetic and copies ran while one was open for 5% of the time, Pallas kernels for 54%

profile of v1, /device:TPU:35, one launch (start us, length us, event | category | flops | bytes accessed | tf_op | source)
XLA Modules:
  0.0 272.4 jit_solution(3407977105150246492)
XLA Ops:
  0.6 1.4 fusion.8
  2.1 1.9 collective-permute-start.1
  4.0 1.5 fusion.11
  5.5 0.2 copy.21
  5.7 1.9 collective-permute-start.2
  7.6 0.2 copy.22
  7.8 3.5 %collective-permute-start = (f32[1,64,128]{2,1,0:T(8,128)}, f32[1,64,128]{2,1,0:T(8,128)}, u32[]{:S(2)}, u32[]{:S(2)}) collective-permute-start(f32[1,64,128]{2,1,0:T(8,128)} %get-tuple-element.12), channel_id=1, source_target_pairs={{0,32},{32,64},{64,96},{1,33},{33,65},{65,97},{2,34},{34,66},{66,9... | collective-permute-start | bytes 98312 | tf_op jit(solution)/shard_map/ppermute | solution.py:458
  12.0 0.9 reshape.24.owners_ref
  12.9 0.9 reshape.25.cells_ref
  13.8 0.8 maximum_bitcast_fusion.fw_ref
  14.6 2.2 copy-done.1
  16.8 14.8 %route.1 = (f32[32,256,128]{2,1,0:T(8,128)S(1)}, bf16[32,256,128]{2,1,0:T(8,128)(2,1)S(1)}, f32[32,8,512]{2,1,0:T(8,128)S(1)}) custom-call(s32[1]{0:T(128)S(6)} %copy.29.count_ref, s32[64,256]{1,0:T(8,128)S(1)} %reshape.24.owners_ref, s32[64,256]{1,0:T(8,128)S(1)} %reshape.25.cells_ref, f32[64,16384]{1,0:T(8,128)S(1)} %copy-done.1), custom_call_target="tpu_custom_call" | custom-call | tf_op jit(solution)/shard_map/route/pallas_call | solution.py:198
  31.6 43.0 %far_gather.1 = (f32[32,8,512]{2,1,0:T(8,128)S(1)}, f32[32,256,128]{2,1,0:T(8,128)S(1)}) custom-call(bf16[32,256,128]{2,1,0:T(8,128)(2,1)S(1)} %get-tuple-element.9.meta_ref, f32[1024,128]{1,0:T(8,128)S(1)} %bitcast.24, f32[1,128]{1,0:T(1,128)S(1)} %maximum_bitcast_fusion.fw_ref), custom_call_target="tpu_custom_call" | custom-call | flops 8589934592 | bytes 8388608 | tf_op jit(solution)/shard_map/far_gather/pallas_call | solution.py:265
  74.7 2.0 copy-done.4
  76.8 0.7 pad_maximum_fusion.1
  77.5 24.4 %all-to-all-start = ((f32[32,8,128]{2,1,0:T(8,128)}), f32[32,8,128]{2,1,0:T(8,128)S(1)}, u32[]{:S(2)}, u32[]{:S(2)}) async-start(f32[32,8,128]{2,1,0:T(8,128)} %pad_maximum_fusion.1), calls=%async_computation | async-start | bytes 262144 | tf_op jit(solution)/shard_map/all_to_all | solution.py:492
  101.9 0.6 fusion.13
  102.9 5.6 %all-to-all-done = f32[32,8,128]{2,1,0:T(8,128)S(1)} async-done(((f32[32,8,128]{2,1,0:T(8,128)}), f32[32,8,128]{2,1,0:T(8,128)S(1)}, u32[]{:S(2)}, u32[]{:S(2)}) %all-to-all-start) | async-done | bytes 131104 | tf_op jit(solution)/shard_map/all_to_all | solution.py:492
  108.5 0.6 copy-done.6
  109.2 5.9 %all-to-all-start.1 = ((f32[32,256,128]{2,1,0:T(8,128)}), f32[32,256,128]{2,1,0:T(8,128)}, u32[]{:S(2)}, u32[]{:S(2)}) async-start(f32[32,256,128]{2,1,0:T(8,128)} %copy-done.2), calls=%async_computation.1 | async-start | bytes 8388608 | tf_op jit(solution)/shard_map/all_to_all | solution.py:487
  115.2 1.1 fusion.9
  116.4 1.1 fusion.10
  117.5 0.4 copy-done.3
  117.9 2.2 copy-done.5
  120.1 72.5 %home_heat.1.heat_ref = f32[32,8,256]{2,1,0:T(8,128)S(1)} custom-call(f32[32,256,128]{2,1,0:T(8,128)S(1)} %copy-done.3, f32[32,256,128]{2,1,0:T(8,128)S(1)} %copy-done.5, bf16[256,256]{1,0:T(8,128)(2,1)S(1)} %maximum_maximum_fusion.weights_ref, f32[8,128]{1,0:T(8,128)S(1)} %maximum_multiply_fusion.flux_ref), custom_call_target="tpu_custom_call" | custom-call | flops 17179869184 | bytes 8388608 | tf_op jit(solution)/shard_map/home_heat/pallas_call | solution.py:330
  192.6 0.2 copy.18
  192.8 0.6 copy-done.9
  193.4 0.9 copy.20
  194.4 2.4 fusion.6
  196.8 17.1 %deposit.1 = f32[1024,128]{1,0:T(8,128)} custom-call(f32[32,8,512]{2,1,0:T(8,128)S(1)} %get-tuple-element.7.lanes_ref, f32[32,8,256]{2,1,0:T(8,128)S(1)} %home_heat.1.heat_ref, f32[1024,128]{1,0:T(8,128)S(1)} %bitcast.25), custom_call_target="tpu_custom_call" | custom-call | flops 8589934592 | bytes 2097152 | tf_op jit(solution)/shard_map/deposit/pallas_call | solution.py:372
  214.0 0.7 convert_reduce_fusion.amount_ref
  214.7 57.7 %settle.1 = f32[64,6144]{1,0:T(8,128)} custom-call(s32[32]{0:T(128)S(1)} %convert_reduce_fusion.amount_ref, s32[32,512]{1,0:T(8,128)S(1)} %bitcast.26, f32[32,256,128]{2,1,0:T(8,128)} %all-to-all-done.1.rows_ref, f32[32,8,512]{2,1,0:T(8,128)S(1)} %broadcast_in_dim.37.far_ref, f32[1,128]{1,0:T(1,128)S(1)} %maximum_bitcast_fusion.fw_ref, ...), custom_call_target="tpu_custom_call" | custom-call | tf_op jit(solution)/shard_map/settle/pallas_call | solution.py:437
  (39 shorter events, 0.9 us)
Async XLA Ops:
  0.6 31.0 %copy-start = (f32[16,64,128]{2,1,0:T(8,128)S(1)}, f32[16,64,128]{2,1,0:T(8,128)}, u32[]{:S(2)}) copy-start(f32[16,64,128]{2,1,0:T(8,128)} %param.11) | copy-start | bytes 1572868
  2.1 192.3 %collective-permute-start.1 = (f32[1,64,128]{2,1,0:T(8,128)}, f32[1,64,128]{2,1,0:T(8,128)}, u32[]{:S(2)}, u32[]{:S(2)}) collective-permute-start(f32[1,64,128]{2,1,0:T(8,128)} %get-tuple-element.13), channel_id=1, source_target_pairs={{32,0},{64,32},{96,64},{33,1},{65,33},{97,65},{34,2},{66,34},{98,6... | collective-permute-start | bytes 98312 | tf_op jit(solution)/shard_map/ppermute | solution.py:459
  5.7 186.9 %collective-permute-start.2 = (f32[16,64]{1,0:T(8,128)S(1)}, f32[16,64]{1,0:T(8,128)S(1)}, u32[]{:S(2)}, u32[]{:S(2)}) collective-permute-start(f32[16,64]{1,0:T(8,128)S(1)} %bitcast.33), channel_id=1, source_target_pairs={{0,1},{1,2},{2,3},{3,4},{4,5},{5,6},{6,7},{7,8},{8,9},{9,10},{10,1... | collective-permute-start | bytes 12296 | tf_op jit(solution)/shard_map/ppermute | solution.py:460
  7.8 185.0 %collective-permute-start.3 = (f32[16,64]{1,0:T(8,128)S(1)}, f32[16,64]{1,0:T(8,128)S(1)}, u32[]{:S(2)}, u32[]{:S(2)}) collective-permute-start(f32[16,64]{1,0:T(8,128)S(1)} %bitcast.35), channel_id=1, source_target_pairs={{1,0},{2,1},{3,2},{4,3},{5,4},{6,5},{7,6},{8,7},{9,8},{10,9},{11,1... | collective-permute-start | bytes 12296 | tf_op jit(solution)/shard_map/ppermute | solution.py:461
  7.8 186.5 %collective-permute-start = (f32[1,64,128]{2,1,0:T(8,128)}, f32[1,64,128]{2,1,0:T(8,128)}, u32[]{:S(2)}, u32[]{:S(2)}) collective-permute-start(f32[1,64,128]{2,1,0:T(8,128)} %get-tuple-element.12), channel_id=1, source_target_pairs={{0,32},{32,64},{64,96},{1,33},{33,65},{65,97},{2,34},{34,66},{66,9... | collective-permute-start | bytes 98312 | tf_op jit(solution)/shard_map/ppermute | solution.py:458
  14.6 2.2 copy-start.1
  31.6 43.1 %copy-start.2 = (f32[32,256,128]{2,1,0:T(8,128)}, f32[32,256,128]{2,1,0:T(8,128)S(1)}, u32[]{:S(2)}) copy-start(f32[32,256,128]{2,1,0:T(8,128)S(1)} %get-tuple-element.8.rows_ref) | copy-start | bytes 12582916
  31.6 70.9 %copy-start.8 = (f32[64,64]{1,0:T(8,128)S(1)}, f32[64,64]{1,0:T(8,128)}, u32[]{:S(2)}) copy-start(f32[64,64]{1,0:T(8,128)} %param.19) | copy-start | bytes 49156
  31.6 70.9 %copy-start.10 = (f32[64]{0:T(128)S(1)}, f32[64]{0:T(128)}, u32[]{:S(2)}) copy-start(f32[64]{0:T(128)} %param.21) | copy-start | bytes 772
  74.7 2.0 copy-start.4
  77.5 31.1 %all-to-all-start = ((f32[32,8,128]{2,1,0:T(8,128)}), f32[32,8,128]{2,1,0:T(8,128)S(1)}, u32[]{:S(2)}, u32[]{:S(2)}) async-start(f32[32,8,128]{2,1,0:T(8,128)} %pad_maximum_fusion.1), calls=%async_computation | async-start | bytes 262144 | tf_op jit(solution)/shard_map/all_to_all | solution.py:492
  108.5 0.6 copy-start.6
  109.2 105.5 %all-to-all-start.1 = ((f32[32,256,128]{2,1,0:T(8,128)}), f32[32,256,128]{2,1,0:T(8,128)}, u32[]{:S(2)}, u32[]{:S(2)}) async-start(f32[32,256,128]{2,1,0:T(8,128)} %copy-done.2), calls=%async_computation.1 | async-start | bytes 8388608 | tf_op jit(solution)/shard_map/all_to_all | solution.py:487
  115.0 2.8 %copy-start.3 = (f32[32,256,128]{2,1,0:T(8,128)S(1)}, f32[32,256,128]{2,1,0:T(8,128)}, u32[]{:S(2)}) copy-start(f32[32,256,128]{2,1,0:T(8,128)} %copy-done.2) | copy-start | bytes 12582916
  117.9 2.2 copy-start.5
  192.8 0.6 copy-start.9
  196.8 17.1 %copy-start.7 = (f32[32,8,128]{2,1,0:T(8,128)S(1)}, f32[32,8,128]{2,1,0:T(8,128)}, u32[]{:S(2)}) copy-start(f32[32,8,128]{2,1,0:T(8,128)} %copy-done.6) | copy-start | bytes 393220

commit v2 on v1

--- a/solution.py
+++ b/solution.py
@@ -12,6 +12,7 @@
 OWN = 6144
 MSG = 512
 HALF = MSG // 2
+LOAD = HALF + 8
 BLK = 256
 NBLK = CAP // BLK
 STRIDE = MSG + 16
@@ -53,8 +54,8 @@
     dest = jnp.where(live, dest, NT)
     cells = cells_ref[...]
     m0_s[...] = (cells & 127).astype(F32)
-    m1_s[...] = ((cells >> 7) & 255).astype(F32)
-    m2_s[...] = (cells >> 15).astype(F32)
+    m1_s[...] = ((cells >> 7) & 3).astype(F32)
+    m2_s[...] = (cells >> 9).astype(F32)
     m3_s[...] = (within & 255).astype(F32)
     m4_s[...] = (within >> 8).astype(F32)
 
@@ -94,7 +95,9 @@
         packed = jnp.where(row8 == 1, base + (first * STRIDE).astype(F32), packed)
         packed = jnp.where(row8 == 2, amount_l, packed)
         packed = jnp.where(row8 == 3, most, packed)
-        tab_v[8 * c : 8 * c + 8] = packed.astype(I32)
+        packed = packed.astype(I32)
+        tab_v[16 * c : 16 * c + 8] = packed[:, :128]
+        tab_v[16 * c + 8 : 16 * c + 16] = packed[:, 128:]
     copy = pltpu.make_async_copy(tab_v, tab_s, sem)
     copy.start()
     total = run
@@ -124,8 +127,8 @@
         out[0:BLK] = got[:, :128] + got[:, 128:]
 
     def copy_block(j, inp):
-        chunk = (j >> 3) * 8
-        at = (j & 7) * NT
+        chunk = (j >> 2) * 8
+        at = (j & 3) * NT
         most = tab_s[chunk + 3, at]
 
         @pl.when(most <= 8)
@@ -169,7 +172,7 @@
     r8, l8 = iota((8, 128), 0), iota((8, 128), 1)
     pick = jnp.where((r8 == 0) & (l8 == 64), one, nil)
     pick = jnp.where((r8 == 1) & (l8 == 65), one, pick)
-    pick = jnp.where((r8 == 1) & (l8 == 66), 256.0 * one, pick)
+    pick = jnp.where((r8 == 1) & (l8 == 66), 4.0 * one, pick)
     pick = jnp.where((r8 == 2) & (l8 == 67), one, pick)
     pick = jnp.where((r8 == 2) & (l8 == 68), 256.0 * one, pick)
     pick = pick.astype(BF16)
@@ -177,12 +180,12 @@
     rank_row = iota((8, MSG), 0)
     lane_dest = iota((8, BLK), 1)
 
-    @pl.loop(0, NT)
+    @pl.loop(0, NT, unroll=4)
     def _(d):
         at = pl.multiple_of(d * STRIDE, 8)
         lo = bucket[pl.ds(at, HALF)]
         hi = bucket[pl.ds(pl.multiple_of(at + HALF, 8), HALF)]
-        rows_ref[d] = jnp.where(low_lanes, lo, pltpu.roll(hi, 64, 1))
+        rows_ref[d, 0:HALF] = jnp.where(low_lanes, lo, pltpu.roll(hi, 64, 1))
         meta_ref[d] = jnp.where(low_lanes, pltpu.roll(lo, 64, 1), hi).astype(BF16)
         both = jnp.concatenate([lo, hi], axis=0).astype(BF16)
         nums = dot_nt(pick, both)
@@ -191,6 +194,9 @@
         nums = jnp.where((rank_row == 2) & ~valid, float(OWN), nums)
         nums = jnp.where(rank_row == 3, jnp.where(valid, one, nil), nums)
         lanes_ref[d] = nums
+        rows_ref[d, HALF : HALF + 8] = jnp.concatenate(
+            [nums[2:3, 128 * q : 128 * q + 128] for q in range(4)] + [jnp.zeros((4, 128), F32)], axis=0
+        )
 
 
 def route(counts, owners, cells, profiles):
@@ -198,7 +204,7 @@
     return pl.pallas_call(
         route_kernel,
         out_shape=(
-            jax.ShapeDtypeStruct((NT, HALF, 128), F32),
+            jax.ShapeDtypeStruct((NT, LOAD, 128), F32),
             jax.ShapeDtypeStruct((NT, HALF, 128), BF16),
             jax.ShapeDtypeStruct((NT, 8, MSG), F32),
         ),
@@ -208,8 +214,8 @@
         + [pltpu.VMEM((BLK + 16, 128), F32)] * 2
         + [
             pltpu.VMEM((NT * STRIDE, 128), F32),
-            pltpu.VMEM((64, BLK), I32),
-            pltpu.SMEM((64, BLK), I32),
+            pltpu.VMEM((128, 128), I32),
+            pltpu.SMEM((128, 128), I32),
             pltpu.SemaphoreType.DMA,
         ],
         compiler_params=pltpu.CompilerParams(vmem_limit_bytes=40 * 2**20),
@@ -217,71 +223,79 @@
     )(counts, owners.reshape(NBLK, BLK), cells.reshape(NBLK, BLK), profiles)
 
 
-def far_kernel(meta_ref, cells_ref, fw_ref, far_ref, add_ref):
-    table = cells_ref[...]
-    t0, t1 = split(table)
-    table2 = jnp.concatenate([t0, t1], axis=1)
+FAR_N = 4
+
+
+def far_kernel(side_ref, meta_ref, cells_ref, fw_ref, out_ref, add_ref, table):
     one, nil = jnp.ones((), F32), jnp.zeros((), F32)
-    fw = fw_ref[...]
-    fw0, fw1 = split(fw)
-    shape = (128, 128)
-    sub, lane = iota(shape, 0), iota(shape, 1)
+    m_rows = FAR_N * HALF
+
+    @pl.when(pl.program_id(0) == 0)
+    def _():
+        cells = cells_ref[...].reshape(ROWS // 4, 4, 128)
+        parts = [split(cells[:, q]) for q in range(4)]
+        table[...] = jnp.concatenate([p[0] for p in parts] + [p[1] for p in parts], axis=1)
+
+    fw0, fw1 = split(fw_ref[...])
+    sub, lane = iota((128, 128), 0), iota((128, 128), 1)
     ones8 = jnp.ones((8, 256), BF16)
-    cell_lane = iota((HALF, 128), 1)
-
-    def half(h):
-        first = 64 if h else 0
-        meta = meta_ref[0]
-        s128 = jnp.where(sub == first, one, nil)
-        r128 = jnp.where(sub == first + 1, one, nil) + jnp.where(sub == first + 2, 256.0 * one, nil)
-        pick = jnp.concatenate([s128, r128], axis=1).astype(BF16)
-        got = dot(meta, pick)
-        s_b = got[:, :128].astype(I32)
-        r_b = got[:, 128:].astype(I32)
+    place = iota((m_rows, 128), 1).astype(F32)
+    meta = meta_ref[...].reshape(m_rows, 128)
+    for i in range(FAR_N):
+        out_ref[i, 0:4] = side_ref[i, 0:4]
+    vals, picks = [], []
+    for h in range(2):
+        first = 0 if h == 0 else 64
+        col = jnp.where(sub == first, one, nil) + jnp.where(sub == first + 1, 128.0 * one, nil)
+        row = jnp.where(sub == first + 2, one, nil)
+        got = dot(meta, jnp.concatenate([col, row], axis=1).astype(BF16))
+        col, row = got[:, :128], got[:, 128:]
         hot = jnp.concatenate(
-            [jnp.where(r_b == cell_lane + 128 * k, one, nil).astype(BF16) for k in range(ROWS // 128)],
-            axis=1,
+            [jnp.where(row == place + 128.0 * q, one, nil).astype(BF16) for q in range(2)], axis=1
         )
-        val = dot(hot, table2)
-        val = val[:, :128] + val[:, 128:]
-        v0, v1 = split(jnp.where(s_b == cell_lane, val, nil))
+        val = dot(hot, table[...])
+        got = jnp.zeros((m_rows, 128), F32)
+        for q in range(4):
+            both = val[:, 128 * q : 128 * q + 128] + val[:, 512 + 128 * q : 640 + 128 * q]
+            got = jnp.where(col == place + 128.0 * q, both, got)
+        v0, v1 = split(got)
         v = jnp.concatenate([v0, v1], axis=1)
         far = dot_nt(ones8, v)
+        for i in range(FAR_N):
+            for q in range(2):
+                at = 256 * i + 128 * q
+                out_ref[i, 4 + 2 * h + q : 5 + 2 * h + q] = far[0:1, at : at + 128]
         mask = (lane >= 64) if h else (lane < 64)
         w0 = jnp.where(mask, fw0.astype(F32), nil).astype(BF16)
         w1 = jnp.where(mask, fw1.astype(F32), nil).astype(BF16)
-        return far, v, w0, w1
-
-    far_a, va, a0, a1 = half(0)
-    far_b, vb, b0, b1 = half(1)
-    far_ref[0] = jnp.concatenate([far_a, far_b], axis=1)
-    w = jnp.concatenate([jnp.concatenate([a0, a1], axis=1)] * 2, axis=0)
-    u = jnp.concatenate([jnp.concatenate([b0, b1], axis=1)] * 2, axis=0)
-    got = dot(va, w) + dot(vb, u)
-    add_ref[0] = got[:, :128] + got[:, 128:]
-
-
-def far_gather(meta, table, fw):
+        vals.append(v)
+        picks.append(jnp.concatenate([jnp.concatenate([w0, w1], axis=1)] * 2, axis=0))
+    got = dot(vals[0], picks[0]) + dot(vals[1], picks[1])
+    add_ref[...] = (got[:, :128] + got[:, 128:]).reshape(FAR_N, HALF, 128)
+
+
+def far_gather(rows, meta, table, fw):
+    side = pl.BlockSpec((FAR_N, 8, 128), lambda d: (d, HALF // 8, 0))
     return pl.pallas_call(
         far_kernel,
-        grid=(NT,),
+        grid=(NT // FAR_N,),
         out_shape=(
-            jax.ShapeDtypeStruct((NT, 8, MSG), F32),
+            jax.ShapeDtypeStruct((NT, LOAD, 128), F32),
             jax.ShapeDtypeStruct((NT, HALF, 128), F32),
         ),
         in_specs=[
-            pl.BlockSpec((1, HALF, 128), lambda d: (d, 0, 0)),
+            side,
+            pl.BlockSpec((FAR_N, HALF, 128), lambda d: (d, 0, 0)),
             pl.BlockSpec((ROWS, 128), lambda d: (0, 0)),
             pl.BlockSpec((1, 128), lambda d: (0, 0)),
         ],
-        out_specs=(
-            pl.BlockSpec((1, 8, MSG), lambda d: (d, 0, 0)),
-            pl.BlockSpec((1, HALF, 128), lambda d: (d, 0, 0)),
-        ),
-        compiler_params=pltpu.CompilerParams(vmem_limit_bytes=24 * 2**20),
-        cost_estimate=pl.CostEstimate(flops=16384 * 1024 * 512, bytes_accessed=8 << 20, transcendentals=0),
+        out_specs=(side, pl.BlockSpec((FAR_N, HALF, 128), lambda d: (d, 0, 0))),
+        scratch_shapes=[pltpu.VMEM((256, 1024), BF16)],
+        input_output_aliases={0: 0},
+        compiler_params=pltpu.CompilerParams(vmem_limit_bytes=32 * 2**20),
+        cost_estimate=pl.CostEstimate(flops=10**10, bytes_accessed=8 << 20, transcendentals=0),
         name="far_gather",
-    )(meta, table, fw)
+    )(rows, meta, table, fw)
 
 
 def step_weights(radial_step):
@@ -314,34 +328,39 @@
     return (got[:, :128] + got[:, 128:]) + (add + 0.25 * jnp.tanh(state))
 
 
+HEAT_N = 4
+
+
 def heat_kernel(rows_ref, add_ref, weights_ref, flux_ref, heat_ref):
     weights = weights_ref[...]
-    state = rows_ref[0]
+    state = rows_ref[...].reshape(HEAT_N * HALF, 128)
+    add = add_ref[...].reshape(HEAT_N * HALF, 128)
     total = jnp.zeros_like(state)
     for _ in range(SUB):
-        state = substep(state, add_ref[0], weights)
+        state = substep(state, add, weights)
         total = total + state
     t0, t1 = split(total)
     f0, f1 = split(flux_ref[...])
-    heat_ref[0] = dot_nt(f0, t0) + dot_nt(f0, t1) + dot_nt(f1, t0)
+    heat = dot_nt(f0, t0) + dot_nt(f0, t1) + dot_nt(f1, t0)
+    for i in range(HEAT_N):
+        heat_ref[i] = heat[:, HALF * i : HALF * i + HALF]
 
 
 def home_heat(rows, add, weights, flux):
+    block = pl.BlockSpec((HEAT_N, HALF, 128), lambda d: (d, 0, 0))
     return pl.pallas_call(
         heat_kernel,
-        grid=(NT,),
+        grid=(NT // HEAT_N,),
         out_shape=jax.ShapeDtypeStruct((NT, 8, HALF), F32),
         in_specs=[
-            pl.BlockSpec((1, HALF, 128), lambda d: (d, 0, 0)),
-            pl.BlockSpec((1, HALF, 128), lambda d: (d, 0, 0)),
+            block,
+            block,
             pl.BlockSpec((256, 256), lambda d: (0, 0)),
             pl.BlockSpec((8, 128), lambda d: (0, 0)),
         ],
-        out_specs=pl.BlockSpec((1, 8, HALF), lambda d: (d, 0, 0)),
-        compiler_params=pltpu.CompilerParams(vmem_limit_bytes=24 * 2**20),
-        cost_estimate=pl.CostEstimate(
-            flops=SUB * 8192 * 256 * 512, bytes_accessed=8 << 20, transcendentals=SUB << 20
-        ),
+        out_specs=pl.BlockSpec((HEAT_N, 8, HALF), lambda d: (d, 0, 0)),
+        compiler_params=pltpu.CompilerParams(vmem_limit_bytes=32 * 2**20),
+        cost_estimate=pl.CostEstimate(flops=2 * 10**10, bytes_accessed=8 << 20, transcendentals=SUB << 20),
         name="home_heat",
     )(rows, add, weights, flux)
 
@@ -386,67 +405,65 @@
     )(lanes, heat, stepped)
 
 
-def settle_kernel(amount_ref, slot_ref, rows_ref, far_ref, fw_ref, weights_ref, out_ref, stage, low_s, high_s):
+SETTLE = 1024
+
+
+def settle_kernel(amount_ref, slot_ref, rows_ref, fw_ref, weights_ref, out_ref, stage, comb):
     low_lanes = iota((HALF, 128), 1) < 64
-    pick = jnp.where(iota((8, 128), 0) == 0, 1.0, 0.0).astype(F32)
+    row8 = iota((8, MSG), 0)
+    pick = jnp.where(iota((8, 128), 0) < 2, 1.0, 0.0).astype(BF16)
     tn = (((0,), (0,)), ((), ()))
+
+    @pl.loop(0, NT, unroll=4)
+    def _(t):
+        rows = rows_ref[t, 0:HALF]
+        side = rows_ref[t, HALF : HALF + 8]
+        far = jnp.concatenate([side[4 + q : 5 + q] for q in range(4)], axis=1)
+        rest = far - far.astype(BF16).astype(F32)
+        terms = jnp.where(row8 == 0, far, jnp.where(row8 == 1, rest, 0.0)).astype(BF16)
+        col = lax.dot_general(terms, pick, tn, preferred_element_type=F32)
+        at = pl.multiple_of(t * MSG, MSG)
+        comb[pl.ds(at, HALF)] = jnp.where(low_lanes, rows, col[:HALF])
+        comb[pl.ds(pl.multiple_of(at + HALF, HALF), HALF)] = jnp.where(
+            low_lanes, pltpu.roll(rows, 64, 1), col[HALF:]
+        )
 
     @pl.loop(0, NT)
     def _(t):
-        rows = rows_ref[t]
-        far = far_ref[t]
-        f0, f1 = split(far)
-        col = lax.dot_general(f0, pick.astype(BF16), tn, preferred_element_type=F32)
-        col = col + lax.dot_general(f1, pick.astype(BF16), tn, preferred_element_type=F32)
-        low_s[...] = jnp.where(low_lanes, rows, col[:HALF])
-        high_s[...] = jnp.where(low_lanes, pltpu.roll(rows, 64, 1), col[HALF:])
-        amount = amount_ref[t]
-
-        @pl.loop(0, (jnp.minimum(amount, HALF) + 7) >> 3)
+        @pl.loop(0, (amount_ref[t] + 31) >> 5)
         def _(k):
-            at = pl.multiple_of(8 * k, 8)
-            for i in range(8):
-                stage[pl.ds(slot_ref[t, at + i], 1)] = low_s[pl.ds(at + i, 1)]
-
-        @pl.loop(0, (jnp.maximum(amount - HALF, 0) + 7) >> 3)
-        def _(k):
-            at = pl.multiple_of(8 * k, 8)
-            for i in range(8):
-                stage[pl.ds(slot_ref[t, HALF + at + i], 1)] = high_s[pl.ds(at + i, 1)]
+            at = pl.multiple_of(t * MSG + 32 * k, 32)
+            for i in range(32):
+                stage[pl.ds(slot_ref[at + i], 1)] = comb[pl.ds(at + i, 1)]
 
     weights = weights_ref[...]
     fw = fw_ref[...]
-
-    @pl.loop(0, OWN2 // HALF)
-    def _(c):
-        at = pl.multiple_of(c * HALF, HALF)
-        a = stage[pl.ds(at, HALF)]
-        b = stage[pl.ds(pl.multiple_of(at + OWN2, HALF), HALF)]
+    low_lanes = iota((SETTLE, 128), 1) < 64
+    for c in range(OWN2 // SETTLE):
+        at = c * SETTLE
+        a = stage[at : at + SETTLE]
+        b = stage[at + OWN2 : at + OWN2 + SETTLE]
         state = jnp.where(low_lanes, a, pltpu.roll(b, 64, 1))
         add = fw * jnp.where(low_lanes, pltpu.roll(a, 64, 1), b)
         for _ in range(SUB):
             state = substep(state, add, weights)
-        for k in range(HALF // 128):
+        for k in range(SETTLE // 128):
             turned = state[128 * k : 128 * k + 128].T
-            out_ref[:, pl.ds(pl.multiple_of(at + 128 * k, 128), 128)] = turned[:64]
-            out_ref[:, pl.ds(pl.multiple_of(at + OWN2 + 128 * k, 128), 128)] = turned[64:]
-
-
-def settle(amount, slots, rows, far, fw, weights):
+            out_ref[:, at + 128 * k : at + 128 * k + 128] = turned[:64]
+            out_ref[:, at + OWN2 + 128 * k : at + OWN2 + 128 * k + 128] = turned[64:]
+
+
+def settle(amount, slots, rows, fw, weights):
     vmem, smem = pl.BlockSpec(memory_space=pltpu.VMEM), pl.BlockSpec(memory_space=pltpu.SMEM)
     return pl.pallas_call(
         settle_kernel,
         out_shape=jax.ShapeDtypeStruct((PTS, OWN), F32),
-        in_specs=[smem, smem, vmem, vmem, vmem, vmem],
+        in_specs=[smem, smem, vmem, vmem, vmem],
         out_specs=vmem,
-        scratch_shapes=[
-            pltpu.VMEM((OWN + 8, 128), F32),
-            pltpu.VMEM((HALF, 128), F32),
-            pltpu.VMEM((HALF, 128), F32),
-        ],
-        compiler_params=pltpu.CompilerParams(vmem_limit_bytes=32 * 2**20),
+        scratch_shapes=[pltpu.VMEM((OWN + 8, 128), F32), pltpu.VMEM((NT * MSG, 128), F32)],
+        compiler_params=pltpu.CompilerParams(vmem_limit_bytes=40 * 2**20),
         name="settle",
-    )(amount, slots, rows, far, fw, weights)
+    )(amount, slots, rows, fw, weights)
 
 
 def halo(cells):
@@ -484,19 +501,15 @@
     fw = jnp.concatenate([far_weights, far_weights])[None, :]
     flux = flux_rows(flux_weights)
     rows, meta, lanes = route(counts, owners, cells, profiles)
-    got_rows = lax.all_to_all(rows, "tile", split_axis=0, concat_axis=0, tiled=True)
-    far, add = far_gather(meta, enthalpy.reshape(ROWS, 128), fw)
-    side = jnp.concatenate(
-        [lanes[:, 2].reshape(NT, 4, 128), far[:, 0].reshape(NT, 4, 128)], axis=1
-    )
-    got_side = lax.all_to_all(side, "tile", split_axis=0, concat_axis=0, tiled=True)
+    rows, add = far_gather(rows, meta, enthalpy.reshape(ROWS, 128), fw)
+    got = lax.all_to_all(rows, "tile", split_axis=0, concat_axis=0, tiled=True)
     heat = home_heat(rows, add, weights, flux)
-    stepped = stencil(enthalpy, *halo(enthalpy), velocity, diffusivity, wall_flux)
+    edges, heat = lax.optimization_barrier((enthalpy, heat))
+    stepped = stencil(enthalpy, *halo(edges), velocity, diffusivity, wall_flux)
     new_enthalpy = deposit(lanes, heat, stepped.reshape(ROWS, 128)).reshape(enthalpy.shape)
-    slots = got_side[:, :4].reshape(NT, MSG).astype(I32)
+    slots = got[:, HALF : HALF + 4].reshape(NT, MSG).astype(I32)
     amount = jnp.sum((slots < OWN).astype(I32), axis=1)
-    got_far = jnp.broadcast_to(got_side[:, 4:].reshape(NT, 1, MSG), (NT, 8, MSG))
-    new_profiles = settle(amount, slots, got_rows, got_far, fw, weights)
+    new_profiles = settle(amount, slots.reshape(-1), got, fw, weights)
     return new_enthalpy, new_profiles
 
 

time: 273 us -> 163 us (0.60)
  Pallas kernels: 205 us -> 98.6 us
  starting transfers between devices: 37.7 us -> 27.8 us
  waiting for transfers between devices: 5.63 us -> 9.81 us
    pallas_call x3, Pallas kernels: 130 us -> 61.4 us  [the longest x1 26.1 us: home_heat(): pl.pallas_call(heat_kernel, grid=(NT // HEAT_N,), out_shape=jax.ShapeDtyp...]
    pallas_call x1, Pallas kernels: 57.7 us -> 20.1 us  [settle(): pl.pallas_call(settle_kernel, out_shape=jax.ShapeDtypeStruct((PTS, OWN),...]
    all_to_all x2 -> x1, starting transfers between devices: 30.3 us -> 20.5 us  [on_device(): got = lax.all_to_all(rows, 'tile', split_axis=0, concat_axis=0, tiled=True)]
    all_to_all x2 -> x1, waiting for transfers between devices: 5.62 us -> 0.01 us  [on_device(): got = lax.all_to_all(rows, 'tile', split_axis=0, concat_axis=0, tiled=True)]
    ppermute x1, waiting for transfers between devices: 0.01 us -> 5.3 us  [halo(): after_s = lax.ppermute(cells[:, :, 0], 'tile', down_s)[:, :, None]]
    ppermute x1, waiting for transfers between devices: 0.01 us -> 4.5 us  [halo(): before_s = lax.ppermute(cells[:, :, -1], 'tile', up_s)[:, :, None]]
    unnamed x27 -> x19, local copies, waits for them, and re-layouts: 8.47 us -> 11.3 us
  transfers between devices with their start and end apart: 6 -> 5, of which waited for: 1 -> 2; matrix products, arithmetic and copies ran while one was open for 5% -> 5% of each run, Pallas kernels for 54% -> 27%
where the time goes in v2:
time: 163 us; the launch traced here: 162 us
  Pallas kernels  98.6 us (60%)
  starting transfers between devices  27.8 us (17%)
  local copies, waits for them, and re-layouts  18.5 us (11%)
  waiting for transfers between devices  9.81 us (6%)
  other arithmetic  5.94 us (4%)
    pallas_call x1, Pallas kernels, home_heat(): pl.pallas_call(heat_kernel, grid=(NT // HEAT_N,), out_shape=jax.ShapeDtyp...  26.1 us
    all_to_all x1, starting transfers between devices, on_device(): got = lax.all_to_all(rows, 'tile', split_axis=0, concat_axis=0, tiled=True)  20.5 us
    pallas_call x1, Pallas kernels, settle(): pl.pallas_call(settle_kernel, out_shape=jax.ShapeDtypeStruct((PTS, OWN),...  20.1 us
    pallas_call x1, Pallas kernels, far_gather(): pl.pallas_call(far_kernel, grid=(NT // FAR_N,), out_shape=(jax.ShapeDtype...  19.9 us
    pallas_call x1, Pallas kernels, deposit(): pl.pallas_call(deposit_kernel, grid=(NT,), out_shape=jax.ShapeDtypeStruct...  17.1 us
    pallas_call x1, Pallas kernels, route(): pl.pallas_call(route_kernel, out_shape=(jax.ShapeDtypeStruct((NT, LOAD, 1...  15.5 us
    unnamed x19, local copies, waits for them, and re-layouts  11.3 us
    ppermute x1, waiting for transfers between devices, halo(): after_s = lax.ppermute(cells[:, :, 0], 'tile', down_s)[:, :, None]  5.3 us
  transfers between devices with their start and end apart: 5, of which 2 were waited for; matrix products, arithmetic and copies ran while one was open for 5% of the time, Pallas kernels for 27%

profile of v2, /device:TPU:35, one launch (start us, length us, event | category | flops | bytes accessed | tf_op | source)
XLA Modules:
  0.0 162.1 jit_solution(15615688242378277714)
XLA Ops:
  1.3 0.9 reshape.24.owners_ref
  2.2 0.9 reshape.25.cells_ref
  3.1 0.8 maximum_bitcast_fusion.fw_ref
  3.9 2.2 %copy-done.3 = f32[64,16384]{1,0:T(8,128)S(1)} copy-done((f32[64,16384]{1,0:T(8,128)S(1)}, f32[64,16384]{1,0:T(8,128)}, u32[]{:S(2)}) %copy-start.3) | copy-done | bytes 4194328
  6.1 15.5 %route.1 = (f32[32,264,128]{2,1,0:T(8,128)S(1)}, bf16[32,256,128]{2,1,0:T(8,128)(2,1)S(1)}, f32[32,8,512]{2,1,0:T(8,128)S(1)}) custom-call(s32[1]{0:T(128)S(6)} %copy.23.count_ref, s32[64,256]{1,0:T(8,128)S(1)} %reshape.24.owners_ref, s32[64,256]{1,0:T(8,128)S(1)} %reshape.25.cells_ref, f32[64,16384]{1,0:T(8,128)S(1)} %copy-done.3), custom_call_target="tpu_custom_call" | custom-call | tf_op jit(solution)/shard_map/route/pallas_call | solution.py:204
  21.6 19.9 %far_gather.1 = (f32[32,264,128]{2,1,0:T(8,128)S(1)}, f32[32,256,128]{2,1,0:T(8,128)S(1)}) custom-call(f32[32,264,128]{2,1,0:T(8,128)S(1)} %get-tuple-element.10.side_ref, bf16[32,256,128]{2,1,0:T(8,128)(2,1)S(1)} %get-tuple-element.11.meta_ref, f32[1024,128]{1,0:T(8,128)S(1)} %bitcast.17, ...), custom_call_target="tpu_custom_call", output_to_operand_aliasing={{0}: (0, {})} | custom-call | flops 10000000000 | bytes 8388608 | tf_op jit(solution)/shard_map/far_gather/pallas_call | solution.py:279
  41.4 2.0 %copy-done.1 = f32[32,264,128]{2,1,0:T(8,128)} copy-done((f32[32,264,128]{2,1,0:T(8,128)}, f32[32,264,128]{2,1,0:T(8,128)S(1)}, u32[]{:S(2)}) %copy-start.1) | copy-done | bytes 4325400
  43.4 2.0 %copy-done.4 = f32[32,256,128]{2,1,0:T(8,128)} copy-done((f32[32,256,128]{2,1,0:T(8,128)}, f32[32,256,128]{2,1,0:T(8,128)S(1)}, u32[]{:S(2)}) %copy-start.4) | copy-done | bytes 4194328
  45.4 20.5 %all-to-all-start = ((f32[32,264,128]{2,1,0:T(8,128)}), f32[32,264,128]{2,1,0:T(8,128)}, u32[]{:S(2)}, u32[]{:S(2)}) async-start(f32[32,264,128]{2,1,0:T(8,128)} %copy-done.1), calls=%async_computation | async-start | bytes 8650752 | tf_op jit(solution)/shard_map/all_to_all | solution.py:505
  66.1 0.1 reduce-precision_convert_fusion
  66.5 2.2 %copy-done.2 = f32[32,264,128]{2,1,0:T(8,128)S(1)} copy-done((f32[32,264,128]{2,1,0:T(8,128)S(1)}, f32[32,264,128]{2,1,0:T(8,128)}, u32[]{:S(2)}) %copy-start.2) | copy-done | bytes 4325400
  68.7 2.2 %copy-done.5 = f32[32,256,128]{2,1,0:T(8,128)S(1)} copy-done((f32[32,256,128]{2,1,0:T(8,128)S(1)}, f32[32,256,128]{2,1,0:T(8,128)}, u32[]{:S(2)}) %copy-start.5) | copy-done | bytes 4194328
  70.9 26.1 %home_heat.1.heat_ref = f32[32,8,256]{2,1,0:T(8,128)S(1)} custom-call(f32[32,264,128]{2,1,0:T(8,128)S(1)} %copy-done.2, f32[32,256,128]{2,1,0:T(8,128)S(1)} %copy-done.5, bf16[256,256]{1,0:T(8,128)(2,1)S(1)} %maximum_maximum_fusion.weights_ref, f32[8,128]{1,0:T(8,128)S(1)} %maximum_multiply_fusion.flux_ref), custom_call_target="tpu_custom_call" | custom-call | flops 20000000000 | bytes 8388608 | tf_op jit(solution)/shard_map/home_heat/pallas_call | solution.py:351
  97.0 0.7 fusion.8
  97.6 1.9 %collective-permute-start.1 = (f32[1,64,128]{2,1,0:T(8,128)}, f32[1,64,128]{2,1,0:T(8,128)}, u32[]{:S(2)}, u32[]{:S(2)}) collective-permute-start(f32[1,64,128]{2,1,0:T(8,128)} %get-tuple-element.19), channel_id=1, source_target_pairs={{32,0},{64,32},{96,64},{33,1},{65,33},{97,65},{34,2},{66,34},{98,6... | collective-permute-start | bytes 98312 | tf_op jit(solution)/shard_map/ppermute | solution.py:476
  99.5 0.5 copy.18
  100.1 1.5 collective-permute-start.2
  101.6 3.8 %collective-permute-start = (f32[1,64,128]{2,1,0:T(8,128)}, f32[1,64,128]{2,1,0:T(8,128)}, u32[]{:S(2)}, u32[]{:S(2)}) collective-permute-start(f32[1,64,128]{2,1,0:T(8,128)} %get-tuple-element.18), channel_id=1, source_target_pairs={{0,32},{32,64},{64,96},{1,33},{33,65},{65,97},{2,34},{34,66},{66,9... | collective-permute-start | bytes 98312 | tf_op jit(solution)/shard_map/ppermute | solution.py:475
  105.4 0.6 fusion.12
  106.0 1.1 fusion.9
  107.1 0.1 fusion.11
  107.2 1.1 fusion.10
  108.3 4.5 %collective-permute-done.2 = f32[16,64]{1,0:T(8,128)S(1)} collective-permute-done((f32[16,64]{1,0:T(8,128)S(1)}, f32[16,64]{1,0:T(8,128)S(1)}, u32[]{:S(2)}, u32[]{:S(2)}) %collective-permute-start.2) | collective-permute-done | bytes 4128 | tf_op jit(solution)/shard_map/ppermute | solution.py:477
  112.8 0.2 copy.19
  113.1 5.3 %collective-permute-done.3 = f32[16,64]{1,0:T(8,128)S(1)} collective-permute-done((f32[16,64]{1,0:T(8,128)S(1)}, f32[16,64]{1,0:T(8,128)S(1)}, u32[]{:S(2)}, u32[]{:S(2)}) %collective-permute-start.3) | collective-permute-done | bytes 4128 | tf_op jit(solution)/shard_map/ppermute | solution.py:478
  118.4 0.6 copy-done.7
  119.0 0.9 copy.21
  119.9 2.5 %fusion.6 = f32[16,64,128]{2,1,0:T(8,128)S(1)} fusion(f32[16,64,128]{2,1,0:T(8,128)S(1)} %copy-done, f32[16,64,128]{2,1,0:T(8,128)} %param.13, f32[1,64,128]{2,1,0:T(8,128)} %collective-permute-done.1, f32[15,64,128]{2,1,0:T(8,128)} %get-tuple-element.21, f32[16,63,128]{2,1,0:T(8,128)S(1)} %get-tuple-element.25, f32[16,1,128]{2,1,0:T(1,128)} %get-tuple-element.27, ...), kind=kLoop, calls=%fused_computation.8 | loop fusion | flops 2621440 | bytes 5251136 | tf_op jit(solution)/shard_map/add | solution.py:493
  122.4 17.1 %deposit.1 = f32[1024,128]{1,0:T(8,128)} custom-call(f32[32,8,512]{2,1,0:T(8,128)S(1)} %get-tuple-element.9.lanes_ref, f32[32,8,256]{2,1,0:T(8,128)S(1)} %home_heat.1.heat_ref, f32[1024,128]{1,0:T(8,128)S(1)} %bitcast.18), custom_call_target="tpu_custom_call" | custom-call | flops 8589934592 | bytes 2097152 | tf_op jit(solution)/shard_map/deposit/pallas_call | solution.py:391
  139.5 1.6 convert_reduce_fusion.amount_ref
  141.1 0.9 slice_convert_fusion
  142.0 20.1 %settle.1 = f32[64,6144]{1,0:T(8,128)} custom-call(s32[32]{0:T(128)S(1)} %convert_reduce_fusion.amount_ref, s32[16384]{0:T(1024)S(1)} %bitcast.19, f32[32,264,128]{2,1,0:T(8,128)} %all-to-all-done.rows_ref, f32[1,128]{1,0:T(1,128)S(1)} %maximum_bitcast_fusion.fw_ref, bf16[256,256]{1,0:T(8,128)(2,1)S(1)} %maximum_maximum_fusion.weights_ref), custom_call_target="tpu_custom_call" | custom-call | tf_op jit(solution)/shard_map/settle/pallas_call | solution.py:458
  (26 shorter events, 0.4 us)
Async XLA Ops:
  0.6 20.9 %copy-start = (f32[16,64,128]{2,1,0:T(8,128)S(1)}, f32[16,64,128]{2,1,0:T(8,128)}, u32[]{:S(2)}) copy-start(f32[16,64,128]{2,1,0:T(8,128)} %param.11) | copy-start | bytes 1572868
  3.9 2.2 %copy-start.3 = (f32[64,16384]{1,0:T(8,128)S(1)}, f32[64,16384]{1,0:T(8,128)}, u32[]{:S(2)}) copy-start(f32[64,16384]{1,0:T(8,128)} %prof_ref.1) | copy-start | bytes 12582916
  41.4 2.0 %copy-start.1 = (f32[32,264,128]{2,1,0:T(8,128)}, f32[32,264,128]{2,1,0:T(8,128)S(1)}, u32[]{:S(2)}) copy-start(f32[32,264,128]{2,1,0:T(8,128)S(1)} %get-tuple-element.12.rows_ref) | copy-start | bytes 12976132
  43.4 2.0 %copy-start.4 = (f32[32,256,128]{2,1,0:T(8,128)}, f32[32,256,128]{2,1,0:T(8,128)S(1)}, u32[]{:S(2)}) copy-start(f32[32,256,128]{2,1,0:T(8,128)S(1)} %get-tuple-element.13.add_ref) | copy-start | bytes 12582916
  45.4 20.5 %copy-start.6 = (f32[64,64]{1,0:T(8,128)S(1)}, f32[64,64]{1,0:T(8,128)}, u32[]{:S(2)}) copy-start(f32[64,64]{1,0:T(8,128)} %param.19) | copy-start | bytes 49156
  45.4 20.7 %copy-start.8 = (f32[64]{0:T(128)S(1)}, f32[64]{0:T(128)}, u32[]{:S(2)}) copy-start(f32[64]{0:T(128)} %param.21) | copy-start | bytes 772
  45.4 94.1 %all-to-all-start = ((f32[32,264,128]{2,1,0:T(8,128)}), f32[32,264,128]{2,1,0:T(8,128)}, u32[]{:S(2)}, u32[]{:S(2)}) async-start(f32[32,264,128]{2,1,0:T(8,128)} %copy-done.1), calls=%async_computation | async-start | bytes 8650752 | tf_op jit(solution)/shard_map/all_to_all | solution.py:505
  66.5 2.2 %copy-start.2 = (f32[32,264,128]{2,1,0:T(8,128)S(1)}, f32[32,264,128]{2,1,0:T(8,128)}, u32[]{:S(2)}) copy-start(f32[32,264,128]{2,1,0:T(8,128)} %copy-done.1) | copy-start | bytes 12976132
  68.7 2.2 %copy-start.5 = (f32[32,256,128]{2,1,0:T(8,128)S(1)}, f32[32,256,128]{2,1,0:T(8,128)}, u32[]{:S(2)}) copy-start(f32[32,256,128]{2,1,0:T(8,128)} %copy-done.4) | copy-start | bytes 12582916
  97.6 22.3 %collective-permute-start.1 = (f32[1,64,128]{2,1,0:T(8,128)}, f32[1,64,128]{2,1,0:T(8,128)}, u32[]{:S(2)}, u32[]{:S(2)}) collective-permute-start(f32[1,64,128]{2,1,0:T(8,128)} %get-tuple-element.19), channel_id=1, source_target_pairs={{32,0},{64,32},{96,64},{33,1},{65,33},{97,65},{34,2},{66,34},{98,6... | collective-permute-start | bytes 98312 | tf_op jit(solution)/shard_map/ppermute | solution.py:476
  100.1 12.8 %collective-permute-start.2 = (f32[16,64]{1,0:T(8,128)S(1)}, f32[16,64]{1,0:T(8,128)S(1)}, u32[]{:S(2)}, u32[]{:S(2)}) collective-permute-start(f32[16,64]{1,0:T(8,128)S(1)} %get-tuple-element.17), channel_id=1, source_target_pairs={{0,1},{1,2},{2,3},{3,4},{4,5},{5,6},{6,7},{7,8},{8,9},{9,10},{10,1... | collective-permute-start | bytes 12296 | tf_op jit(solution)/shard_map/ppermute | solution.py:477
  101.6 16.8 %collective-permute-start.3 = (f32[16,64]{1,0:T(8,128)S(1)}, f32[16,64]{1,0:T(8,128)S(1)}, u32[]{:S(2)}, u32[]{:S(2)}) collective-permute-start(f32[16,64]{1,0:T(8,128)S(1)} %get-tuple-element.16), channel_id=1, source_target_pairs={{1,0},{2,1},{3,2},{4,3},{5,4},{6,5},{7,6},{8,7},{9,8},{10,9},{11,1... | collective-permute-start | bytes 12296 | tf_op jit(solution)/shard_map/ppermute | solution.py:478
  101.6 18.4 %collective-permute-start = (f32[1,64,128]{2,1,0:T(8,128)}, f32[1,64,128]{2,1,0:T(8,128)}, u32[]{:S(2)}, u32[]{:S(2)}) collective-permute-start(f32[1,64,128]{2,1,0:T(8,128)} %get-tuple-element.18), channel_id=1, source_target_pairs={{0,32},{32,64},{64,96},{1,33},{33,65},{65,97},{2,34},{34,66},{66,9... | collective-permute-start | bytes 98312 | tf_op jit(solution)/shard_map/ppermute | solution.py:475
  118.4 0.6 copy-start.7

commit v3 on v2

--- a/solution.py
+++ b/solution.py
@@ -19,6 +19,8 @@
 ROWS = 1024
 OWN2 = OWN // 2
 
+ROOM = 60 * 2**20
+
 F32, BF16, I32 = jnp.float32, jnp.bfloat16, jnp.int32
 NTD = (((1,), (1,)), ((), ()))
 
@@ -43,16 +45,24 @@
 def route_kernel(
     count_ref, owners_ref, cells_ref, prof_ref,
     rows_ref, meta_ref, lanes_ref,
-    pos_s, m0_s, m1_s, m2_s, m3_s, m4_s, sorted_a, sorted_b, bucket, tab_v, tab_s, sem,
+    pos_s, m0_s, m1_s, m2_s, m3_s, m4_s, sorted_a, sorted_b, sorted_c, sorted_d,
+    bucket, tab_v, tab_s, sem, prof_v, prof_sem, pack_v, pack_sem,
 ):
     count = count_ref[0]
+    fetch = pltpu.make_async_copy(prof_ref, prof_v, prof_sem)
+    fetch.start()
+
+    def blocks(ref):
+        x = ref[...].reshape(NBLK, 2, 128)
+        return jnp.concatenate([x[:, 0], x[:, 1]], axis=1)
+
     slot = iota((NBLK, BLK), 0) * BLK + iota((NBLK, BLK), 1)
-    owners = owners_ref[...]
+    owners = blocks(owners_ref)
     dest = jnp.floor((owners.astype(F32) + 0.5) * (1.0 / OWN)).astype(I32)
     within = owners - dest * OWN
     live = slot < count
     dest = jnp.where(live, dest, NT)
-    cells = cells_ref[...]
+    cells = blocks(cells_ref)
     m0_s[...] = (cells & 127).astype(F32)
     m1_s[...] = ((cells >> 7) & 3).astype(F32)
     m2_s[...] = (cells >> 9).astype(F32)
@@ -71,6 +81,7 @@
     ones_a = jnp.ones((8, BLK), BF16)
     ones_b = jnp.ones((BLK, 128), BF16)
     run = jnp.zeros((8, BLK), F32)
+    longest = jnp.zeros((8, BLK), F32)
     for c in range(8):
         part = dest[8 * c : 8 * c + 8]
         hot = jnp.where(part[:, None, :] == iota((8, NT, BLK), 1), one, nil).reshape(BLK, BLK)
@@ -86,6 +97,7 @@
         src = dot(amount_lb, seg_right)
         base = dot(amount_lb, base_right) + run
         run = run + dot(amount_lb, all_right)
+        longest = jnp.maximum(longest, amount_l)
         most = amount_l
         for shift in (1, 2, 4, 8, 16):
             most = jnp.maximum(most, pltpu.roll(most, BLK - shift, 1))
@@ -100,6 +112,7 @@
         tab_v[16 * c + 8 : 16 * c + 16] = packed[:, 128:]
     copy = pltpu.make_async_copy(tab_v, tab_s, sem)
     copy.start()
+    short = jnp.max(longest) <= 8.0
     total = run
 
     zero8 = jnp.zeros((STRIDE, 128), F32)
@@ -109,13 +122,14 @@
         bucket[pl.ds(pl.multiple_of(d * STRIDE, 8), STRIDE)] = zero8
 
     copy.wait()
+    fetch.wait()
 
     meta_rest = jnp.zeros((56, BLK), BF16)
     low_rest = jnp.zeros((64, BLK), BF16)
     row8 = iota((8, BLK), 0)
 
     def sort_block(j, out):
-        x = prof_ref[:, pl.ds(pl.multiple_of(j * BLK, BLK), BLK)]
+        x = prof_v[:, pl.ds(pl.multiple_of(j * BLK, BLK), BLK)]
         high, low = split(x)
         meta = jnp.zeros((8, BLK), F32)
         for k, ref in enumerate((m0_s, m1_s, m2_s, m3_s, m4_s)):
@@ -156,17 +170,34 @@
                 def _(k):
                     bucket[pl.ds(dst + 8 * k, 8)] = inp[pl.ds(src + 8 * k, 8)]
 
-    sorted_a[BLK:] = jnp.zeros((16, 128), F32)
-    sorted_b[BLK:] = jnp.zeros((16, 128), F32)
-    pairs = (count + 2 * BLK - 1) // (2 * BLK)
+    def copy_short(j, inp):
+        chunk = (j >> 2) * 8
+        at = (j & 3) * NT
+        for d in range(NT):
+            src = tab_s[chunk, at + d]
+            dst = tab_s[chunk + 1, at + d]
+            bucket[pl.ds(dst, 8)] = inp[pl.ds(src, 8)]
+
+    for ref in (sorted_a, sorted_b, sorted_c, sorted_d):
+        ref[BLK:] = jnp.zeros((16, 128), F32)
+    quads = (count + 4 * BLK - 1) // (4 * BLK)
     sort_block(0, sorted_a)
-
-    @pl.loop(0, pairs)
-    def _(p):
-        sort_block(2 * p + 1, sorted_b)
-        copy_block(2 * p, sorted_a)
-        sort_block(jnp.minimum(2 * p + 2, NBLK - 1), sorted_a)
-        copy_block(2 * p + 1, sorted_b)
+    sort_block(1, sorted_b)
+
+    def quad(copy_any):
+        @pl.loop(0, quads)
+        def _(p):
+            sort_block(4 * p + 2, sorted_c)
+            copy_any(4 * p, sorted_a)
+            sort_block(4 * p + 3, sorted_d)
+            copy_any(4 * p + 1, sorted_b)
+            sort_block(jnp.minimum(4 * p + 4, NBLK - 1), sorted_a)
+            copy_any(4 * p + 2, sorted_c)
+            sort_block(jnp.minimum(4 * p + 5, NBLK - 1), sorted_b)
+            copy_any(4 * p + 3, sorted_d)
+
+    pl.when(short)(lambda: quad(copy_short))
+    pl.when(jnp.logical_not(short))(lambda: quad(copy_block))
 
     low_lanes = iota((HALF, 128), 1) < 64
     r8, l8 = iota((8, 128), 0), iota((8, 128), 1)
@@ -180,23 +211,34 @@
     rank_row = iota((8, MSG), 0)
     lane_dest = iota((8, BLK), 1)
 
-    @pl.loop(0, NT, unroll=4)
-    def _(d):
-        at = pl.multiple_of(d * STRIDE, 8)
-        lo = bucket[pl.ds(at, HALF)]
-        hi = bucket[pl.ds(pl.multiple_of(at + HALF, 8), HALF)]
-        rows_ref[d, 0:HALF] = jnp.where(low_lanes, lo, pltpu.roll(hi, 64, 1))
-        meta_ref[d] = jnp.where(low_lanes, pltpu.roll(lo, 64, 1), hi).astype(BF16)
-        both = jnp.concatenate([lo, hi], axis=0).astype(BF16)
-        nums = dot_nt(pick, both)
-        mine = jnp.max(jnp.where(lane_dest == d, total, nil), axis=1, keepdims=True)
-        valid = rank.astype(F32) < mine
-        nums = jnp.where((rank_row == 2) & ~valid, float(OWN), nums)
-        nums = jnp.where(rank_row == 3, jnp.where(valid, one, nil), nums)
-        lanes_ref[d] = nums
-        rows_ref[d, HALF : HALF + 8] = jnp.concatenate(
-            [nums[2:3, 128 * q : 128 * q + 128] for q in range(4)] + [jnp.zeros((4, 128), F32)], axis=0
-        )
+    def send(g):
+        part = pl.ds(g * 4, 4)
+        return pltpu.make_async_copy(pack_v.at[part], rows_ref.at[part], pack_sem.at[g])
+
+    @pl.loop(0, NT // 4)
+    def _(g):
+        for k in range(4):
+            d = 4 * g + k
+            at = pl.multiple_of(d * STRIDE, 8)
+            lo = bucket[pl.ds(at, HALF)]
+            hi = bucket[pl.ds(pl.multiple_of(at + HALF, 8), HALF)]
+            pack_v[d, 0:HALF] = jnp.where(low_lanes, lo, pltpu.roll(hi, 64, 1))
+            meta_ref[d] = jnp.where(low_lanes, pltpu.roll(lo, 64, 1), hi).astype(BF16)
+            both = jnp.concatenate([lo, hi], axis=0).astype(BF16)
+            nums = dot_nt(pick, both)
+            mine = jnp.max(jnp.where(lane_dest == d, total, nil), axis=1, keepdims=True)
+            valid = rank.astype(F32) < mine
+            nums = jnp.where((rank_row == 2) & ~valid, float(OWN), nums)
+            nums = jnp.where(rank_row == 3, jnp.where(valid, one, nil), nums)
+            lanes_ref[d] = nums
+            pack_v[d, HALF:LOAD] = jnp.concatenate(
+                [nums[2:3, 128 * q : 128 * q + 128] for q in range(4)] + [jnp.zeros((4, 128), F32)],
+                axis=0,
+            )
+        send(g).start()
+
+    for g in range(NT // 4):
+        send(g).wait()
 
 
 def route(counts, owners, cells, profiles):
@@ -208,25 +250,29 @@
             jax.ShapeDtypeStruct((NT, HALF, 128), BF16),
             jax.ShapeDtypeStruct((NT, 8, MSG), F32),
         ),
-        in_specs=[pl.BlockSpec(memory_space=pltpu.SMEM), vmem, vmem, vmem],
-        out_specs=(vmem, vmem, vmem),
+        in_specs=[pl.BlockSpec(memory_space=pltpu.SMEM), vmem, vmem, pl.BlockSpec(memory_space=pl.ANY)],
+        out_specs=(pl.BlockSpec(memory_space=pl.ANY), vmem, vmem),
         scratch_shapes=[pltpu.VMEM((NBLK, BLK), F32)] * 6
-        + [pltpu.VMEM((BLK + 16, 128), F32)] * 2
+        + [pltpu.VMEM((BLK + 16, 128), F32)] * 4
         + [
             pltpu.VMEM((NT * STRIDE, 128), F32),
             pltpu.VMEM((128, 128), I32),
             pltpu.SMEM((128, 128), I32),
             pltpu.SemaphoreType.DMA,
+            pltpu.VMEM((PTS, CAP), F32),
+            pltpu.SemaphoreType.DMA,
+            pltpu.VMEM((NT, LOAD, 128), F32),
+            pltpu.SemaphoreType.DMA((NT // 4,)),
         ],
-        compiler_params=pltpu.CompilerParams(vmem_limit_bytes=40 * 2**20),
+        compiler_params=pltpu.CompilerParams(vmem_limit_bytes=ROOM),
         name="route",
-    )(counts, owners.reshape(NBLK, BLK), cells.reshape(NBLK, BLK), profiles)
+    )(counts, owners.reshape(128, 128), cells.reshape(128, 128), profiles)
 
 
 FAR_N = 4
 
 
-def far_kernel(side_ref, meta_ref, cells_ref, fw_ref, out_ref, add_ref, table):
+def far_kernel(side_ref, meta_ref, cells_ref, out_ref, table):
     one, nil = jnp.ones((), F32), jnp.zeros((), F32)
     m_rows = FAR_N * HALF
 
@@ -236,14 +282,12 @@
         parts = [split(cells[:, q]) for q in range(4)]
         table[...] = jnp.concatenate([p[0] for p in parts] + [p[1] for p in parts], axis=1)
 
-    fw0, fw1 = split(fw_ref[...])
-    sub, lane = iota((128, 128), 0), iota((128, 128), 1)
+    sub = iota((128, 128), 0)
     ones8 = jnp.ones((8, 256), BF16)
     place = iota((m_rows, 128), 1).astype(F32)
     meta = meta_ref[...].reshape(m_rows, 128)
     for i in range(FAR_N):
         out_ref[i, 0:4] = side_ref[i, 0:4]
-    vals, picks = [], []
     for h in range(2):
         first = 0 if h == 0 else 64
         col = jnp.where(sub == first, one, nil) + jnp.where(sub == first + 1, 128.0 * one, nil)
@@ -265,37 +309,26 @@
             for q in range(2):
                 at = 256 * i + 128 * q
                 out_ref[i, 4 + 2 * h + q : 5 + 2 * h + q] = far[0:1, at : at + 128]
-        mask = (lane >= 64) if h else (lane < 64)
-        w0 = jnp.where(mask, fw0.astype(F32), nil).astype(BF16)
-        w1 = jnp.where(mask, fw1.astype(F32), nil).astype(BF16)
-        vals.append(v)
-        picks.append(jnp.concatenate([jnp.concatenate([w0, w1], axis=1)] * 2, axis=0))
-    got = dot(vals[0], picks[0]) + dot(vals[1], picks[1])
-    add_ref[...] = (got[:, :128] + got[:, 128:]).reshape(FAR_N, HALF, 128)
-
-
-def far_gather(rows, meta, table, fw):
+
+
+def far_gather(rows, meta, table):
     side = pl.BlockSpec((FAR_N, 8, 128), lambda d: (d, HALF // 8, 0))
     return pl.pallas_call(
         far_kernel,
         grid=(NT // FAR_N,),
-        out_shape=(
-            jax.ShapeDtypeStruct((NT, LOAD, 128), F32),
-            jax.ShapeDtypeStruct((NT, HALF, 128), F32),
-        ),
+        out_shape=jax.ShapeDtypeStruct((NT, LOAD, 128), F32),
         in_specs=[
             side,
             pl.BlockSpec((FAR_N, HALF, 128), lambda d: (d, 0, 0)),
             pl.BlockSpec((ROWS, 128), lambda d: (0, 0)),
-            pl.BlockSpec((1, 128), lambda d: (0, 0)),
         ],
-        out_specs=(side, pl.BlockSpec((FAR_N, HALF, 128), lambda d: (d, 0, 0))),
+        out_specs=side,
         scratch_shapes=[pltpu.VMEM((256, 1024), BF16)],
         input_output_aliases={0: 0},
-        compiler_params=pltpu.CompilerParams(vmem_limit_bytes=32 * 2**20),
+        compiler_params=pltpu.CompilerParams(vmem_limit_bytes=ROOM),
         cost_estimate=pl.CostEstimate(flops=10**10, bytes_accessed=8 << 20, transcendentals=0),
         name="far_gather",
-    )(rows, meta, table, fw)
+    )(rows, meta, table)
 
 
 def step_weights(radial_step):
@@ -331,10 +364,24 @@
 HEAT_N = 4
 
 
-def heat_kernel(rows_ref, add_ref, weights_ref, flux_ref, heat_ref):
+def far_columns(side):
+    far = jnp.concatenate([side[4 + q : 5 + q] for q in range(4)], axis=1)
+    rest = far - far.astype(BF16).astype(F32)
+    row8 = iota((8, MSG), 0)
+    terms = jnp.where(row8 == 0, far, jnp.where(row8 == 1, rest, 0.0)).astype(BF16)
+    pick = jnp.where(iota((8, 128), 0) < 2, 1.0, 0.0).astype(BF16)
+    return lax.dot_general(terms, pick, (((0,), (0,)), ((), ())), preferred_element_type=F32)
+
+
+def heat_kernel(rows_ref, side_ref, fw_ref, weights_ref, flux_ref, heat_ref):
     weights = weights_ref[...]
     state = rows_ref[...].reshape(HEAT_N * HALF, 128)
-    add = add_ref[...].reshape(HEAT_N * HALF, 128)
+    low_lanes = iota((HALF, 128), 1) < 64
+    adds = []
+    for i in range(HEAT_N):
+        far = far_columns(side_ref[i])
+        adds.append(fw_ref[...] * jnp.where(low_lanes, far[:HALF], far[HALF:]))
+    add = jnp.concatenate(adds, axis=0)
     total = jnp.zeros_like(state)
     for _ in range(SUB):
         state = substep(state, add, weights)
@@ -346,7 +393,7 @@
         heat_ref[i] = heat[:, HALF * i : HALF * i + HALF]
 
 
-def home_heat(rows, add, weights, flux):
+def home_heat(rows, fw, weights, flux):
     block = pl.BlockSpec((HEAT_N, HALF, 128), lambda d: (d, 0, 0))
     return pl.pallas_call(
         heat_kernel,
@@ -354,18 +401,25 @@
         out_shape=jax.ShapeDtypeStruct((NT, 8, HALF), F32),
         in_specs=[
             block,
-            block,
+            pl.BlockSpec((HEAT_N, 8, 128), lambda d: (d, HALF // 8, 0)),
+            pl.BlockSpec((1, 128), lambda d: (0, 0)),
             pl.BlockSpec((256, 256), lambda d: (0, 0)),
             pl.BlockSpec((8, 128), lambda d: (0, 0)),
         ],
         out_specs=pl.BlockSpec((HEAT_N, 8, HALF), lambda d: (d, 0, 0)),
-        compiler_params=pltpu.CompilerParams(vmem_limit_bytes=32 * 2**20),
+        compiler_params=pltpu.CompilerParams(vmem_limit_bytes=ROOM),
         cost_estimate=pl.CostEstimate(flops=2 * 10**10, bytes_accessed=8 << 20, transcendentals=SUB << 20),
         name="home_heat",
-    )(rows, add, weights, flux)
-
-
-def deposit_kernel(lanes_ref, heat_ref, stepped_ref, out_ref, acc):
+    )(rows, rows, fw, weights, flux)
+
+
+DEP_N = 4
+
+
+def deposit_kernel(
+    lanes_ref, heat_ref, cells_ref, vel_ref, dif_ref, flux_ref, below_ref, above_ref, left_ref, right_ref,
+    out_ref, acc,
+):
     d = pl.program_id(0)
 
     @pl.when(d == 0)
@@ -373,36 +427,72 @@
         acc[...] = jnp.zeros_like(acc)
 
     one, nil = jnp.ones((), F32), jnp.zeros((), F32)
-    nums = lanes_ref[0]
-    s, r, valid = nums[0:1].astype(I32), nums[1:2].astype(I32), nums[3:4]
-    heat = jnp.concatenate([heat_ref[0, 0:1], heat_ref[0, 1:2]], axis=1)
-    heat = jnp.where(valid > 0.5, 0.5 * heat, nil)
-    spread = jnp.where(s == iota((128, MSG), 0), heat, nil)
-    h0, h1 = split(spread)
-    hot = jnp.where(r == iota((ROWS, MSG), 0), one, nil).astype(BF16)
-    acc[...] += dot_nt(hot, jnp.concatenate([h0, h1], axis=0))
-
-    @pl.when(d == NT - 1)
+    width = DEP_N * MSG
+    cols, rows, heats = [], [], []
+    for i in range(DEP_N):
+        nums = lanes_ref[i]
+        heat = jnp.concatenate([heat_ref[i, 0:1], heat_ref[i, 1:2]], axis=1)
+        cols.append(nums[0:1])
+        rows.append(nums[1:2])
+        heats.append(jnp.where(nums[3:4] > 0.5, 0.5 * heat, nil))
+    col = jnp.concatenate(cols, axis=1).astype(I32)
+    row = jnp.concatenate(rows, axis=1).astype(I32)
+    heat = jnp.concatenate(heats, axis=1)
+    high = heat.astype(BF16).astype(F32)
+    here = col == iota((128, width), 0)
+    spread = jnp.concatenate(
+        [jnp.where(here, high, nil).astype(BF16), jnp.where(here, heat - high, nil).astype(BF16)], axis=0
+    )
+    hot = jnp.where(row == iota((ROWS, width), 0), one, nil).astype(BF16)
+    acc[...] += dot_nt(hot, spread)
+
+    @pl.when(d == NT // DEP_N - 1)
     def _():
-        out_ref[...] = stepped_ref[...] + acc[:, :128] + acc[:, 128:]
-
-
-def deposit(lanes, heat, stepped):
+        layers = ROWS // 64
+        wall, lane = iota((64, 128), 0), iota((64, 128), 1)
+        left, right = left_ref[...], right_ref[...]
+        for x in range(layers):
+            at = 64 * x
+            h = cells_ref[at : at + 64]
+            x_lower = cells_ref[at - 64 : at] if x else below_ref[...]
+            x_upper = cells_ref[at + 64 : at + 128] if x < layers - 1 else above_ref[...]
+            w_lower = jnp.where(wall == 0, h, pltpu.roll(h, 1, 0))
+            w_upper = jnp.where(wall == 63, h, pltpu.roll(h, 63, 0))
+            s_lower = jnp.where(lane == 0, left[:, x : x + 1], pltpu.roll(h, 1, 1))
+            s_upper = jnp.where(lane == 127, right[:, x : x + 1], pltpu.roll(h, 127, 1))
+            laplace = (x_lower + x_upper) + (w_lower + w_upper) + (s_lower + s_upper) - 6.0 * h
+            new = h + dif_ref[at : at + 64] * laplace - vel_ref[at : at + 64] * (h - x_lower)
+            new = new + jnp.where(wall == 0, flux_ref[x : x + 1], nil)
+            out_ref[at : at + 64] = new + (acc[at : at + 64, :128] + acc[at : at + 64, 128:])
+
+
+def deposit(lanes, heat, cells, velocity, diffusivity, wall_flux, edges):
+    def whole(shape):
+        return pl.BlockSpec(shape, lambda d: (0, 0))
+
+    field = whole((ROWS, 128))
     return pl.pallas_call(
         deposit_kernel,
-        grid=(NT,),
+        grid=(NT // DEP_N,),
         out_shape=jax.ShapeDtypeStruct((ROWS, 128), F32),
         in_specs=[
-            pl.BlockSpec((1, 8, MSG), lambda d: (d, 0, 0)),
-            pl.BlockSpec((1, 8, HALF), lambda d: (d, 0, 0)),
-            pl.BlockSpec((ROWS, 128), lambda d: (0, 0)),
+            pl.BlockSpec((DEP_N, 8, MSG), lambda d: (d, 0, 0)),
+            pl.BlockSpec((DEP_N, 8, HALF), lambda d: (d, 0, 0)),
+            field,
+            field,
+            field,
+            whole((ROWS // 64, 128)),
+            whole((64, 128)),
+            whole((64, 128)),
+            whole((64, ROWS // 64)),
+            whole((64, ROWS // 64)),
         ],
-        out_specs=pl.BlockSpec((ROWS, 128), lambda d: (0, 0)),
+        out_specs=field,
         scratch_shapes=[pltpu.VMEM((ROWS, 256), F32)],
-        compiler_params=pltpu.CompilerParams(vmem_limit_bytes=24 * 2**20),
-        cost_estimate=pl.CostEstimate(flops=16384 * 1024 * 512, bytes_accessed=2 << 20, transcendentals=0),
+        compiler_params=pltpu.CompilerParams(vmem_limit_bytes=40 * 2**20),
+        cost_estimate=pl.CostEstimate(flops=10**10, bytes_accessed=4 << 20, transcendentals=0),
         name="deposit",
-    )(lanes, heat, stepped)
+    )(lanes, heat, cells, velocity, diffusivity, wall_flux, *edges)
 
 
 SETTLE = 1024
@@ -410,18 +500,11 @@
 
 def settle_kernel(amount_ref, slot_ref, rows_ref, fw_ref, weights_ref, out_ref, stage, comb):
     low_lanes = iota((HALF, 128), 1) < 64
-    row8 = iota((8, MSG), 0)
-    pick = jnp.where(iota((8, 128), 0) < 2, 1.0, 0.0).astype(BF16)
-    tn = (((0,), (0,)), ((), ()))
 
     @pl.loop(0, NT, unroll=4)
     def _(t):
         rows = rows_ref[t, 0:HALF]
-        side = rows_ref[t, HALF : HALF + 8]
-        far = jnp.concatenate([side[4 + q : 5 + q] for q in range(4)], axis=1)
-        rest = far - far.astype(BF16).astype(F32)
-        terms = jnp.where(row8 == 0, far, jnp.where(row8 == 1, rest, 0.0)).astype(BF16)
-        col = lax.dot_general(terms, pick, tn, preferred_element_type=F32)
+        col = far_columns(rows_ref[t, HALF:LOAD])
         at = pl.multiple_of(t * MSG, MSG)
         comb[pl.ds(at, HALF)] = jnp.where(low_lanes, rows, col[:HALF])
         comb[pl.ds(pl.multiple_of(at + HALF, HALF), HALF)] = jnp.where(
@@ -466,47 +549,43 @@
     )(amount, slots, rows, fw, weights)
 
 
-def halo(cells):
+def edges_of(cells):
     n_x, n_s = lax.axis_size("stream"), lax.axis_size("tile")
-    up_x = [(i, i + 1) for i in range(n_x - 1)]
-    down_x = [(i + 1, i) for i in range(n_x - 1)]
-    up_s = [(i, (i + 1) % n_s) for i in range(n_s)]
-    down_s = [((i + 1) % n_s, i) for i in range(n_s)]
-    before_x = lax.ppermute(cells[-1:], "stream", up_x)
-    after_x = lax.ppermute(cells[:1], "stream", down_x)
-    before_s = lax.ppermute(cells[:, :, -1], "tile", up_s)[:, :, None]
-    after_s = lax.ppermute(cells[:, :, 0], "tile", down_s)[:, :, None]
-    return (
-        jnp.concatenate([before_x, cells[:-1]], axis=0),
-        jnp.concatenate([cells[1:], after_x], axis=0),
-        jnp.concatenate([before_s, cells[..., :-1]], axis=2),
-        jnp.concatenate([cells[..., 1:], after_s], axis=2),
-    )
-
-
-def stencil(enthalpy, x_lower, x_upper, s_lower, s_upper, velocity, diffusivity, wall_flux):
-    wall_low = jnp.concatenate([enthalpy[:, :1], enthalpy[:, :-1]], axis=1)
-    wall_high = jnp.concatenate([enthalpy[:, 1:], enthalpy[:, -1:]], axis=1)
-    laplace = x_lower + x_upper + (wall_low + wall_high) + (s_lower + s_upper) - 6.0 * enthalpy
-    stepped = enthalpy + diffusivity * laplace - velocity * (enthalpy - x_lower)
-    at_wall = lax.broadcasted_iota(I32, stepped.shape, 1) == 0
-    return stepped + jnp.where(at_wall, wall_flux[:, None, :], 0.0)
+    x, s = lax.axis_index("stream"), lax.axis_index("tile")
+    ends_x = jnp.stack([cells[0], cells[-1]])
+    ends_s = jnp.stack([cells[:, :, 0].T, cells[:, :, -1].T])
+    all_x = lax.all_gather(ends_x, "stream")
+    all_s = lax.all_gather(ends_s.reshape(2, -1, 128), "tile")
+
+    def of(arrays, i, end):
+        return lax.dynamic_index_in_dim(arrays[:, end], i, 0, keepdims=False)
+
+    below = jnp.where(x > 0, of(all_x, lax.rem(x + n_x - 1, n_x), 1), 0.0)
+    above = jnp.where(x < n_x - 1, of(all_x, lax.rem(x + 1, n_x), 0), 0.0)
+    left = of(all_s, lax.rem(s + n_s - 1, n_s), 1).reshape(ends_s.shape[1:])
+    right = of(all_s, lax.rem(s + 1, n_s), 0).reshape(ends_s.shape[1:])
+    return below, above, left, right
 
 
 def on_device(
     enthalpy, velocity, diffusivity, wall_flux, profiles, counts, owners, cells,
     radial_step, far_weights, flux_weights,
 ):
+    table = enthalpy.reshape(ROWS, 128)
+    rows, meta, lanes = route(counts, owners, cells, profiles)
+    rows = far_gather(rows, meta, table)
+    rows, radial_step, far_weights, flux_weights = lax.optimization_barrier(
+        (rows, radial_step, far_weights, flux_weights)
+    )
     weights = step_weights(radial_step)
     fw = jnp.concatenate([far_weights, far_weights])[None, :]
     flux = flux_rows(flux_weights)
-    rows, meta, lanes = route(counts, owners, cells, profiles)
-    rows, add = far_gather(rows, meta, enthalpy.reshape(ROWS, 128), fw)
     got = lax.all_to_all(rows, "tile", split_axis=0, concat_axis=0, tiled=True)
-    heat = home_heat(rows, add, weights, flux)
-    edges, heat = lax.optimization_barrier((enthalpy, heat))
-    stepped = stencil(enthalpy, *halo(edges), velocity, diffusivity, wall_flux)
-    new_enthalpy = deposit(lanes, heat, stepped.reshape(ROWS, 128)).reshape(enthalpy.shape)
+    heat = home_heat(rows, fw, weights, flux)
+    new_enthalpy = deposit(
+        lanes, heat, table, velocity.reshape(ROWS, 128), diffusivity.reshape(ROWS, 128), wall_flux,
+        edges_of(enthalpy),
+    ).reshape(enthalpy.shape)
     slots = got[:, HALF : HALF + 4].reshape(NT, MSG).astype(I32)
     amount = jnp.sum((slots < OWN).astype(I32), axis=1)
     new_profiles = settle(amount, slots.reshape(-1), got, fw, weights)

time: 163 us -> 198 us (1.21); the launches traced: 162 us -> 195 us
  blocking collectives: 0 us -> 78.3 us
  local copies, waits for them, and re-layouts: 18.5 us -> 2.75 us
  starting transfers between devices: 27.8 us -> 14.2 us
  waiting for transfers between devices: 9.81 us -> 0.01 us
  Pallas kernels: 98.6 us -> 93.7 us
    all_gather x0 -> x2, blocking collectives: none -> 78.3 us  [the longest x1 68.1 us: edges_of(): all_s = lax.all_gather(ends_s.reshape(2, -1, 128), 'tile')]
    unnamed x19 -> x22, local copies, waits for them, and re-layouts: 11.3 us -> 0.99 us
    ppermute x4 -> x0, waiting for transfers between devices: 9.81 us -> none  [the longest x1 5.3 us: halo(): after_s = lax.ppermute(cells[:, :, 0], 'tile', down_s)[:, :, None]]
    ppermute x4 -> x0, starting transfers between devices: 7.22 us -> none  [the longest x1 3.81 us: halo(): before_x = lax.ppermute(cells[-1:], 'stream', up_x)]
    all_to_all x1, starting transfers between devices: 20.5 us -> 14.2 us  [on_device(): got = lax.all_to_all(rows, 'tile', split_axis=0, concat_axis=0, tiled=True)]
    pallas_call x2, Pallas kernels: 37 us -> 31.2 us  [the longest x1 19 us: far_gather(): pl.pallas_call(far_kernel, grid=(NT // FAR_N,), out_shape=jax.ShapeDtypeS...]
    slice x5 -> x4, local copies, waits for them, and re-layouts: 3.59 us -> 0.26 us  [the longest x1 0.21 us: edges_of(): ends_s = jnp.stack([cells[:, :, 0].T, cells[:, :, -1].T])]
    add x1 -> x0, other arithmetic: 2.46 us -> none  [stencil(): return stepped + jnp.where(at_wall, wall_flux[:, None, :], 0.0)]
  transfers between devices with their start and end apart: 5 -> 1, of which waited for: 2 -> 0; matrix products, arithmetic and copies ran while one was open for 5% -> 2% of each run, Pallas kernels for 27% -> 20%
where the time goes in v3:
time: 198 us; the launch traced here: 195 us
  Pallas kernels  93.7 us (47%)
  blocking collectives  78.3 us (40%)
  starting transfers between devices  14.2 us (7%)
  other arithmetic  4.52 us (2%)
  local copies, waits for them, and re-layouts  2.75 us (1%)
    all_gather x1, blocking collectives, edges_of(): all_s = lax.all_gather(ends_s.reshape(2, -1, 128), 'tile')  68.1 us
    pallas_call x1, Pallas kernels, home_heat(): pl.pallas_call(heat_kernel, grid=(NT // HEAT_N,), out_shape=jax.ShapeDtyp...  27.1 us
    pallas_call x1, Pallas kernels, settle(): pl.pallas_call(settle_kernel, out_shape=jax.ShapeDtypeStruct((PTS, OWN),...  20.2 us
    pallas_call x1, Pallas kernels, far_gather(): pl.pallas_call(far_kernel, grid=(NT // FAR_N,), out_shape=jax.ShapeDtypeS...  19 us
    pallas_call x1, Pallas kernels, route(): pl.pallas_call(route_kernel, out_shape=(jax.ShapeDtypeStruct((NT, LOAD, 1...  15.1 us
    all_to_all x1, starting transfers between devices, on_device(): got = lax.all_to_all(rows, 'tile', split_axis=0, concat_axis=0, tiled=True)  14.2 us
    pallas_call x1, Pallas kernels, deposit(): pl.pallas_call(deposit_kernel, grid=(NT // DEP_N,), out_shape=jax.ShapeDt...  12.3 us
    all_gather x1, blocking collectives, edges_of(): all_x = lax.all_gather(ends_x, 'stream')  10.2 us
  transfers between devices with their start and end apart: 1, of which 0 were waited for; matrix products, arithmetic and copies ran while one was open for 2% of the time, Pallas kernels for 20%

profile of v3, /device:TPU:35, one launch (start us, length us, event | category | flops | bytes accessed | tf_op | source)
XLA Modules:
  0.0 195.0 jit_solution(16657966634865594756)
XLA Ops:
  1.3 15.1 %route.1 = (f32[32,264,128]{2,1,0:T(8,128)}, bf16[32,256,128]{2,1,0:T(8,128)(2,1)}, f32[32,8,512]{2,1,0:T(8,128)}) custom-call(s32[1]{0:T(128)S(6)} %copy.30.count_ref, s32[128,128]{1,0:T(8,128)} %bitcast.40, s32[128,128]{1,0:T(8,128)} %bitcast.41, f32[64,16384]{1,0:T(8,128)} %prof_ref.1), custom_call_target="tpu_custom_call" | custom-call | tf_op jit(solution)/shard_map/route/pallas_call | solution.py:246
  16.4 19.0 %far_gather.1.rows_ref.side_ref = f32[32,264,128]{2,1,0:T(8,128)} custom-call(f32[32,264,128]{2,1,0:T(8,128)} %get-tuple-element.10.side_ref, bf16[32,256,128]{2,1,0:T(8,128)(2,1)} %get-tuple-element.11.meta_ref, f32[1024,128]{1,0:T(8,128)} %bitcast.31), custom_call_target="tpu_custom_call", output_to_operand_aliasing={{}: (0, {})} | custom-call | flops 10000000000 | bytes 8388608 | tf_op jit(solution)/shard_map/far_gather/pallas_call | solution.py:316
  35.4 14.2 %all-to-all-start = ((f32[32,264,128]{2,1,0:T(8,128)}), f32[32,264,128]{2,1,0:T(8,128)}, u32[]{:S(2)}, u32[]{:S(2)}) async-start(f32[32,264,128]{2,1,0:T(8,128)} %far_gather.1.rows_ref.side_ref), calls=%async_computation | async-start | bytes 8650752 | tf_op jit(solution)/shard_map/all_to_all | solution.py:583
  49.6 0.0 copy-start.9
  49.7 0.0 copy-start.10
  49.7 0.0 copy-done
  49.7 0.2 fusion.1
  49.9 0.5 copy.28
  50.4 0.1 stack.34
  50.5 0.5 copy.27
  50.9 0.1 stack.33
  51.0 68.1 %all_gather.11 = f32[32,2,8,128]{3,2,1,0:T(8,128)S(1)} all-gather(f32[1,2,8,128]{3,2,1,0:T(8,128)S(1)} %pad_maximum_fusion.1), channel_id=1, replica_groups=mesh['stream'=4,'tile'=32] {'tile'}, dimensions={0}, use_global_device_ids=true | all-gather | bytes 270336 | tf_op jit(solution)/shard_map/all_gather | solution.py:558
  119.2 0.0 copy-done.8
  119.3 0.1 copy.20
  119.3 0.1 pad.11.clone
  119.4 0.1 pad.10.clone
  119.5 0.1 reshape.57.left_ref
  119.6 0.1 reshape.58.right_ref
  119.7 10.2 %all-gather = f32[8,64,128]{2,1,0:T(8,128)S(1)} all-gather(f32[2,64,128]{2,1,0:T(8,128)S(1)} %pad_maximum_fusion), channel_id=2, replica_groups=mesh['stream'=4,'tile'=32] {'stream'}, dimensions={0}, use_global_device_ids=true | all-gather | bytes 327680 | tf_op jit(solution)/shard_map/all_gather | solution.py:557
  129.9 0.0 copy-done.10
  129.9 0.6 pad_bitcast_fusion.1
  130.5 0.1 reduce-precision_convert_fusion
  130.6 0.7 maximum_maximum_fusion.weights_ref
  131.3 0.6 maximum_multiply_fusion.flux_ref
  132.0 27.1 %home_heat.1.heat_ref = f32[32,8,256]{2,1,0:T(8,128)} custom-call(f32[32,264,128]{2,1,0:T(8,128)} %far_gather.1.rows_ref.side_ref, f32[32,264,128]{2,1,0:T(8,128)} %far_gather.1.rows_ref.side_ref, f32[1,128]{1,0:T(1,128)} %get-tuple-element.28.fw_ref, bf16[256,256]{1,0:T(8,128)(2,1)} %maximum_maximum_fusion.weights_ref, f32[8,128]{1,0:T(8,128)} %maximum_multiply_fusion.flux_ref), custom_call_target="tpu_custom_call" | custom-call | flops 20000000000 | bytes 8388608 | tf_op jit(solution)/shard_map/home_heat/pallas_call | solution.py:398
  159.1 0.0 copy-start.7
  159.1 0.9 copy-done.7
  160.1 12.3 %deposit.1 = f32[1024,128]{1,0:T(8,128)} custom-call(f32[32,8,512]{2,1,0:T(8,128)S(1)} %copy-done.5, f32[32,8,256]{2,1,0:T(8,128)S(1)} %copy-done.7, f32[1024,128]{1,0:T(8,128)S(1)} %bitcast.32, f32[1024,128]{1,0:T(8,128)S(1)} %bitcast.34, f32[1024,128]{1,0:T(8,128)S(1)} %bitcast.35, f32[16,128]{1,0:T(8,128)S(1)} %copy-done.6, ...), custom_call_target="tpu_custom_call" | custom-call | flops 10000000000 | bytes 4194304 | tf_op jit(solution)/shard_map/deposit/pallas_call | solution.py:474
  172.3 0.0 all-to-all-done.rows_ref
  172.3 1.6 convert_reduce_fusion.amount_ref
  173.9 0.9 slice_convert_fusion
  174.8 20.2 %settle.1 = f32[64,6144]{1,0:T(8,128)} custom-call(s32[32]{0:T(128)S(1)} %convert_reduce_fusion.amount_ref, s32[16384]{0:T(1024)S(1)} %bitcast.33, f32[32,264,128]{2,1,0:T(8,128)} %all-to-all-done.rows_ref, f32[1,128]{1,0:T(1,128)S(1)} %copy-done.2, bf16[256,256]{1,0:T(8,128)(2,1)S(1)} %copy-done.1), custom_call_target="tpu_custom_call" | custom-call | tf_op jit(solution)/shard_map/settle/pallas_call | solution.py:541
  (24 shorter events, 0.1 us)
Async XLA Ops:
  35.4 14.3 %copy-start = (f32[16,64,128]{2,1,0:T(8,128)S(1)}, f32[16,64,128]{2,1,0:T(8,128)}, u32[]{:S(2)}) copy-start(f32[16,64,128]{2,1,0:T(8,128)} %param.11) | copy-start | bytes 1572868
  35.4 83.9 %copy-start.8 = (f32[64,64]{1,0:T(8,128)S(1)}, f32[64,64]{1,0:T(8,128)}, u32[]{:S(2)}) copy-start(f32[64,64]{1,0:T(8,128)} %param.19) | copy-start | bytes 49156
  35.4 136.9 %all-to-all-start = ((f32[32,264,128]{2,1,0:T(8,128)}), f32[32,264,128]{2,1,0:T(8,128)}, u32[]{:S(2)}, u32[]{:S(2)}) async-start(f32[32,264,128]{2,1,0:T(8,128)} %far_gather.1.rows_ref.side_ref), calls=%async_computation | async-start | bytes 8650752 | tf_op jit(solution)/shard_map/all_to_all | solution.py:583
  49.6 80.2 %copy-start.9 = (f32[64]{0:T(128)S(1)}, f32[64]{0:T(128)}, u32[]{:S(2)}) copy-start(f32[64]{0:T(128)} %param.21) | copy-start | bytes 772
  49.7 80.2 %copy-start.10 = (f32[64]{0:T(128)S(1)}, f32[64]{0:T(128)}, u32[]{:S(2)}) copy-start(f32[64]{0:T(128)} %param.20) | copy-start | bytes 772
  131.9 27.2 %copy-start.3 = (f32[16,64,128]{2,1,0:T(8,128)S(1)}, f32[16,64,128]{2,1,0:T(8,128)}, u32[]{:S(2)}) copy-start(f32[16,64,128]{2,1,0:T(8,128)} %param.12) | copy-start | bytes 1572868
  131.9 27.2 %copy-start.4 = (f32[16,64,128]{2,1,0:T(8,128)S(1)}, f32[16,64,128]{2,1,0:T(8,128)}, u32[]{:S(2)}) copy-start(f32[16,64,128]{2,1,0:T(8,128)} %param.13) | copy-start | bytes 1572868
  131.9 27.2 %copy-start.5 = (f32[32,8,512]{2,1,0:T(8,128)S(1)}, f32[32,8,512]{2,1,0:T(8,128)}, u32[]{:S(2)}) copy-start(f32[32,8,512]{2,1,0:T(8,128)} %get-tuple-element.9.lanes_ref) | copy-start | bytes 1572868
  131.9 27.2 %copy-start.6 = (f32[16,128]{1,0:T(8,128)S(1)}, f32[16,128]{1,0:T(8,128)}, u32[]{:S(2)}) copy-start(f32[16,128]{1,0:T(8,128)} %flux_ref.1) | copy-start | bytes 24580
  159.1 1.0 copy-start.7
  160.1 14.8 %copy-start.1 = (bf16[256,256]{1,0:T(8,128)(2,1)S(1)}, bf16[256,256]{1,0:T(8,128)(2,1)}, u32[]{:S(2)}) copy-start(bf16[256,256]{1,0:T(8,128)(2,1)} %maximum_maximum_fusion.weights_ref) | copy-start | bytes 393220
  160.1 14.8 %copy-start.2 = (f32[1,128]{1,0:T(1,128)S(1)}, f32[1,128]{1,0:T(1,128)}, u32[]{:S(2)}) copy-start(f32[1,128]{1,0:T(1,128)} %get-tuple-element.28.fw_ref) | copy-start | bytes 1540

commit v4 on v3

--- a/solution.py
+++ b/solution.py
@@ -551,20 +551,15 @@
 
 def edges_of(cells):
     n_x, n_s = lax.axis_size("stream"), lax.axis_size("tile")
-    x, s = lax.axis_index("stream"), lax.axis_index("tile")
-    ends_x = jnp.stack([cells[0], cells[-1]])
-    ends_s = jnp.stack([cells[:, :, 0].T, cells[:, :, -1].T])
-    all_x = lax.all_gather(ends_x, "stream")
-    all_s = lax.all_gather(ends_s.reshape(2, -1, 128), "tile")
-
-    def of(arrays, i, end):
-        return lax.dynamic_index_in_dim(arrays[:, end], i, 0, keepdims=False)
-
-    below = jnp.where(x > 0, of(all_x, lax.rem(x + n_x - 1, n_x), 1), 0.0)
-    above = jnp.where(x < n_x - 1, of(all_x, lax.rem(x + 1, n_x), 0), 0.0)
-    left = of(all_s, lax.rem(s + n_s - 1, n_s), 1).reshape(ends_s.shape[1:])
-    right = of(all_s, lax.rem(s + 1, n_s), 0).reshape(ends_s.shape[1:])
-    return below, above, left, right
+    up_x = [(i, i + 1) for i in range(n_x - 1)]
+    down_x = [(i + 1, i) for i in range(n_x - 1)]
+    up_s = [(i, (i + 1) % n_s) for i in range(n_s)]
+    down_s = [((i + 1) % n_s, i) for i in range(n_s)]
+    below = lax.ppermute(cells[-1], "stream", up_x)
+    above = lax.ppermute(cells[0], "stream", down_x)
+    left = lax.ppermute(cells[:, :, -1], "tile", up_s)
+    right = lax.ppermute(cells[:, :, 0], "tile", down_s)
+    return below, above, left.T, right.T
 
 
 def on_device(
@@ -582,9 +577,10 @@
     flux = flux_rows(flux_weights)
     got = lax.all_to_all(rows, "tile", split_axis=0, concat_axis=0, tiled=True)
     heat = home_heat(rows, fw, weights, flux)
+    ends, heat = lax.optimization_barrier((enthalpy, heat))
     new_enthalpy = deposit(
         lanes, heat, table, velocity.reshape(ROWS, 128), diffusivity.reshape(ROWS, 128), wall_flux,
-        edges_of(enthalpy),
+        edges_of(ends),
     ).reshape(enthalpy.shape)
     slots = got[:, HALF : HALF + 4].reshape(NT, MSG).astype(I32)
     amount = jnp.sum((slots < OWN).astype(I32), axis=1)

time: 198 us -> 138 us (0.70); the launches traced: 195 us -> 138 us
  blocking collectives: 78.3 us -> 0 us
  waiting for transfers between devices: 0.01 us -> 10.5 us
  starting transfers between devices: 14.2 us -> 21.4 us
  local copies, waits for them, and re-layouts: 2.75 us -> 5.5 us
    all_gather x2 -> x0, blocking collectives: 78.3 us -> none  [the longest x1 68.1 us: edges_of(): all_s = lax.all_gather(ends_s.reshape(2, -1, 128), 'tile')]
    ppermute x0 -> x4, waiting for transfers between devices: none -> 10.4 us  [the longest x1 5.28 us: edges_of(): right = lax.ppermute(cells[:, :, 0], 'tile', down_s)]
    ppermute x0 -> x4, starting transfers between devices: none -> 7.58 us  [the longest x1 3.5 us: edges_of(): below = lax.ppermute(cells[-1], 'stream', up_x)]
    optimization_barrier x0 -> x1, local copies, waits for them, and re-layouts: none -> 4.43 us  [on_device(): ends, heat = lax.optimization_barrier((enthalpy, heat))]
  transfers between devices with their start and end apart: 1 -> 5, of which waited for: 0 -> 2; matrix products, arithmetic and copies ran while one was open for 2% -> 5% of each run, Pallas kernels for 20% -> 29%
where the time goes in v4:
time: 138 us
  Pallas kernels  94.7 us (69%)
  starting transfers between devices  21.4 us (16%)
  waiting for transfers between devices  10.5 us (8%)
  local copies, waits for them, and re-layouts  5.5 us (4%)
  other arithmetic  4.51 us (3%)
  between operations  1.46 us (1%)
    pallas_call x1, Pallas kernels, home_heat(): pl.pallas_call(heat_kernel, grid=(NT // HEAT_N,), out_shape=jax.ShapeDtyp...  27.1 us
    pallas_call x1, Pallas kernels, settle(): pl.pallas_call(settle_kernel, out_shape=jax.ShapeDtypeStruct((PTS, OWN),...  20.7 us
    pallas_call x1, Pallas kernels, far_gather(): pl.pallas_call(far_kernel, grid=(NT // FAR_N,), out_shape=jax.ShapeDtypeS...  19 us
    pallas_call x1, Pallas kernels, route(): pl.pallas_call(route_kernel, out_shape=(jax.ShapeDtypeStruct((NT, LOAD, 1...  15.8 us
    all_to_all x1, starting transfers between devices, on_device(): got = lax.all_to_all(rows, 'tile', split_axis=0, concat_axis=0, tiled=True)  13.8 us
    pallas_call x1, Pallas kernels, deposit(): pl.pallas_call(deposit_kernel, grid=(NT // DEP_N,), out_shape=jax.ShapeDt...  12.3 us
    ppermute x1, waiting for transfers between devices, edges_of(): right = lax.ppermute(cells[:, :, 0], 'tile', down_s)  5.28 us
    ppermute x1, waiting for transfers between devices, edges_of(): left = lax.ppermute(cells[:, :, -1], 'tile', up_s)  5.16 us
  transfers between devices with their start and end apart: 5, of which 2 were waited for; matrix products, arithmetic and copies ran while one was open for 5% of the time, Pallas kernels for 29%

profile of v4, /device:TPU:35, one launch (start us, length us, event | category | flops | bytes accessed | tf_op | source)
XLA Modules:
  0.0 138.0 jit_solution(14589139193707589248)
XLA Ops:
  1.3 15.8 %route.1 = (f32[32,264,128]{2,1,0:T(8,128)}, bf16[32,256,128]{2,1,0:T(8,128)(2,1)}, f32[32,8,512]{2,1,0:T(8,128)}) custom-call(s32[1]{0:T(128)S(6)} %copy.18.count_ref, s32[128,128]{1,0:T(8,128)} %bitcast.32, s32[128,128]{1,0:T(8,128)} %bitcast.33, f32[64,16384]{1,0:T(8,128)} %prof_ref.1), custom_call_target="tpu_custom_call" | custom-call | tf_op jit(solution)/shard_map/route/pallas_call | solution.py:246
  17.0 19.0 %far_gather.1.rows_ref.side_ref = f32[32,264,128]{2,1,0:T(8,128)} custom-call(f32[32,264,128]{2,1,0:T(8,128)} %get-tuple-element.12.side_ref, bf16[32,256,128]{2,1,0:T(8,128)(2,1)} %get-tuple-element.13.meta_ref, f32[1024,128]{1,0:T(8,128)} %bitcast.24), custom_call_target="tpu_custom_call", output_to_operand_aliasing={{}: (0, {})} | custom-call | flops 10000000000 | bytes 8388608 | tf_op jit(solution)/shard_map/far_gather/pallas_call | solution.py:316
  36.0 13.8 %all-to-all-start = ((f32[32,264,128]{2,1,0:T(8,128)}), f32[32,264,128]{2,1,0:T(8,128)}, u32[]{:S(2)}, u32[]{:S(2)}) async-start(f32[32,264,128]{2,1,0:T(8,128)} %far_gather.1.rows_ref.side_ref), calls=%async_computation | async-start | bytes 8650752 | tf_op jit(solution)/shard_map/all_to_all | solution.py:578
  49.8 0.0 copy-done.8
  49.9 0.1 copy.14
  49.9 0.1 pad.7.clone
  50.0 0.1 pad.6.clone
  50.1 0.0 copy-done.9
  50.1 0.6 pad_bitcast_fusion.1
  50.7 0.1 reduce-precision_convert_fusion
  50.8 0.7 maximum_maximum_fusion.weights_ref
  51.5 0.7 maximum_multiply_fusion.flux_ref
  52.1 27.1 %home_heat.1.heat_ref = f32[32,8,256]{2,1,0:T(8,128)} custom-call(f32[32,264,128]{2,1,0:T(8,128)} %far_gather.1.rows_ref.side_ref, f32[32,264,128]{2,1,0:T(8,128)} %far_gather.1.rows_ref.side_ref, f32[1,128]{1,0:T(1,128)} %get-tuple-element.28.fw_ref, bf16[256,256]{1,0:T(8,128)(2,1)} %maximum_maximum_fusion.weights_ref, f32[8,128]{1,0:T(8,128)} %maximum_multiply_fusion.flux_ref), custom_call_target="tpu_custom_call" | custom-call | flops 20000000000 | bytes 8388608 | tf_op jit(solution)/shard_map/home_heat/pallas_call | solution.py:398
  79.2 0.0 copy-start.4
  79.2 0.0 copy-start.5
  79.2 0.0 copy-start.6
  79.2 0.0 copy-start.7
  79.3 3.5 %collective-permute-start = (f32[64,128]{1,0:T(8,128)S(1)}, f32[64,128]{1,0:T(8,128)S(1)}, u32[]{:S(2)}, u32[]{:S(2)}) collective-permute-start(f32[64,128]{1,0:T(8,128)S(1)} %get-tuple-element.23), channel_id=1, source_target_pairs={{0,32},{32,64},{64,96},{1,33},{33,65},{65,97},{2,34},{34,66},{66,9... | collective-permute-start | bytes 98312 | tf_op jit(solution)/shard_map/ppermute | solution.py:558
  82.8 2.1 %collective-permute-start.1 = (f32[64,128]{1,0:T(8,128)S(1)}, f32[64,128]{1,0:T(8,128)S(1)}, u32[]{:S(2)}, u32[]{:S(2)}) collective-permute-start(f32[64,128]{1,0:T(8,128)S(1)} %get-tuple-element.22), channel_id=1, source_target_pairs={{32,0},{64,32},{96,64},{33,1},{65,33},{97,65},{34,2},{66,34},{98,6... | collective-permute-start | bytes 98312 | tf_op jit(solution)/shard_map/ppermute | solution.py:559
  84.9 4.4 %copy.15 = f32[16,64,128]{0,1,2:T(8,128)} copy(f32[16,64,128]{2,1,0:T(8,128)S(1)} %copy-done) | data formatting | bytes 1048576 | tf_op jit(solution)/shard_map/optimization_barrier | solution.py:580
  89.3 0.8 slice_bitcast_fusion
  90.1 2.0 %collective-permute-start.2 = (f32[16,64]{0,1:T(8,128)S(1)}, f32[16,64]{0,1:T(8,128)S(1)}, u32[]{:S(2)}, u32[]{:S(2)}) collective-permute-start(f32[16,64]{0,1:T(8,128)S(1)} %get-tuple-element.21), channel_id=1, source_target_pairs={{0,1},{1,2},{2,3},{3,4},{4,5},{5,6},{6,7},{7,8},{8,9},{9,10},{10,1... | collective-permute-start | bytes 12296 | tf_op jit(solution)/shard_map/ppermute | solution.py:560
  92.1 0.0 collective-permute-start.3
  92.1 5.2 %collective-permute-done.2 = f32[16,64]{0,1:T(8,128)S(1)} collective-permute-done((f32[16,64]{0,1:T(8,128)S(1)}, f32[16,64]{0,1:T(8,128)S(1)}, u32[]{:S(2)}, u32[]{:S(2)}) %collective-permute-start.2) | collective-permute-done | bytes 4128 | tf_op jit(solution)/shard_map/ppermute | solution.py:560
  97.2 5.3 %collective-permute-done.3 = f32[16,64]{0,1:T(8,128)S(1)} collective-permute-done((f32[16,64]{0,1:T(8,128)S(1)}, f32[16,64]{0,1:T(8,128)S(1)}, u32[]{:S(2)}, u32[]{:S(2)}) %collective-permute-start.3) | collective-permute-done | bytes 4128 | tf_op jit(solution)/shard_map/ppermute | solution.py:561
  102.5 0.0 collective-permute-done.below_ref
  102.5 0.0 collective-permute-done.1.above_ref
  102.6 12.3 %deposit.1 = f32[1024,128]{1,0:T(8,128)} custom-call(f32[32,8,512]{2,1,0:T(8,128)S(1)} %copy-done.5, f32[32,8,256]{2,1,0:T(8,128)S(1)} %copy-done.7, f32[1024,128]{1,0:T(8,128)S(1)} %bitcast.25, f32[1024,128]{1,0:T(8,128)S(1)} %bitcast.27, f32[1024,128]{1,0:T(8,128)S(1)} %bitcast.28, f32[16,128]{1,0:T(8,128)S(1)} %copy-done.6, ...), custom_call_target="tpu_custom_call" | custom-call | flops 10000000000 | bytes 4194304 | tf_op jit(solution)/shard_map/deposit/pallas_call | solution.py:474
  114.9 0.0 all-to-all-done.rows_ref
  114.9 1.6 %convert_reduce_fusion.amount_ref = s32[32]{0:T(128)S(1)} fusion(f32[32,264,128]{2,1,0:T(8,128)} %all-to-all-done.rows_ref), kind=kLoop, calls=%fused_computation.8 | loop fusion | flops 65504 | bytes 65664 | tf_op jit(solution)/shard_map/reduce_sum | solution.py:586
  116.4 0.9 slice_convert_fusion
  117.4 20.7 %settle.1 = f32[64,6144]{1,0:T(8,128)} custom-call(s32[32]{0:T(128)S(1)} %convert_reduce_fusion.amount_ref, s32[16384]{0:T(1024)S(1)} %bitcast.26, f32[32,264,128]{2,1,0:T(8,128)} %all-to-all-done.rows_ref, f32[1,128]{1,0:T(1,128)S(1)} %copy-done.2, bf16[256,256]{1,0:T(8,128)(2,1)S(1)} %copy-done.1), custom_call_target="tpu_custom_call" | custom-call | tf_op jit(solution)/shard_map/settle/pallas_call | solution.py:541
  (19 shorter events, 0.0 us)
Async XLA Ops:
  36.0 13.8 %copy-start.8 = (f32[64,64]{1,0:T(8,128)S(1)}, f32[64,64]{1,0:T(8,128)}, u32[]{:S(2)}) copy-start(f32[64,64]{1,0:T(8,128)} %param.19) | copy-start | bytes 49156
  36.0 14.1 %copy-start.9 = (f32[64]{0:T(128)S(1)}, f32[64]{0:T(128)}, u32[]{:S(2)}) copy-start(f32[64]{0:T(128)} %param.21) | copy-start | bytes 772
  36.0 14.1 %copy-start.10 = (f32[64]{0:T(128)S(1)}, f32[64]{0:T(128)}, u32[]{:S(2)}) copy-start(f32[64]{0:T(128)} %param.20) | copy-start | bytes 772
  36.0 78.8 %all-to-all-start = ((f32[32,264,128]{2,1,0:T(8,128)}), f32[32,264,128]{2,1,0:T(8,128)}, u32[]{:S(2)}, u32[]{:S(2)}) async-start(f32[32,264,128]{2,1,0:T(8,128)} %far_gather.1.rows_ref.side_ref), calls=%async_computation | async-start | bytes 8650752 | tf_op jit(solution)/shard_map/all_to_all | solution.py:578
  52.1 27.1 %copy-start = (f32[16,64,128]{2,1,0:T(8,128)S(1)}, f32[16,64,128]{2,1,0:T(8,128)}, u32[]{:S(2)}) copy-start(f32[16,64,128]{2,1,0:T(8,128)} %param.11) | copy-start | bytes 1572868
  79.2 23.3 %copy-start.3 = (f32[16,64,128]{2,1,0:T(8,128)S(1)}, f32[16,64,128]{2,1,0:T(8,128)}, u32[]{:S(2)}) copy-start(f32[16,64,128]{2,1,0:T(8,128)} %param.12) | copy-start | bytes 1572868
  79.2 23.3 %copy-start.4 = (f32[16,64,128]{2,1,0:T(8,128)S(1)}, f32[16,64,128]{2,1,0:T(8,128)}, u32[]{:S(2)}) copy-start(f32[16,64,128]{2,1,0:T(8,128)} %param.13) | copy-start | bytes 1572868
  79.2 23.3 %copy-start.5 = (f32[32,8,512]{2,1,0:T(8,128)S(1)}, f32[32,8,512]{2,1,0:T(8,128)}, u32[]{:S(2)}) copy-start(f32[32,8,512]{2,1,0:T(8,128)} %get-tuple-element.11.lanes_ref) | copy-start | bytes 1572868
  79.2 23.3 %copy-start.6 = (f32[16,128]{1,0:T(8,128)S(1)}, f32[16,128]{1,0:T(8,128)}, u32[]{:S(2)}) copy-start(f32[16,128]{1,0:T(8,128)} %flux_ref.1) | copy-start | bytes 24580
  79.2 23.3 %copy-start.7 = (f32[32,8,256]{2,1,0:T(8,128)S(1)}, f32[32,8,256]{2,1,0:T(8,128)}, u32[]{:S(2)}) copy-start(f32[32,8,256]{2,1,0:T(8,128)} %home_heat.1.heat_ref) | copy-start | bytes 786436
  79.3 23.3 %collective-permute-start = (f32[64,128]{1,0:T(8,128)S(1)}, f32[64,128]{1,0:T(8,128)S(1)}, u32[]{:S(2)}, u32[]{:S(2)}) collective-permute-start(f32[64,128]{1,0:T(8,128)S(1)} %get-tuple-element.23), channel_id=1, source_target_pairs={{0,32},{32,64},{64,96},{1,33},{33,65},{65,97},{2,34},{34,66},{66,9... | collective-permute-start | bytes 98312 | tf_op jit(solution)/shard_map/ppermute | solution.py:558
  82.8 19.7 %collective-permute-start.1 = (f32[64,128]{1,0:T(8,128)S(1)}, f32[64,128]{1,0:T(8,128)S(1)}, u32[]{:S(2)}, u32[]{:S(2)}) collective-permute-start(f32[64,128]{1,0:T(8,128)S(1)} %get-tuple-element.22), channel_id=1, source_target_pairs={{32,0},{64,32},{96,64},{33,1},{65,33},{97,65},{34,2},{66,34},{98,6... | collective-permute-start | bytes 98312 | tf_op jit(solution)/shard_map/ppermute | solution.py:559
  90.1 7.1 %collective-permute-start.2 = (f32[16,64]{0,1:T(8,128)S(1)}, f32[16,64]{0,1:T(8,128)S(1)}, u32[]{:S(2)}, u32[]{:S(2)}) collective-permute-start(f32[16,64]{0,1:T(8,128)S(1)} %get-tuple-element.21), channel_id=1, source_target_pairs={{0,1},{1,2},{2,3},{3,4},{4,5},{5,6},{6,7},{7,8},{8,9},{9,10},{10,1... | collective-permute-start | bytes 12296 | tf_op jit(solution)/shard_map/ppermute | solution.py:560
  92.1 10.4 %collective-permute-start.3 = (f32[16,64]{0,1:T(8,128)S(1)}, f32[16,64]{0,1:T(8,128)S(1)}, u32[]{:S(2)}, u32[]{:S(2)}) collective-permute-start(f32[16,64]{0,1:T(8,128)S(1)} %get-tuple-element.20), channel_id=1, source_target_pairs={{1,0},{2,1},{3,2},{4,3},{5,4},{6,5},{7,6},{8,7},{9,8},{10,9},{11,1... | collective-permute-start | bytes 12296 | tf_op jit(solution)/shard_map/ppermute | solution.py:561
  102.6 14.8 %copy-start.1 = (bf16[256,256]{1,0:T(8,128)(2,1)S(1)}, bf16[256,256]{1,0:T(8,128)(2,1)}, u32[]{:S(2)}) copy-start(bf16[256,256]{1,0:T(8,128)(2,1)} %maximum_maximum_fusion.weights_ref) | copy-start | bytes 393220
  102.6 14.8 %copy-start.2 = (f32[1,128]{1,0:T(1,128)S(1)}, f32[1,128]{1,0:T(1,128)}, u32[]{:S(2)}) copy-start(f32[1,128]{1,0:T(1,128)} %get-tuple-element.28.fw_ref) | copy-start | bytes 1540

commit v5 on v4

--- a/solution.py
+++ b/solution.py
@@ -19,6 +19,7 @@
 ROWS = 1024
 OWN2 = OWN // 2
 
+GROUP = 4
 ROOM = 60 * 2**20
 
 F32, BF16, I32 = jnp.float32, jnp.bfloat16, jnp.int32
@@ -43,10 +44,10 @@
 
 
 def route_kernel(
-    count_ref, owners_ref, cells_ref, prof_ref,
-    rows_ref, meta_ref, lanes_ref,
+    count_ref, owners_ref, cells_ref, field_ref, prof_ref,
+    rows_ref, lanes_ref, ends_ref,
     pos_s, m0_s, m1_s, m2_s, m3_s, m4_s, sorted_a, sorted_b, sorted_c, sorted_d,
-    bucket, tab_v, tab_s, sem, prof_v, prof_sem, pack_v, pack_sem,
+    bucket, tab_v, tab_s, sem, prof_v, prof_sem, pack_v, pack_sem, meta_v, table,
 ):
     count = count_ref[0]
     fetch = pltpu.make_async_copy(prof_ref, prof_v, prof_sem)
@@ -212,18 +213,17 @@
     lane_dest = iota((8, BLK), 1)
 
     def send(g):
-        part = pl.ds(g * 4, 4)
+        part = pl.ds(g * GROUP, GROUP)
         return pltpu.make_async_copy(pack_v.at[part], rows_ref.at[part], pack_sem.at[g])
 
-    @pl.loop(0, NT // 4)
-    def _(g):
-        for k in range(4):
-            d = 4 * g + k
+    def pack(g):
+        for k in range(GROUP):
+            d = GROUP * g + k
             at = pl.multiple_of(d * STRIDE, 8)
             lo = bucket[pl.ds(at, HALF)]
             hi = bucket[pl.ds(pl.multiple_of(at + HALF, 8), HALF)]
             pack_v[d, 0:HALF] = jnp.where(low_lanes, lo, pltpu.roll(hi, 64, 1))
-            meta_ref[d] = jnp.where(low_lanes, pltpu.roll(lo, 64, 1), hi).astype(BF16)
+            meta_v[d] = jnp.where(low_lanes, pltpu.roll(lo, 64, 1), hi).astype(BF16)
             both = jnp.concatenate([lo, hi], axis=0).astype(BF16)
             nums = dot_nt(pick, both)
             mine = jnp.max(jnp.where(lane_dest == d, total, nil), axis=1, keepdims=True)
@@ -231,27 +231,73 @@
             nums = jnp.where((rank_row == 2) & ~valid, float(OWN), nums)
             nums = jnp.where(rank_row == 3, jnp.where(valid, one, nil), nums)
             lanes_ref[d] = nums
-            pack_v[d, HALF:LOAD] = jnp.concatenate(
-                [nums[2:3, 128 * q : 128 * q + 128] for q in range(4)] + [jnp.zeros((4, 128), F32)],
-                axis=0,
+            pack_v[d, HALF : HALF + 4] = jnp.concatenate(
+                [nums[2:3, 128 * q : 128 * q + 128] for q in range(4)], axis=0
             )
+
+    cells = field_ref[...].reshape(ROWS // 4, 4, 128)
+    parts = [split(cells[:, q]) for q in range(4)]
+    table[...] = jnp.concatenate([p[0] for p in parts] + [p[1] for p in parts], axis=1)
+    m_rows = GROUP * HALF
+    ones8 = jnp.ones((8, 256), BF16)
+    sub128 = iota((128, 128), 0)
+    place = iota((m_rows, 128), 1).astype(F32)
+
+    def far(g):
+        meta = meta_v[pl.ds(g * GROUP, GROUP)].reshape(m_rows, 128)
+        for h in range(2):
+            first = 0 if h == 0 else 64
+            col = jnp.where(sub128 == first, one, nil) + jnp.where(sub128 == first + 1, 128.0 * one, nil)
+            row = jnp.where(sub128 == first + 2, one, nil)
+            got = dot(meta, jnp.concatenate([col, row], axis=1).astype(BF16))
+            col, row = got[:, :128], got[:, 128:]
+            hot = jnp.concatenate(
+                [jnp.where(row == place + 128.0 * q, one, nil).astype(BF16) for q in range(2)], axis=1
+            )
+            val = dot(hot, table[...])
+            got = jnp.zeros((m_rows, 128), F32)
+            for q in range(4):
+                both = val[:, 128 * q : 128 * q + 128] + val[:, 512 + 128 * q : 640 + 128 * q]
+                got = jnp.where(col == place + 128.0 * q, both, got)
+            v0, v1 = split(got)
+            far_l = dot_nt(ones8, jnp.concatenate([v0, v1], axis=1))
+            for i in range(GROUP):
+                for q in range(2):
+                    at = HALF * i + 128 * q
+                    row_at = HALF + 4 + 2 * h + q
+                    pack_v[GROUP * g + i, row_at : row_at + 1] = far_l[0:1, at : at + 128]
+
+    pack(0)
+
+    @pl.loop(0, NT // GROUP - 1)
+    def _(g):
+        far(g)
+        pack(g + 1)
         send(g).start()
 
-    for g in range(NT // 4):
+    far(NT // GROUP - 1)
+    send(NT // GROUP - 1).start()
+    pick = jnp.where((r8 == 0) & (l8 == 0), one, nil) + jnp.where((r8 == 1) & (l8 == 127), one, nil)
+    pick = pick.astype(BF16)
+    f0, f1 = split(field_ref[...])
+    f2 = (field_ref[...] - f0.astype(F32) - f1.astype(F32)).astype(BF16)
+    ends_ref[...] = dot_nt(pick, f0) + dot_nt(pick, f1) + dot_nt(pick, f2)
+    for g in range(NT // GROUP):
         send(g).wait()
 
 
-def route(counts, owners, cells, profiles):
+def route(counts, owners, cells, field, profiles):
     vmem = pl.BlockSpec(memory_space=pltpu.VMEM)
+    anywhere = pl.BlockSpec(memory_space=pl.ANY)
     return pl.pallas_call(
         route_kernel,
         out_shape=(
             jax.ShapeDtypeStruct((NT, LOAD, 128), F32),
-            jax.ShapeDtypeStruct((NT, HALF, 128), BF16),
             jax.ShapeDtypeStruct((NT, 8, MSG), F32),
+            jax.ShapeDtypeStruct((8, ROWS), F32),
         ),
-        in_specs=[pl.BlockSpec(memory_space=pltpu.SMEM), vmem, vmem, pl.BlockSpec(memory_space=pl.ANY)],
-        out_specs=(pl.BlockSpec(memory_space=pl.ANY), vmem, vmem),
+        in_specs=[pl.BlockSpec(memory_space=pltpu.SMEM), vmem, vmem, vmem, anywhere],
+        out_specs=(anywhere, vmem, vmem),
         scratch_shapes=[pltpu.VMEM((NBLK, BLK), F32)] * 6
         + [pltpu.VMEM((BLK + 16, 128), F32)] * 4
         + [
@@ -262,73 +308,13 @@
             pltpu.VMEM((PTS, CAP), F32),
             pltpu.SemaphoreType.DMA,
             pltpu.VMEM((NT, LOAD, 128), F32),
-            pltpu.SemaphoreType.DMA((NT // 4,)),
+            pltpu.SemaphoreType.DMA((NT // GROUP,)),
+            pltpu.VMEM((NT, HALF, 128), BF16),
+            pltpu.VMEM((ROWS // 4, 1024), BF16),
         ],
         compiler_params=pltpu.CompilerParams(vmem_limit_bytes=ROOM),
         name="route",
-    )(counts, owners.reshape(128, 128), cells.reshape(128, 128), profiles)
-
-
-FAR_N = 4
-
-
-def far_kernel(side_ref, meta_ref, cells_ref, out_ref, table):
-    one, nil = jnp.ones((), F32), jnp.zeros((), F32)
-    m_rows = FAR_N * HALF
-
-    @pl.when(pl.program_id(0) == 0)
-    def _():
-        cells = cells_ref[...].reshape(ROWS // 4, 4, 128)
-        parts = [split(cells[:, q]) for q in range(4)]
-        table[...] = jnp.concatenate([p[0] for p in parts] + [p[1] for p in parts], axis=1)
-
-    sub = iota((128, 128), 0)
-    ones8 = jnp.ones((8, 256), BF16)
-    place = iota((m_rows, 128), 1).astype(F32)
-    meta = meta_ref[...].reshape(m_rows, 128)
-    for i in range(FAR_N):
-        out_ref[i, 0:4] = side_ref[i, 0:4]
-    for h in range(2):
-        first = 0 if h == 0 else 64
-        col = jnp.where(sub == first, one, nil) + jnp.where(sub == first + 1, 128.0 * one, nil)
-        row = jnp.where(sub == first + 2, one, nil)
-        got = dot(meta, jnp.concatenate([col, row], axis=1).astype(BF16))
-        col, row = got[:, :128], got[:, 128:]
-        hot = jnp.concatenate(
-            [jnp.where(row == place + 128.0 * q, one, nil).astype(BF16) for q in range(2)], axis=1
-        )
-        val = dot(hot, table[...])
-        got = jnp.zeros((m_rows, 128), F32)
-        for q in range(4):
-            both = val[:, 128 * q : 128 * q + 128] + val[:, 512 + 128 * q : 640 + 128 * q]
-            got = jnp.where(col == place + 128.0 * q, both, got)
-        v0, v1 = split(got)
-        v = jnp.concatenate([v0, v1], axis=1)
-        far = dot_nt(ones8, v)
-        for i in range(FAR_N):
-            for q in range(2):
-                at = 256 * i + 128 * q
-                out_ref[i, 4 + 2 * h + q : 5 + 2 * h + q] = far[0:1, at : at + 128]
-
-
-def far_gather(rows, meta, table):
-    side = pl.BlockSpec((FAR_N, 8, 128), lambda d: (d, HALF // 8, 0))
-    return pl.pallas_call(
-        far_kernel,
-        grid=(NT // FAR_N,),
-        out_shape=jax.ShapeDtypeStruct((NT, LOAD, 128), F32),
-        in_specs=[
-            side,
-            pl.BlockSpec((FAR_N, HALF, 128), lambda d: (d, 0, 0)),
-            pl.BlockSpec((ROWS, 128), lambda d: (0, 0)),
-        ],
-        out_specs=side,
-        scratch_shapes=[pltpu.VMEM((256, 1024), BF16)],
-        input_output_aliases={0: 0},
-        compiler_params=pltpu.CompilerParams(vmem_limit_bytes=ROOM),
-        cost_estimate=pl.CostEstimate(flops=10**10, bytes_accessed=8 << 20, transcendentals=0),
-        name="far_gather",
-    )(rows, meta, table)
+    )(counts, owners.reshape(128, 128), cells.reshape(128, 128), field, profiles)
 
 
 def step_weights(radial_step):
@@ -361,7 +347,7 @@
     return (got[:, :128] + got[:, 128:]) + (add + 0.25 * jnp.tanh(state))
 
 
-HEAT_N = 4
+HEAT_N = GROUP
 
 
 def far_columns(side):
@@ -393,31 +379,44 @@
         heat_ref[i] = heat[:, HALF * i : HALF * i + HALF]
 
 
-def home_heat(rows, fw, weights, flux):
-    block = pl.BlockSpec((HEAT_N, HALF, 128), lambda d: (d, 0, 0))
+def home_heat(rows, fw, weights, flux, first, steps):
     return pl.pallas_call(
         heat_kernel,
-        grid=(NT // HEAT_N,),
-        out_shape=jax.ShapeDtypeStruct((NT, 8, HALF), F32),
+        grid=(steps,),
+        out_shape=jax.ShapeDtypeStruct((steps * HEAT_N, 8, HALF), F32),
         in_specs=[
-            block,
-            pl.BlockSpec((HEAT_N, 8, 128), lambda d: (d, HALF // 8, 0)),
+            pl.BlockSpec((HEAT_N, HALF, 128), lambda d: (d + first, 0, 0)),
+            pl.BlockSpec((HEAT_N, 8, 128), lambda d: (d + first, HALF // 8, 0)),
             pl.BlockSpec((1, 128), lambda d: (0, 0)),
             pl.BlockSpec((256, 256), lambda d: (0, 0)),
             pl.BlockSpec((8, 128), lambda d: (0, 0)),
         ],
         out_specs=pl.BlockSpec((HEAT_N, 8, HALF), lambda d: (d, 0, 0)),
         compiler_params=pltpu.CompilerParams(vmem_limit_bytes=ROOM),
-        cost_estimate=pl.CostEstimate(flops=2 * 10**10, bytes_accessed=8 << 20, transcendentals=SUB << 20),
+        cost_estimate=pl.CostEstimate(
+            flops=25 * 10**8 * steps, bytes_accessed=steps << 20, transcendentals=steps << 21
+        ),
         name="home_heat",
     )(rows, rows, fw, weights, flux)
 
 
-DEP_N = 4
+DEP_N = GROUP
+HEAT_A = 2
+
+
+def columns(values):
+    v0 = values.astype(BF16).astype(F32)
+    v1 = (values - v0).astype(BF16).astype(F32)
+    row8 = iota((8, values.shape[1]), 0)
+    terms = jnp.where(row8 == 0, v0, jnp.where(row8 == 1, v1, jnp.where(row8 == 2, values - v0 - v1, 0.0)))
+    pick = jnp.where(iota((8, 128), 0) < 3, 1.0, 0.0).astype(BF16)
+    return lax.dot_general(
+        terms.astype(BF16), pick, (((0,), (0,)), ((), ())), preferred_element_type=F32
+    )
 
 
 def deposit_kernel(
-    lanes_ref, heat_ref, cells_ref, vel_ref, dif_ref, flux_ref, below_ref, above_ref, left_ref, right_ref,
+    lanes_ref, heat_a_ref, heat_b_ref, cells_ref, vel_ref, dif_ref, flux_ref, below_ref, above_ref, left_ref, right_ref,
     out_ref, acc,
 ):
     d = pl.program_id(0)
@@ -431,7 +430,8 @@
     cols, rows, heats = [], [], []
     for i in range(DEP_N):
         nums = lanes_ref[i]
-        heat = jnp.concatenate([heat_ref[i, 0:1], heat_ref[i, 1:2]], axis=1)
+        both = jnp.where(d < HEAT_A, heat_a_ref[i], heat_b_ref[i])
+        heat = jnp.concatenate([both[0:1], both[1:2]], axis=1)
         cols.append(nums[0:1])
         rows.append(nums[1:2])
         heats.append(jnp.where(nums[3:4] > 0.5, 0.5 * heat, nil))
@@ -450,7 +450,7 @@
     def _():
         layers = ROWS // 64
         wall, lane = iota((64, 128), 0), iota((64, 128), 1)
-        left, right = left_ref[...], right_ref[...]
+        left, right = columns(left_ref[...]), columns(right_ref[...])
         for x in range(layers):
             at = 64 * x
             h = cells_ref[at : at + 64]
@@ -458,15 +458,15 @@
             x_upper = cells_ref[at + 64 : at + 128] if x < layers - 1 else above_ref[...]
             w_lower = jnp.where(wall == 0, h, pltpu.roll(h, 1, 0))
             w_upper = jnp.where(wall == 63, h, pltpu.roll(h, 63, 0))
-            s_lower = jnp.where(lane == 0, left[:, x : x + 1], pltpu.roll(h, 1, 1))
-            s_upper = jnp.where(lane == 127, right[:, x : x + 1], pltpu.roll(h, 127, 1))
+            s_lower = jnp.where(lane == 0, left[at : at + 64], pltpu.roll(h, 1, 1))
+            s_upper = jnp.where(lane == 127, right[at : at + 64], pltpu.roll(h, 127, 1))
             laplace = (x_lower + x_upper) + (w_lower + w_upper) + (s_lower + s_upper) - 6.0 * h
             new = h + dif_ref[at : at + 64] * laplace - vel_ref[at : at + 64] * (h - x_lower)
             new = new + jnp.where(wall == 0, flux_ref[x : x + 1], nil)
             out_ref[at : at + 64] = new + (acc[at : at + 64, :128] + acc[at : at + 64, 128:])
 
 
-def deposit(lanes, heat, cells, velocity, diffusivity, wall_flux, edges):
+def deposit(lanes, heat_a, heat_b, cells, velocity, diffusivity, wall_flux, edges):
     def whole(shape):
         return pl.BlockSpec(shape, lambda d: (0, 0))
 
@@ -477,47 +477,81 @@
         out_shape=jax.ShapeDtypeStruct((ROWS, 128), F32),
         in_specs=[
             pl.BlockSpec((DEP_N, 8, MSG), lambda d: (d, 0, 0)),
-            pl.BlockSpec((DEP_N, 8, HALF), lambda d: (d, 0, 0)),
+            pl.BlockSpec((DEP_N, 8, HALF), lambda d: (jnp.minimum(d, HEAT_A - 1), 0, 0)),
+            pl.BlockSpec((DEP_N, 8, HALF), lambda d: (jnp.maximum(d - HEAT_A, 0), 0, 0)),
             field,
             field,
             field,
             whole((ROWS // 64, 128)),
             whole((64, 128)),
             whole((64, 128)),
-            whole((64, ROWS // 64)),
-            whole((64, ROWS // 64)),
+            whole((1, ROWS)),
+            whole((1, ROWS)),
         ],
         out_specs=field,
         scratch_shapes=[pltpu.VMEM((ROWS, 256), F32)],
         compiler_params=pltpu.CompilerParams(vmem_limit_bytes=40 * 2**20),
         cost_estimate=pl.CostEstimate(flops=10**10, bytes_accessed=4 << 20, transcendentals=0),
         name="deposit",
-    )(lanes, heat, cells, velocity, diffusivity, wall_flux, *edges)
+    )(lanes, heat_a, heat_b, cells, velocity, diffusivity, wall_flux, *edges)
 
 
 SETTLE = 1024
 
 
-def settle_kernel(amount_ref, slot_ref, rows_ref, fw_ref, weights_ref, out_ref, stage, comb):
+def settle_kernel(
+    rows_ref, fw_ref, weights_ref, out_ref,
+    stage, comb, got, got_sem, side, side_sem, slot_v, slot_s, slot_sem, amount_v, amount_s, amount_sem,
+):
+    fetch_side = pltpu.make_async_copy(rows_ref.at[:, pl.ds(HALF, 8)], side, side_sem)
+    fetch_side.start()
+
+    def fetch(g):
+        part = pl.ds(g * GROUP, GROUP)
+        return pltpu.make_async_copy(rows_ref.at[part, pl.ds(0, HALF)], got.at[part], got_sem.at[g])
+
+    for g in range(NT // GROUP):
+        fetch(g).start()
+    fetch_side.wait()
+    for t in range(NT):
+        slot_v[4 * t : 4 * t + 4] = side[t, 0:4].astype(I32)
+    valid = jnp.where(slot_v[...] < OWN, 1.0, 0.0).astype(BF16)
+    by_row = dot(valid, jnp.ones((128, 128), BF16)).astype(BF16)
+    of_sender = jnp.where(iota((NT, 128), 1) >> 2 == iota((NT, 128), 0), 1.0, 0.0).astype(BF16)
+    amount_v[...] = dot(of_sender, by_row).astype(I32)
+    copies = (
+        pltpu.make_async_copy(slot_v, slot_s, slot_sem),
+        pltpu.make_async_copy(amount_v, amount_s, amount_sem),
+    )
+    for copy in copies:
+        copy.start()
+
     low_lanes = iota((HALF, 128), 1) < 64
 
-    @pl.loop(0, NT, unroll=4)
-    def _(t):
-        rows = rows_ref[t, 0:HALF]
-        col = far_columns(rows_ref[t, HALF:LOAD])
-        at = pl.multiple_of(t * MSG, MSG)
-        comb[pl.ds(at, HALF)] = jnp.where(low_lanes, rows, col[:HALF])
-        comb[pl.ds(pl.multiple_of(at + HALF, HALF), HALF)] = jnp.where(
-            low_lanes, pltpu.roll(rows, 64, 1), col[HALF:]
-        )
+    @pl.loop(0, NT // GROUP)
+    def _(g):
+        fetch(g).wait()
+        for k in range(GROUP):
+            t = GROUP * g + k
+            rows = got[t]
+            col = far_columns(side[t])
+            at = pl.multiple_of(t * MSG, MSG)
+            comb[pl.ds(at, HALF)] = jnp.where(low_lanes, rows, col[:HALF])
+            comb[pl.ds(pl.multiple_of(at + HALF, HALF), HALF)] = jnp.where(
+                low_lanes, pltpu.roll(rows, 64, 1), col[HALF:]
+            )
+
+    for copy in copies:
+        copy.wait()
 
     @pl.loop(0, NT)
     def _(t):
-        @pl.loop(0, (amount_ref[t] + 31) >> 5)
+        @pl.loop(0, (amount_s[t, 0] + 31) >> 5)
         def _(k):
             at = pl.multiple_of(t * MSG + 32 * k, 32)
+            row, lane = t * 4 + (k >> 2), (k & 3) * 32
             for i in range(32):
-                stage[pl.ds(slot_ref[at + i], 1)] = comb[pl.ds(at + i, 1)]
+                stage[pl.ds(slot_s[row, lane + i], 1)] = comb[pl.ds(at + i, 1)]
 
     weights = weights_ref[...]
     fw = fw_ref[...]
@@ -536,20 +570,33 @@
             out_ref[:, at + OWN2 + 128 * k : at + OWN2 + 128 * k + 128] = turned[64:]
 
 
-def settle(amount, slots, rows, fw, weights):
-    vmem, smem = pl.BlockSpec(memory_space=pltpu.VMEM), pl.BlockSpec(memory_space=pltpu.SMEM)
+def settle(rows, fw, weights):
+    vmem = pl.BlockSpec(memory_space=pltpu.VMEM)
     return pl.pallas_call(
         settle_kernel,
         out_shape=jax.ShapeDtypeStruct((PTS, OWN), F32),
-        in_specs=[smem, smem, vmem, vmem, vmem],
+        in_specs=[pl.BlockSpec(memory_space=pl.ANY), vmem, vmem],
         out_specs=vmem,
-        scratch_shapes=[pltpu.VMEM((OWN + 8, 128), F32), pltpu.VMEM((NT * MSG, 128), F32)],
-        compiler_params=pltpu.CompilerParams(vmem_limit_bytes=40 * 2**20),
+        scratch_shapes=[
+            pltpu.VMEM((OWN + 8, 128), F32),
+            pltpu.VMEM((NT * MSG, 128), F32),
+            pltpu.VMEM((NT, HALF, 128), F32),
+            pltpu.SemaphoreType.DMA((NT // GROUP,)),
+            pltpu.VMEM((NT, 8, 128), F32),
+            pltpu.SemaphoreType.DMA,
+            pltpu.VMEM((128, 128), I32),
+            pltpu.SMEM((128, 128), I32),
+            pltpu.SemaphoreType.DMA,
+            pltpu.VMEM((NT, 128), I32),
+            pltpu.SMEM((NT, 128), I32),
+            pltpu.SemaphoreType.DMA,
+        ],
+        compiler_params=pltpu.CompilerParams(vmem_limit_bytes=ROOM),
         name="settle",
-    )(amount, slots, rows, fw, weights)
-
-
-def edges_of(cells):
+    )(rows, fw, weights)
+
+
+def edges_of(cells, ends):
     n_x, n_s = lax.axis_size("stream"), lax.axis_size("tile")
     up_x = [(i, i + 1) for i in range(n_x - 1)]
     down_x = [(i + 1, i) for i in range(n_x - 1)]
@@ -557,9 +604,9 @@
     down_s = [((i + 1) % n_s, i) for i in range(n_s)]
     below = lax.ppermute(cells[-1], "stream", up_x)
     above = lax.ppermute(cells[0], "stream", down_x)
-    left = lax.ppermute(cells[:, :, -1], "tile", up_s)
-    right = lax.ppermute(cells[:, :, 0], "tile", down_s)
-    return below, above, left.T, right.T
+    left = lax.ppermute(ends[1:2], "tile", up_s)
+    right = lax.ppermute(ends[0:1], "tile", down_s)
+    return below, above, left, right
 
 
 def on_device(
@@ -567,8 +614,7 @@
     radial_step, far_weights, flux_weights,
 ):
     table = enthalpy.reshape(ROWS, 128)
-    rows, meta, lanes = route(counts, owners, cells, profiles)
-    rows = far_gather(rows, meta, table)
+    rows, lanes, ends = route(counts, owners, cells, table, profiles)
     rows, radial_step, far_weights, flux_weights = lax.optimization_barrier(
         (rows, radial_step, far_weights, flux_weights)
     )
@@ -576,15 +622,14 @@
     fw = jnp.concatenate([far_weights, far_weights])[None, :]
     flux = flux_rows(flux_weights)
     got = lax.all_to_all(rows, "tile", split_axis=0, concat_axis=0, tiled=True)
-    heat = home_heat(rows, fw, weights, flux)
-    ends, heat = lax.optimization_barrier((enthalpy, heat))
+    heat_a = home_heat(rows, fw, weights, flux, 0, HEAT_A)
+    layers, ends, heat_a = lax.optimization_barrier((enthalpy, ends, heat_a))
+    heat_b = home_heat(rows, fw, weights, flux, HEAT_A, NT // HEAT_N - HEAT_A)
     new_enthalpy = deposit(
-        lanes, heat, table, velocity.reshape(ROWS, 128), diffusivity.reshape(ROWS, 128), wall_flux,
-        edges_of(ends),
+        lanes, heat_a, heat_b, table, velocity.reshape(ROWS, 128), diffusivity.reshape(ROWS, 128),
+        wall_flux, edges_of(layers, ends),
     ).reshape(enthalpy.shape)
-    slots = got[:, HALF : HALF + 4].reshape(NT, MSG).astype(I32)
-    amount = jnp.sum((slots < OWN).astype(I32), axis=1)
-    new_profiles = settle(amount, slots.reshape(-1), got, fw, weights)
+    new_profiles = settle(got, fw, weights)
     return new_enthalpy, new_profiles
 
 

time: 138 us -> 144 us (1.043)
  the two profiles are of different devices: /device:TPU:35 before, /device:TPU:67 now
where the time goes in v5:
time: 144 us; the launch traced here: 143 us
  Pallas kernels  102 us (71%)
  starting transfers between devices  22.4 us (16%)
  waiting for transfers between devices  12.9 us (9%)
  other arithmetic  2.07 us (1%)
  local copies, waits for them, and re-layouts  2.04 us (1%)
  between operations  1.62 us (1%)
    pallas_call x1, Pallas kernels, route(): pl.pallas_call(route_kernel, out_shape=(jax.ShapeDtypeStruct((NT, LOAD, 1...  30.6 us
    pallas_call x1, Pallas kernels, settle(): pl.pallas_call(settle_kernel, out_shape=jax.ShapeDtypeStruct((PTS, OWN),...  30.4 us
    pallas_call x2, Pallas kernels, home_heat(): pl.pallas_call(heat_kernel, grid=(steps,), out_shape=jax.ShapeDtypeStruct...  28.9 us
    all_to_all x1, starting transfers between devices, on_device(): got = lax.all_to_all(rows, 'tile', split_axis=0, concat_axis=0, tiled=True)  15 us
    pallas_call x1, Pallas kernels, deposit(): pl.pallas_call(deposit_kernel, grid=(NT // DEP_N,), out_shape=jax.ShapeDt...  12.3 us
    ppermute x1, waiting for transfers between devices, edges_of(): right = lax.ppermute(ends[0:1], 'tile', down_s)  6.85 us
    ppermute x1, waiting for transfers between devices, edges_of(): left = lax.ppermute(ends[1:2], 'tile', up_s)  6.04 us
    ppermute x1, starting transfers between devices, edges_of(): above = lax.ppermute(cells[0], 'stream', down_x)  3.36 us
  transfers between devices with their start and end apart: 5, of which 2 were waited for; matrix products, arithmetic and copies ran while one was open for 2% of the time, Pallas kernels for 29%

profile of v5, /device:TPU:67, one launch (start us, length us, event | category | flops | bytes accessed | tf_op | source)
XLA Modules:
  0.0 143.1 jit_solution(1807772405022585286)
XLA Ops:
  1.3 30.6 %route.1 = (f32[32,264,128]{2,1,0:T(8,128)}, f32[32,8,512]{2,1,0:T(8,128)}, f32[8,1024]{1,0:T(8,128)}) custom-call(s32[1]{0:T(128)S(6)} %copy.14.count_ref, s32[128,128]{1,0:T(8,128)} %bitcast.22, s32[128,128]{1,0:T(8,128)} %bitcast.23, f32[1024,128]{1,0:T(8,128)} %bitcast.17, f32[64,16384]{1,0:T(8,128)} %prof_ref.1), custom_call_target="tpu_custom_call" | custom-call | tf_op jit(solution)/shard_map/route/pallas_call | solution.py:292
  31.8 0.0 copy-start.7
  31.9 0.0 copy-start.8
  31.9 0.0 copy-start.9
  31.9 15.0 %all-to-all-start = ((f32[32,264,128]{2,1,0:T(8,128)}), f32[32,264,128]{2,1,0:T(8,128)}, u32[]{:S(2)}, u32[]{:S(2)}) async-start(f32[32,264,128]{2,1,0:T(8,128)} %get-tuple-element.15.rows_ref.side_ref), calls=%async_computation | async-start | bytes 8650752 | tf_op jit(solution)/shard_map/all_to_all | solution.py:624
  46.9 0.1 pad.6.clone
  47.0 0.1 pad.7.clone
  47.1 0.0 copy-done.7
  47.1 0.1 copy.13
  47.1 0.0 copy-done.8
  47.2 0.0 copy-done.9
  47.2 0.7 pad_bitcast_fusion.1
  47.8 0.1 reduce-precision_convert_fusion
  47.9 0.7 maximum_maximum_fusion.weights_ref
  48.6 0.7 maximum_multiply_fusion.flux_ref
  49.2 8.1 %home_heat.2.heat_a_ref = f32[8,8,256]{2,1,0:T(8,128)} custom-call(f32[32,264,128]{2,1,0:T(8,128)} %get-tuple-element.15.rows_ref.side_ref, f32[32,264,128]{2,1,0:T(8,128)} %get-tuple-element.15.rows_ref.side_ref, f32[1,128]{1,0:T(1,128)} %get-tuple-element.30.fw_ref, bf16[256,256]{1,0:T(8,128)(2,1)} %maximum_maximum_fusion.weights_ref, ...), custom_call_target="tpu_custom_call" | custom-call | flops 5000000000 | bytes 2097152 | tf_op jit(solution)/shard_map/home_heat/pallas_call | solution.py:383
  57.3 0.0 copy-done
  57.3 1.9 %collective-permute-start = (f32[64,128]{1,0:T(8,128)S(1)}, f32[64,128]{1,0:T(8,128)S(1)}, u32[]{:S(2)}, u32[]{:S(2)}) collective-permute-start(f32[64,128]{1,0:T(8,128)S(1)} %get-tuple-element.23), channel_id=1, source_target_pairs={{0,32},{32,64},{64,96},{1,33},{33,65},{65,97},{2,34},{34,66},{66,9... | collective-permute-start | bytes 98312 | tf_op jit(solution)/shard_map/ppermute | solution.py:605
  59.3 3.4 %collective-permute-start.1 = (f32[64,128]{1,0:T(8,128)S(1)}, f32[64,128]{1,0:T(8,128)S(1)}, u32[]{:S(2)}, u32[]{:S(2)}) collective-permute-start(f32[64,128]{1,0:T(8,128)S(1)} %get-tuple-element.22), channel_id=1, source_target_pairs={{32,0},{64,32},{96,64},{33,1},{65,33},{97,65},{34,2},{66,34},{98,6... | collective-permute-start | bytes 98312 | tf_op jit(solution)/shard_map/ppermute | solution.py:606
  62.6 0.8 fusion.1
  63.5 2.0 %collective-permute-start.2 = (f32[1,1024]{1,0:T(1,128)S(1)}, f32[1,1024]{1,0:T(1,128)S(1)}, u32[]{:S(2)}, u32[]{:S(2)}) collective-permute-start(f32[1,1024]{1,0:T(1,128)S(1)} %get-tuple-element.25), channel_id=1, source_target_pairs={{0,1},{1,2},{2,3},{3,4},{4,5},{5,6},{6,7},{7,8},{8,9},{9,10},{10,1... | collective-permute-start | bytes 12296 | tf_op jit(solution)/shard_map/ppermute | solution.py:607
  65.5 0.1 collective-permute-start.3
  65.6 20.8 %home_heat.3.heat_b_ref = f32[24,8,256]{2,1,0:T(8,128)} custom-call(f32[32,264,128]{2,1,0:T(8,128)} %get-tuple-element.15.rows_ref.side_ref, f32[32,264,128]{2,1,0:T(8,128)} %get-tuple-element.15.rows_ref.side_ref, f32[1,128]{1,0:T(1,128)} %get-tuple-element.30.fw_ref, bf16[256,256]{1,0:T(8,128)(2,1)} %maximum_maximum_fusion.weights_ref, ...), custom_call_target="tpu_custom_call" | custom-call | flops 15000000512 | bytes 6291456 | tf_op jit(solution)/shard_map/home_heat/pallas_call | solution.py:383
  86.4 6.0 %collective-permute-done.2.left_ref = f32[1,1024]{1,0:T(1,128)S(1)} collective-permute-done((f32[1,1024]{1,0:T(1,128)S(1)}, f32[1,1024]{1,0:T(1,128)S(1)}, u32[]{:S(2)}, u32[]{:S(2)}) %collective-permute-start.2) | collective-permute-done | bytes 4128 | tf_op jit(solution)/shard_map/ppermute | solution.py:607
  92.4 6.8 %collective-permute-done.3.right_ref = f32[1,1024]{1,0:T(1,128)S(1)} collective-permute-done((f32[1,1024]{1,0:T(1,128)S(1)}, f32[1,1024]{1,0:T(1,128)S(1)}, u32[]{:S(2)}, u32[]{:S(2)}) %collective-permute-start.3) | collective-permute-done | bytes 4128 | tf_op jit(solution)/shard_map/ppermute | solution.py:608
  99.3 0.0 collective-permute-done.below_ref
  99.3 0.0 collective-permute-done.1.above_ref
  99.3 0.0 copy-start.6
  99.4 0.9 copy-done.6
  100.3 12.3 %deposit.1 = f32[1024,128]{1,0:T(8,128)} custom-call(f32[32,8,512]{2,1,0:T(8,128)S(1)} %copy-done.3, f32[8,8,256]{2,1,0:T(8,128)S(1)} %copy-done.5, f32[24,8,256]{2,1,0:T(8,128)S(1)} %copy-done.6, f32[1024,128]{1,0:T(8,128)S(1)} %bitcast.18, f32[1024,128]{1,0:T(8,128)S(1)} %bitcast.19, f32[1024,128]{1,0:T(8,128)S(1)} %bitcast.20, f32[16,128]{1,0:T(8,128)S(1)} %copy-done.4, ...), custom_call_target="tpu_custom_call" | custom-call | flops 10000000000 | bytes 4194304 | tf_op jit(solution)/shard_map/deposit/pallas_call | solution.py:474
  112.6 0.0 all-to-all-done.rows_ref
  112.6 30.4 %settle.1 = f32[64,6144]{1,0:T(8,128)} custom-call(f32[32,264,128]{2,1,0:T(8,128)} %all-to-all-done.rows_ref, f32[1,128]{1,0:T(1,128)} %get-tuple-element.30.fw_ref, bf16[256,256]{1,0:T(8,128)(2,1)} %maximum_maximum_fusion.weights_ref), custom_call_target="tpu_custom_call" | custom-call | tf_op jit(solution)/shard_map/settle/pallas_call | solution.py:575
  (14 shorter events, 0.0 us)
Async XLA Ops:
  31.8 15.2 %copy-start.7 = (f32[64,64]{1,0:T(8,128)S(1)}, f32[64,64]{1,0:T(8,128)}, u32[]{:S(2)}) copy-start(f32[64,64]{1,0:T(8,128)} %param.19) | copy-start | bytes 49156
  31.9 15.3 %copy-start.8 = (f32[64]{0:T(128)S(1)}, f32[64]{0:T(128)}, u32[]{:S(2)}) copy-start(f32[64]{0:T(128)} %param.21) | copy-start | bytes 772
  31.9 15.3 %copy-start.9 = (f32[64]{0:T(128)S(1)}, f32[64]{0:T(128)}, u32[]{:S(2)}) copy-start(f32[64]{0:T(128)} %param.20) | copy-start | bytes 772
  31.9 80.7 %all-to-all-start = ((f32[32,264,128]{2,1,0:T(8,128)}), f32[32,264,128]{2,1,0:T(8,128)}, u32[]{:S(2)}, u32[]{:S(2)}) async-start(f32[32,264,128]{2,1,0:T(8,128)} %get-tuple-element.15.rows_ref.side_ref), calls=%async_computation | async-start | bytes 8650752 | tf_op jit(solution)/shard_map/all_to_all | solution.py:624
  49.2 8.1 %copy-start = (f32[16,64,128]{2,1,0:T(8,128)S(1)}, f32[16,64,128]{2,1,0:T(8,128)}, u32[]{:S(2)}) copy-start(f32[16,64,128]{2,1,0:T(8,128)} %param.11) | copy-start | bytes 1572868
  57.3 42.0 %collective-permute-start = (f32[64,128]{1,0:T(8,128)S(1)}, f32[64,128]{1,0:T(8,128)S(1)}, u32[]{:S(2)}, u32[]{:S(2)}) collective-permute-start(f32[64,128]{1,0:T(8,128)S(1)} %get-tuple-element.23), channel_id=1, source_target_pairs={{0,32},{32,64},{64,96},{1,33},{33,65},{65,97},{2,34},{34,66},{66,9... | collective-permute-start | bytes 98312 | tf_op jit(solution)/shard_map/ppermute | solution.py:605
  59.3 40.0 %collective-permute-start.1 = (f32[64,128]{1,0:T(8,128)S(1)}, f32[64,128]{1,0:T(8,128)S(1)}, u32[]{:S(2)}, u32[]{:S(2)}) collective-permute-start(f32[64,128]{1,0:T(8,128)S(1)} %get-tuple-element.22), channel_id=1, source_target_pairs={{32,0},{64,32},{96,64},{33,1},{65,33},{97,65},{34,2},{66,34},{98,6... | collective-permute-start | bytes 98312 | tf_op jit(solution)/shard_map/ppermute | solution.py:606
  63.5 29.0 %collective-permute-start.2 = (f32[1,1024]{1,0:T(1,128)S(1)}, f32[1,1024]{1,0:T(1,128)S(1)}, u32[]{:S(2)}, u32[]{:S(2)}) collective-permute-start(f32[1,1024]{1,0:T(1,128)S(1)} %get-tuple-element.25), channel_id=1, source_target_pairs={{0,1},{1,2},{2,3},{3,4},{4,5},{5,6},{6,7},{7,8},{8,9},{9,10},{10,1... | collective-permute-start | bytes 12296 | tf_op jit(solution)/shard_map/ppermute | solution.py:607
  65.5 33.8 %copy-start.1 = (f32[16,64,128]{2,1,0:T(8,128)S(1)}, f32[16,64,128]{2,1,0:T(8,128)}, u32[]{:S(2)}) copy-start(f32[16,64,128]{2,1,0:T(8,128)} %param.12) | copy-start | bytes 1572868
  65.5 33.8 %copy-start.2 = (f32[16,64,128]{2,1,0:T(8,128)S(1)}, f32[16,64,128]{2,1,0:T(8,128)}, u32[]{:S(2)}) copy-start(f32[16,64,128]{2,1,0:T(8,128)} %param.13) | copy-start | bytes 1572868
  65.5 33.8 %copy-start.3 = (f32[32,8,512]{2,1,0:T(8,128)S(1)}, f32[32,8,512]{2,1,0:T(8,128)}, u32[]{:S(2)}) copy-start(f32[32,8,512]{2,1,0:T(8,128)} %get-tuple-element.12.lanes_ref) | copy-start | bytes 1572868
  65.5 33.8 %copy-start.4 = (f32[16,128]{1,0:T(8,128)S(1)}, f32[16,128]{1,0:T(8,128)}, u32[]{:S(2)}) copy-start(f32[16,128]{1,0:T(8,128)} %flux_ref.1) | copy-start | bytes 24580
  65.5 33.8 %copy-start.5 = (f32[8,8,256]{2,1,0:T(8,128)S(1)}, f32[8,8,256]{2,1,0:T(8,128)}, u32[]{:S(2)}) copy-start(f32[8,8,256]{2,1,0:T(8,128)} %home_heat.2.heat_a_ref) | copy-start | bytes 196612
  65.5 33.8 %collective-permute-start.3 = (f32[1,1024]{1,0:T(1,128)S(1)}, f32[1,1024]{1,0:T(1,128)S(1)}, u32[]{:S(2)}, u32[]{:S(2)}) collective-permute-start(f32[1,1024]{1,0:T(1,128)S(1)} %get-tuple-element.24), channel_id=1, source_target_pairs={{1,0},{2,1},{3,2},{4,3},{5,4},{6,5},{7,6},{8,7},{9,8},{10,9},{11,1... | collective-permute-start | bytes 12296 | tf_op jit(solution)/shard_map/ppermute | solution.py:608
  99.3 0.9 copy-start.6

commit v6 on v5

--- a/solution.py
+++ b/solution.py
@@ -141,9 +141,8 @@
         got = dot_nt(perm, data)
         out[0:BLK] = got[:, :128] + got[:, 128:]
 
-    def copy_block(j, inp):
-        chunk = (j >> 2) * 8
-        at = (j & 3) * NT
+    def copy_block(p, c, inp):
+        chunk, at = p * 8, c * NT
         most = tab_s[chunk + 3, at]
 
         @pl.when(most <= 8)
@@ -171,9 +170,8 @@
                 def _(k):
                     bucket[pl.ds(dst + 8 * k, 8)] = inp[pl.ds(src + 8 * k, 8)]
 
-    def copy_short(j, inp):
-        chunk = (j >> 2) * 8
-        at = (j & 3) * NT
+    def copy_short(p, c, inp):
+        chunk, at = p * 8, c * NT
         for d in range(NT):
             src = tab_s[chunk, at + d]
             dst = tab_s[chunk + 1, at + d]
@@ -189,13 +187,13 @@
         @pl.loop(0, quads)
         def _(p):
             sort_block(4 * p + 2, sorted_c)
-            copy_any(4 * p, sorted_a)
+            copy_any(p, 0, sorted_a)
             sort_block(4 * p + 3, sorted_d)
-            copy_any(4 * p + 1, sorted_b)
+            copy_any(p, 1, sorted_b)
             sort_block(jnp.minimum(4 * p + 4, NBLK - 1), sorted_a)
-            copy_any(4 * p + 2, sorted_c)
+            copy_any(p, 2, sorted_c)
             sort_block(jnp.minimum(4 * p + 5, NBLK - 1), sorted_b)
-            copy_any(4 * p + 3, sorted_d)
+            copy_any(p, 3, sorted_d)
 
     pl.when(short)(lambda: quad(copy_short))
     pl.when(jnp.logical_not(short))(lambda: quad(copy_block))
@@ -379,14 +377,15 @@
         heat_ref[i] = heat[:, HALF * i : HALF * i + HALF]
 
 
-def home_heat(rows, fw, weights, flux, first, steps):
+def home_heat(rows, fw, weights, flux):
+    steps = NT // HEAT_N
     return pl.pallas_call(
         heat_kernel,
         grid=(steps,),
         out_shape=jax.ShapeDtypeStruct((steps * HEAT_N, 8, HALF), F32),
         in_specs=[
-            pl.BlockSpec((HEAT_N, HALF, 128), lambda d: (d + first, 0, 0)),
-            pl.BlockSpec((HEAT_N, 8, 128), lambda d: (d + first, HALF // 8, 0)),
+            pl.BlockSpec((HEAT_N, HALF, 128), lambda d: (d, 0, 0)),
+            pl.BlockSpec((HEAT_N, 8, 128), lambda d: (d, HALF // 8, 0)),
             pl.BlockSpec((1, 128), lambda d: (0, 0)),
             pl.BlockSpec((256, 256), lambda d: (0, 0)),
             pl.BlockSpec((8, 128), lambda d: (0, 0)),
@@ -401,7 +400,6 @@
 
 
 DEP_N = GROUP
-HEAT_A = 2
 
 
 def columns(values):
@@ -416,7 +414,7 @@
 
 
 def deposit_kernel(
-    lanes_ref, heat_a_ref, heat_b_ref, cells_ref, vel_ref, dif_ref, flux_ref, below_ref, above_ref, left_ref, right_ref,
+    lanes_ref, heat_ref, cells_ref, vel_ref, dif_ref, flux_ref, below_ref, above_ref, left_ref, right_ref,
     out_ref, acc,
 ):
     d = pl.program_id(0)
@@ -430,8 +428,7 @@
     cols, rows, heats = [], [], []
     for i in range(DEP_N):
         nums = lanes_ref[i]
-        both = jnp.where(d < HEAT_A, heat_a_ref[i], heat_b_ref[i])
-        heat = jnp.concatenate([both[0:1], both[1:2]], axis=1)
+        heat = jnp.concatenate([heat_ref[i, 0:1], heat_ref[i, 1:2]], axis=1)
         cols.append(nums[0:1])
         rows.append(nums[1:2])
         heats.append(jnp.where(nums[3:4] > 0.5, 0.5 * heat, nil))
@@ -466,7 +463,7 @@
             out_ref[at : at + 64] = new + (acc[at : at + 64, :128] + acc[at : at + 64, 128:])
 
 
-def deposit(lanes, heat_a, heat_b, cells, velocity, diffusivity, wall_flux, edges):
+def deposit(lanes, heat, cells, velocity, diffusivity, wall_flux, edges):
     def whole(shape):
         return pl.BlockSpec(shape, lambda d: (0, 0))
 
@@ -477,8 +474,7 @@
         out_shape=jax.ShapeDtypeStruct((ROWS, 128), F32),
         in_specs=[
             pl.BlockSpec((DEP_N, 8, MSG), lambda d: (d, 0, 0)),
-            pl.BlockSpec((DEP_N, 8, HALF), lambda d: (jnp.minimum(d, HEAT_A - 1), 0, 0)),
-            pl.BlockSpec((DEP_N, 8, HALF), lambda d: (jnp.maximum(d - HEAT_A, 0), 0, 0)),
+            pl.BlockSpec((DEP_N, 8, HALF), lambda d: (d, 0, 0)),
             field,
             field,
             field,
@@ -493,7 +489,7 @@
         compiler_params=pltpu.CompilerParams(vmem_limit_bytes=40 * 2**20),
         cost_estimate=pl.CostEstimate(flops=10**10, bytes_accessed=4 << 20, transcendentals=0),
         name="deposit",
-    )(lanes, heat_a, heat_b, cells, velocity, diffusivity, wall_flux, *edges)
+    )(lanes, heat, cells, velocity, diffusivity, wall_flux, *edges)
 
 
 SETTLE = 1024
@@ -546,12 +542,15 @@
 
     @pl.loop(0, NT)
     def _(t):
-        @pl.loop(0, (amount_s[t, 0] + 31) >> 5)
-        def _(k):
-            at = pl.multiple_of(t * MSG + 32 * k, 32)
-            row, lane = t * 4 + (k >> 2), (k & 3) * 32
-            for i in range(32):
-                stage[pl.ds(slot_s[row, lane + i], 1)] = comb[pl.ds(at + i, 1)]
+        amount = amount_s[t, 0]
+        for first in range(0, MSG, 32):
+            row, lane = 4 * t + first // 128, first % 128
+
+            @pl.when(amount > first)
+            def _():
+                at = pl.multiple_of(t * MSG + first, 32)
+                for i in range(32):
+                    stage[pl.ds(slot_s[row, lane + i], 1)] = comb[pl.ds(at + i, 1)]
 
     weights = weights_ref[...]
     fw = fw_ref[...]
@@ -622,11 +621,10 @@
     fw = jnp.concatenate([far_weights, far_weights])[None, :]
     flux = flux_rows(flux_weights)
     got = lax.all_to_all(rows, "tile", split_axis=0, concat_axis=0, tiled=True)
-    heat_a = home_heat(rows, fw, weights, flux, 0, HEAT_A)
-    layers, ends, heat_a = lax.optimization_barrier((enthalpy, ends, heat_a))
-    heat_b = home_heat(rows, fw, weights, flux, HEAT_A, NT // HEAT_N - HEAT_A)
+    layers, ends = lax.optimization_barrier((enthalpy, ends))
+    heat = home_heat(rows, fw, weights, flux)
     new_enthalpy = deposit(
-        lanes, heat_a, heat_b, table, velocity.reshape(ROWS, 128), diffusivity.reshape(ROWS, 128),
+        lanes, heat, table, velocity.reshape(ROWS, 128), diffusivity.reshape(ROWS, 128),
         wall_flux, edges_of(layers, ends),
     ).reshape(enthalpy.shape)
     new_profiles = settle(got, fw, weights)

time: 144 us -> 131 us (0.910)
  the two profiles are of different devices: /device:TPU:67 before, /device:TPU:35 now
where the time goes in v6:
time: 131 us; the launch traced here: 130 us
  Pallas kernels  91.4 us (70%)
  starting transfers between devices  18.4 us (14%)
  waiting for transfers between devices  14.7 us (11%)
  local copies, waits for them, and re-layouts  2.14 us (2%)
  other arithmetic  2.01 us (2%)
  between operations  1.6 us (1%)
    pallas_call x1, Pallas kernels, route(): pl.pallas_call(route_kernel, out_shape=(jax.ShapeDtypeStruct((NT, LOAD, 1...  29.1 us
    pallas_call x1, Pallas kernels, home_heat(): pl.pallas_call(heat_kernel, grid=(steps,), out_shape=jax.ShapeDtypeStruct...  27.1 us
    pallas_call x1, Pallas kernels, settle(): pl.pallas_call(settle_kernel, out_shape=jax.ShapeDtypeStruct((PTS, OWN),...  23 us
    pallas_call x1, Pallas kernels, deposit(): pl.pallas_call(deposit_kernel, grid=(NT // DEP_N,), out_shape=jax.ShapeDt...  12.2 us
    all_to_all x1, starting transfers between devices, on_device(): got = lax.all_to_all(rows, 'tile', split_axis=0, concat_axis=0, tiled=True)  11.1 us
    ppermute x1, waiting for transfers between devices, edges_of(): left = lax.ppermute(ends[1:2], 'tile', up_s)  8.74 us
    ppermute x1, waiting for transfers between devices, edges_of(): right = lax.ppermute(ends[0:1], 'tile', down_s)  5.95 us
    ppermute x1, starting transfers between devices, edges_of(): above = lax.ppermute(cells[0], 'stream', down_x)  3.18 us
  transfers between devices with their start and end apart: 5, of which 2 were waited for; matrix products, arithmetic and copies ran while one was open for 2% of the time, Pallas kernels for 30%

profile of v6, /device:TPU:35, one launch (start us, length us, event | category | flops | bytes accessed | tf_op | source)
XLA Modules:
  0.0 130.3 jit_solution(12570337501391130988)
XLA Ops:
  1.3 29.1 %route.1 = (f32[32,264,128]{2,1,0:T(8,128)}, f32[32,8,512]{2,1,0:T(8,128)}, f32[8,1024]{1,0:T(8,128)}) custom-call(s32[1]{0:T(128)S(6)} %copy.14.count_ref, s32[128,128]{1,0:T(8,128)} %bitcast.22, s32[128,128]{1,0:T(8,128)} %bitcast.23, f32[1024,128]{1,0:T(8,128)} %bitcast.17, f32[64,16384]{1,0:T(8,128)} %prof_ref.1), custom_call_target="tpu_custom_call" | custom-call | tf_op jit(solution)/shard_map/route/pallas_call | solution.py:290
  30.4 0.0 copy-start
  30.4 0.0 copy-start.6
  30.4 0.0 copy-start.7
  30.4 0.0 copy-start.8
  30.4 11.1 %all-to-all-start = ((f32[32,264,128]{2,1,0:T(8,128)}), f32[32,264,128]{2,1,0:T(8,128)}, u32[]{:S(2)}, u32[]{:S(2)}) async-start(f32[32,264,128]{2,1,0:T(8,128)} %get-tuple-element.13.rows_ref.side_ref), calls=%async_computation | async-start | bytes 8650752 | tf_op jit(solution)/shard_map/all_to_all | solution.py:623
  41.5 0.0 copy-done
  41.5 2.1 %collective-permute-start = (f32[64,128]{1,0:T(8,128)S(1)}, f32[64,128]{1,0:T(8,128)S(1)}, u32[]{:S(2)}, u32[]{:S(2)}) collective-permute-start(f32[64,128]{1,0:T(8,128)S(1)} %get-tuple-element.21), channel_id=1, source_target_pairs={{0,32},{32,64},{64,96},{1,33},{33,65},{65,97},{2,34},{34,66},{66,9... | collective-permute-start | bytes 98312 | tf_op jit(solution)/shard_map/ppermute | solution.py:604
  43.7 3.2 %collective-permute-start.1 = (f32[64,128]{1,0:T(8,128)S(1)}, f32[64,128]{1,0:T(8,128)S(1)}, u32[]{:S(2)}, u32[]{:S(2)}) collective-permute-start(f32[64,128]{1,0:T(8,128)S(1)} %get-tuple-element.20), channel_id=1, source_target_pairs={{32,0},{64,32},{96,64},{33,1},{65,33},{97,65},{34,2},{66,34},{98,6... | collective-permute-start | bytes 98312 | tf_op jit(solution)/shard_map/ppermute | solution.py:605
  46.8 0.8 fusion.1
  47.7 2.0 %collective-permute-start.2 = (f32[1,1024]{1,0:T(1,128)S(1)}, f32[1,1024]{1,0:T(1,128)S(1)}, u32[]{:S(2)}, u32[]{:S(2)}) collective-permute-start(f32[1,1024]{1,0:T(1,128)S(1)} %get-tuple-element.23), channel_id=1, source_target_pairs={{0,1},{1,2},{2,3},{3,4},{4,5},{5,6},{6,7},{7,8},{8,9},{9,10},{10,1... | collective-permute-start | bytes 12296 | tf_op jit(solution)/shard_map/ppermute | solution.py:606
  49.7 0.0 collective-permute-start.3
  49.7 0.0 copy-done.6
  49.7 0.1 copy.13
  49.8 0.1 pad.6.clone
  49.9 0.1 pad.7.clone
  49.9 0.6 maximum_bitcast_fusion.fw_ref
  50.6 0.0 copy-done.8
  50.6 0.1 pad_bitcast_fusion.1
  50.6 0.1 reduce-precision_convert_fusion
  50.7 0.7 maximum_maximum_fusion.weights_ref
  51.4 0.6 maximum_multiply_fusion.flux_ref
  52.0 27.1 %home_heat.1.heat_ref = f32[32,8,256]{2,1,0:T(8,128)} custom-call(f32[32,264,128]{2,1,0:T(8,128)} %get-tuple-element.13.rows_ref.side_ref, f32[32,264,128]{2,1,0:T(8,128)} %get-tuple-element.13.rows_ref.side_ref, f32[1,128]{1,0:T(1,128)} %maximum_bitcast_fusion.fw_ref, bf16[256,256]{1,0:T(8,128)(2,1)} %maximum_maximum_fusion.weights_ref, ...), custom_call_target="tpu_custom_call" | custom-call | flops 20000000000 | bytes 8388608 | tf_op jit(solution)/shard_map/home_heat/pallas_call | solution.py:382
  79.2 8.7 %collective-permute-done.2.left_ref = f32[1,1024]{1,0:T(1,128)S(1)} collective-permute-done((f32[1,1024]{1,0:T(1,128)S(1)}, f32[1,1024]{1,0:T(1,128)S(1)}, u32[]{:S(2)}, u32[]{:S(2)}) %collective-permute-start.2) | collective-permute-done | bytes 4128 | tf_op jit(solution)/shard_map/ppermute | solution.py:606
  87.9 5.9 %collective-permute-done.3.right_ref = f32[1,1024]{1,0:T(1,128)S(1)} collective-permute-done((f32[1,1024]{1,0:T(1,128)S(1)}, f32[1,1024]{1,0:T(1,128)S(1)}, u32[]{:S(2)}, u32[]{:S(2)}) %collective-permute-start.3) | collective-permute-done | bytes 4128 | tf_op jit(solution)/shard_map/ppermute | solution.py:607
  93.9 0.0 collective-permute-done.below_ref
  93.9 0.0 collective-permute-done.1.above_ref
  93.9 0.0 copy-start.5
  93.9 0.9 copy-done.5
  94.9 12.2 %deposit.1 = f32[1024,128]{1,0:T(8,128)} custom-call(f32[32,8,512]{2,1,0:T(8,128)S(1)} %copy-done.3, f32[32,8,256]{2,1,0:T(8,128)S(1)} %copy-done.5, f32[1024,128]{1,0:T(8,128)S(1)} %bitcast.18, f32[1024,128]{1,0:T(8,128)S(1)} %bitcast.19, f32[1024,128]{1,0:T(8,128)S(1)} %bitcast.20, f32[16,128]{1,0:T(8,128)S(1)} %copy-done.4, ...), custom_call_target="tpu_custom_call" | custom-call | flops 10000000000 | bytes 4194304 | tf_op jit(solution)/shard_map/deposit/pallas_call | solution.py:471
  107.1 0.0 all-to-all-done.rows_ref
  107.1 23.0 %settle.1 = f32[64,6144]{1,0:T(8,128)} custom-call(f32[32,264,128]{2,1,0:T(8,128)} %all-to-all-done.rows_ref, f32[1,128]{1,0:T(1,128)} %maximum_bitcast_fusion.fw_ref, bf16[256,256]{1,0:T(8,128)(2,1)} %maximum_maximum_fusion.weights_ref), custom_call_target="tpu_custom_call" | custom-call | tf_op jit(solution)/shard_map/settle/pallas_call | solution.py:574
  (12 shorter events, 0.0 us)
Async XLA Ops:
  30.4 11.1 %copy-start = (f32[16,64,128]{2,1,0:T(8,128)S(1)}, f32[16,64,128]{2,1,0:T(8,128)}, u32[]{:S(2)}) copy-start(f32[16,64,128]{2,1,0:T(8,128)} %param.11) | copy-start | bytes 1572868
  30.4 19.3 %copy-start.6 = (f32[64,64]{1,0:T(8,128)S(1)}, f32[64,64]{1,0:T(8,128)}, u32[]{:S(2)}) copy-start(f32[64,64]{1,0:T(8,128)} %param.19) | copy-start | bytes 49156
  30.4 19.5 %copy-start.7 = (f32[64]{0:T(128)S(1)}, f32[64]{0:T(128)}, u32[]{:S(2)}) copy-start(f32[64]{0:T(128)} %param.20) | copy-start | bytes 772
  30.4 20.2 %copy-start.8 = (f32[64]{0:T(128)S(1)}, f32[64]{0:T(128)}, u32[]{:S(2)}) copy-start(f32[64]{0:T(128)} %param.21) | copy-start | bytes 772
  30.4 76.7 %all-to-all-start = ((f32[32,264,128]{2,1,0:T(8,128)}), f32[32,264,128]{2,1,0:T(8,128)}, u32[]{:S(2)}, u32[]{:S(2)}) async-start(f32[32,264,128]{2,1,0:T(8,128)} %get-tuple-element.13.rows_ref.side_ref), calls=%async_computation | async-start | bytes 8650752 | tf_op jit(solution)/shard_map/all_to_all | solution.py:623
  41.5 52.3 %collective-permute-start = (f32[64,128]{1,0:T(8,128)S(1)}, f32[64,128]{1,0:T(8,128)S(1)}, u32[]{:S(2)}, u32[]{:S(2)}) collective-permute-start(f32[64,128]{1,0:T(8,128)S(1)} %get-tuple-element.21), channel_id=1, source_target_pairs={{0,32},{32,64},{64,96},{1,33},{33,65},{65,97},{2,34},{34,66},{66,9... | collective-permute-start | bytes 98312 | tf_op jit(solution)/shard_map/ppermute | solution.py:604
  43.7 50.2 %collective-permute-start.1 = (f32[64,128]{1,0:T(8,128)S(1)}, f32[64,128]{1,0:T(8,128)S(1)}, u32[]{:S(2)}, u32[]{:S(2)}) collective-permute-start(f32[64,128]{1,0:T(8,128)S(1)} %get-tuple-element.20), channel_id=1, source_target_pairs={{32,0},{64,32},{96,64},{33,1},{65,33},{97,65},{34,2},{66,34},{98,6... | collective-permute-start | bytes 98312 | tf_op jit(solution)/shard_map/ppermute | solution.py:605
  47.7 40.3 %collective-permute-start.2 = (f32[1,1024]{1,0:T(1,128)S(1)}, f32[1,1024]{1,0:T(1,128)S(1)}, u32[]{:S(2)}, u32[]{:S(2)}) collective-permute-start(f32[1,1024]{1,0:T(1,128)S(1)} %get-tuple-element.23), channel_id=1, source_target_pairs={{0,1},{1,2},{2,3},{3,4},{4,5},{5,6},{6,7},{7,8},{8,9},{9,10},{10,1... | collective-permute-start | bytes 12296 | tf_op jit(solution)/shard_map/ppermute | solution.py:606
  49.7 44.2 %collective-permute-start.3 = (f32[1,1024]{1,0:T(1,128)S(1)}, f32[1,1024]{1,0:T(1,128)S(1)}, u32[]{:S(2)}, u32[]{:S(2)}) collective-permute-start(f32[1,1024]{1,0:T(1,128)S(1)} %get-tuple-element.22), channel_id=1, source_target_pairs={{1,0},{2,1},{3,2},{4,3},{5,4},{6,5},{7,6},{8,7},{9,8},{10,9},{11,1... | collective-permute-start | bytes 12296 | tf_op jit(solution)/shard_map/ppermute | solution.py:607
  52.0 41.9 %copy-start.1 = (f32[16,64,128]{2,1,0:T(8,128)S(1)}, f32[16,64,128]{2,1,0:T(8,128)}, u32[]{:S(2)}) copy-start(f32[16,64,128]{2,1,0:T(8,128)} %param.12) | copy-start | bytes 1572868
  52.0 41.9 %copy-start.2 = (f32[16,64,128]{2,1,0:T(8,128)S(1)}, f32[16,64,128]{2,1,0:T(8,128)}, u32[]{:S(2)}) copy-start(f32[16,64,128]{2,1,0:T(8,128)} %param.13) | copy-start | bytes 1572868
  52.0 41.9 %copy-start.3 = (f32[32,8,512]{2,1,0:T(8,128)S(1)}, f32[32,8,512]{2,1,0:T(8,128)}, u32[]{:S(2)}) copy-start(f32[32,8,512]{2,1,0:T(8,128)} %get-tuple-element.11.lanes_ref) | copy-start | bytes 1572868
  52.0 41.9 %copy-start.4 = (f32[16,128]{1,0:T(8,128)S(1)}, f32[16,128]{1,0:T(8,128)}, u32[]{:S(2)}) copy-start(f32[16,128]{1,0:T(8,128)} %flux_ref.1) | copy-start | bytes 24580
  93.9 1.0 copy-start.5

commit v7 on v6

--- a/solution.py
+++ b/solution.py
@@ -402,19 +402,8 @@
 DEP_N = GROUP
 
 
-def columns(values):
-    v0 = values.astype(BF16).astype(F32)
-    v1 = (values - v0).astype(BF16).astype(F32)
-    row8 = iota((8, values.shape[1]), 0)
-    terms = jnp.where(row8 == 0, v0, jnp.where(row8 == 1, v1, jnp.where(row8 == 2, values - v0 - v1, 0.0)))
-    pick = jnp.where(iota((8, 128), 0) < 3, 1.0, 0.0).astype(BF16)
-    return lax.dot_general(
-        terms.astype(BF16), pick, (((0,), (0,)), ((), ())), preferred_element_type=F32
-    )
-
-
 def deposit_kernel(
-    lanes_ref, heat_ref, cells_ref, vel_ref, dif_ref, flux_ref, below_ref, above_ref, left_ref, right_ref,
+    lanes_ref, heat_ref, cells_ref, vel_ref, dif_ref, flux_ref, below_ref, above_ref,
     out_ref, acc,
 ):
     d = pl.program_id(0)
@@ -447,7 +436,6 @@
     def _():
         layers = ROWS // 64
         wall, lane = iota((64, 128), 0), iota((64, 128), 1)
-        left, right = columns(left_ref[...]), columns(right_ref[...])
         for x in range(layers):
             at = 64 * x
             h = cells_ref[at : at + 64]
@@ -455,15 +443,15 @@
             x_upper = cells_ref[at + 64 : at + 128] if x < layers - 1 else above_ref[...]
             w_lower = jnp.where(wall == 0, h, pltpu.roll(h, 1, 0))
             w_upper = jnp.where(wall == 63, h, pltpu.roll(h, 63, 0))
-            s_lower = jnp.where(lane == 0, left[at : at + 64], pltpu.roll(h, 1, 1))
-            s_upper = jnp.where(lane == 127, right[at : at + 64], pltpu.roll(h, 127, 1))
+            s_lower = jnp.where(lane == 0, nil, pltpu.roll(h, 1, 1))
+            s_upper = jnp.where(lane == 127, nil, pltpu.roll(h, 127, 1))
             laplace = (x_lower + x_upper) + (w_lower + w_upper) + (s_lower + s_upper) - 6.0 * h
             new = h + dif_ref[at : at + 64] * laplace - vel_ref[at : at + 64] * (h - x_lower)
             new = new + jnp.where(wall == 0, flux_ref[x : x + 1], nil)
             out_ref[at : at + 64] = new + (acc[at : at + 64, :128] + acc[at : at + 64, 128:])
 
 
-def deposit(lanes, heat, cells, velocity, diffusivity, wall_flux, edges):
+def deposit(lanes, heat, cells, velocity, diffusivity, wall_flux, below, above):
     def whole(shape):
         return pl.BlockSpec(shape, lambda d: (0, 0))
 
@@ -481,15 +469,41 @@
             whole((ROWS // 64, 128)),
             whole((64, 128)),
             whole((64, 128)),
-            whole((1, ROWS)),
-            whole((1, ROWS)),
         ],
         out_specs=field,
         scratch_shapes=[pltpu.VMEM((ROWS, 256), F32)],
         compiler_params=pltpu.CompilerParams(vmem_limit_bytes=40 * 2**20),
         cost_estimate=pl.CostEstimate(flops=10**10, bytes_accessed=4 << 20, transcendentals=0),
         name="deposit",
-    )(lanes, heat, cells, velocity, diffusivity, wall_flux, *edges)
+    )(lanes, heat, cells, velocity, diffusivity, wall_flux, below, above)
+
+
+def span_kernel(new_ref, dif_ref, left_ref, right_ref, out_ref):
+    row8, lane = iota((8, ROWS), 0), iota((8, 128), 1)
+    terms = jnp.zeros((8, ROWS), F32)
+    for i, ref in enumerate((left_ref, right_ref)):
+        rest = ref[...]
+        for k in range(3):
+            high = rest.astype(BF16).astype(F32)
+            terms = jnp.where(row8 == 3 * i + k, high, terms)
+            rest = rest - high
+    row = iota((8, 128), 0)
+    first, last = (row < 3) & (lane == 0), (row >= 3) & (row < 6) & (lane == 127)
+    pick = jnp.where(first | last, 1.0, 0.0).astype(BF16)
+    ends = lax.dot_general(terms.astype(BF16), pick, (((0,), (0,)), ((), ())), preferred_element_type=F32)
+    out_ref[...] = new_ref[...] + dif_ref[...] * ends
+
+
+def add_span(new, diffusivity, left, right):
+    vmem = pl.BlockSpec(memory_space=pltpu.VMEM)
+    return pl.pallas_call(
+        span_kernel,
+        out_shape=jax.ShapeDtypeStruct((ROWS, 128), F32),
+        in_specs=[vmem] * 4,
+        out_specs=vmem,
+        cost_estimate=pl.CostEstimate(flops=10**7, bytes_accessed=2 << 20, transcendentals=0),
+        name="span",
+    )(new, diffusivity, left, right)
 
 
 SETTLE = 1024
@@ -524,9 +538,11 @@
 
     low_lanes = iota((HALF, 128), 1) < 64
 
-    @pl.loop(0, NT // GROUP)
+    for g in range(NT // GROUP):
+        fetch(g).wait()
+
+    @pl.loop(0, NT // GROUP, unroll=2)
     def _(g):
-        fetch(g).wait()
         for k in range(GROUP):
             t = GROUP * g + k
             rows = got[t]
@@ -543,14 +559,17 @@
     @pl.loop(0, NT)
     def _(t):
         amount = amount_s[t, 0]
-        for first in range(0, MSG, 32):
-            row, lane = 4 * t + first // 128, first % 128
-
-            @pl.when(amount > first)
-            def _():
-                at = pl.multiple_of(t * MSG + first, 32)
-                for i in range(32):
-                    stage[pl.ds(slot_s[row, lane + i], 1)] = comb[pl.ds(at + i, 1)]
+
+        @pl.loop(0, (amount + 127) >> 7)
+        def _(r):
+            row = 4 * t + r
+            for lane in range(0, 128, 32):
+
+                @pl.when(amount > r * 128 + lane)
+                def _():
+                    at = pl.multiple_of(t * MSG + r * 128 + lane, 32)
+                    for i in range(32):
+                        stage[pl.ds(slot_s[row, lane + i], 1)] = comb[pl.ds(at + i, 1)]
 
     weights = weights_ref[...]
     fw = fw_ref[...]
@@ -623,10 +642,10 @@
     got = lax.all_to_all(rows, "tile", split_axis=0, concat_axis=0, tiled=True)
     layers, ends = lax.optimization_barrier((enthalpy, ends))
     heat = home_heat(rows, fw, weights, flux)
-    new_enthalpy = deposit(
-        lanes, heat, table, velocity.reshape(ROWS, 128), diffusivity.reshape(ROWS, 128),
-        wall_flux, edges_of(layers, ends),
-    ).reshape(enthalpy.shape)
+    below, above, left, right = edges_of(layers, ends)
+    spread = diffusivity.reshape(ROWS, 128)
+    new = deposit(lanes, heat, table, velocity.reshape(ROWS, 128), spread, wall_flux, below, above)
+    new_enthalpy = add_span(new, spread, left, right).reshape(enthalpy.shape)
     new_profiles = settle(got, fw, weights)
     return new_enthalpy, new_profiles
 

time: 131 us -> 122 us (0.931)
  the two profiles are of different devices: /device:TPU:35 before, /device:TPU:32 now
where the time goes in v7:
time: 122 us; the launch traced here: 121 us
  Pallas kernels  90.7 us (74%)
  starting transfers between devices  22.2 us (18%)
  local copies, waits for them, and re-layouts  4.1 us (3%)
  other arithmetic  2.04 us (2%)
  between operations  1.63 us (1%)
    pallas_call x1, Pallas kernels, route(): pl.pallas_call(route_kernel, out_shape=(jax.ShapeDtypeStruct((NT, LOAD, 1...  28.4 us
    pallas_call x1, Pallas kernels, home_heat(): pl.pallas_call(heat_kernel, grid=(steps,), out_shape=jax.ShapeDtypeStruct...  27.1 us
    pallas_call x1, Pallas kernels, settle(): pl.pallas_call(settle_kernel, out_shape=jax.ShapeDtypeStruct((PTS, OWN),...  21.7 us
    all_to_all x1, starting transfers between devices, on_device(): got = lax.all_to_all(rows, 'tile', split_axis=0, concat_axis=0, tiled=True)  11.3 us
    pallas_call x1, Pallas kernels, deposit(): pl.pallas_call(deposit_kernel, grid=(NT // DEP_N,), out_shape=jax.ShapeDt...  11.2 us
    ppermute x1, starting transfers between devices, edges_of(): right = lax.ppermute(ends[0:1], 'tile', down_s)  5.05 us
    ppermute x1, starting transfers between devices, edges_of(): below = lax.ppermute(cells[-1], 'stream', up_x)  3.56 us
    unnamed x24, local copies, waits for them, and re-layouts  2.95 us
  transfers between devices with their start and end apart: 5, of which 0 were waited for; matrix products, arithmetic and copies ran while one was open for 3% of the time, Pallas kernels for 34%

profile of v7, /device:TPU:32, one launch (start us, length us, event | category | flops | bytes accessed | tf_op | source)
XLA Modules:
  0.0 120.7 jit_solution(15889636246801094527)
XLA Ops:
  1.3 28.4 %route.1 = (f32[32,264,128]{2,1,0:T(8,128)}, f32[32,8,512]{2,1,0:T(8,128)}, f32[8,1024]{1,0:T(8,128)}) custom-call(s32[1]{0:T(128)S(6)} %copy.14.count_ref, s32[128,128]{1,0:T(8,128)} %bitcast.24, s32[128,128]{1,0:T(8,128)} %bitcast.25, f32[1024,128]{1,0:T(8,128)} %bitcast.17, f32[64,16384]{1,0:T(8,128)} %prof_ref.1), custom_call_target="tpu_custom_call" | custom-call | tf_op jit(solution)/shard_map/route/pallas_call | solution.py:290
  29.7 0.0 copy-start
  29.7 0.0 copy-start.7
  29.7 0.0 copy-start.10
  29.7 0.0 copy-start.11
  29.7 11.3 %all-to-all-start = ((f32[32,264,128]{2,1,0:T(8,128)}), f32[32,264,128]{2,1,0:T(8,128)}, u32[]{:S(2)}, u32[]{:S(2)}) async-start(f32[32,264,128]{2,1,0:T(8,128)} %get-tuple-element.13.rows_ref.side_ref), calls=%async_computation | async-start | bytes 8650752 | tf_op jit(solution)/shard_map/all_to_all | solution.py:642
  41.1 3.6 %collective-permute-start = (f32[64,128]{1,0:T(8,128)S(1)}, f32[64,128]{1,0:T(8,128)S(1)}, u32[]{:S(2)}, u32[]{:S(2)}) collective-permute-start(f32[64,128]{1,0:T(8,128)S(1)} %get-tuple-element.21), channel_id=1, source_target_pairs={{0,32},{32,64},{64,96},{1,33},{33,65},{65,97},{2,34},{34,66},{66,9... | collective-permute-start | bytes 98312 | tf_op jit(solution)/shard_map/ppermute | solution.py:623
  44.6 2.3 %collective-permute-start.1 = (f32[64,128]{1,0:T(8,128)S(1)}, f32[64,128]{1,0:T(8,128)S(1)}, u32[]{:S(2)}, u32[]{:S(2)}) collective-permute-start(f32[64,128]{1,0:T(8,128)S(1)} %get-tuple-element.20), channel_id=1, source_target_pairs={{32,0},{64,32},{96,64},{33,1},{65,33},{97,65},{34,2},{66,34},{98,6... | collective-permute-start | bytes 98312 | tf_op jit(solution)/shard_map/ppermute | solution.py:624
  46.9 0.8 fusion.1
  47.8 0.0 collective-permute-start.2
  47.8 5.1 %collective-permute-start.3 = (f32[1,1024]{1,0:T(1,128)S(1)}, f32[1,1024]{1,0:T(1,128)S(1)}, u32[]{:S(2)}, u32[]{:S(2)}) collective-permute-start(f32[1,1024]{1,0:T(1,128)S(1)} %get-tuple-element.22), channel_id=1, source_target_pairs={{1,0},{2,1},{3,2},{4,3},{5,4},{6,5},{7,6},{8,7},{9,8},{10,9},{11,1... | collective-permute-start | bytes 12296 | tf_op jit(solution)/shard_map/ppermute | solution.py:626
  52.9 0.1 copy.13
  52.9 0.1 pad.6.clone
  53.0 0.1 pad.7.clone
  53.1 0.6 maximum_bitcast_fusion.fw_ref
  53.7 0.1 pad_bitcast_fusion.1
  53.8 0.1 reduce-precision_convert_fusion
  53.9 0.7 maximum_maximum_fusion.weights_ref
  54.6 0.7 maximum_multiply_fusion.flux_ref
  55.2 27.1 %home_heat.1.heat_ref = f32[32,8,256]{2,1,0:T(8,128)} custom-call(f32[32,264,128]{2,1,0:T(8,128)} %get-tuple-element.13.rows_ref.side_ref, f32[32,264,128]{2,1,0:T(8,128)} %get-tuple-element.13.rows_ref.side_ref, f32[1,128]{1,0:T(1,128)} %maximum_bitcast_fusion.fw_ref, bf16[256,256]{1,0:T(8,128)(2,1)} %maximum_maximum_fusion.weights_ref, ...), custom_call_target="tpu_custom_call" | custom-call | flops 20000000000 | bytes 8388608 | tf_op jit(solution)/shard_map/home_heat/pallas_call | solution.py:382
  82.4 0.0 collective-permute-done.below_ref
  82.4 0.0 collective-permute-done.1.above_ref
  82.4 0.0 copy-start.6
  82.4 0.9 copy-done.6
  83.4 11.2 %deposit.1.new_ref = f32[1024,128]{1,0:T(8,128)S(1)} custom-call(f32[32,8,512]{2,1,0:T(8,128)S(1)} %copy-done.4, f32[32,8,256]{2,1,0:T(8,128)S(1)} %copy-done.6, f32[1024,128]{1,0:T(8,128)S(1)} %bitcast.18, f32[1024,128]{1,0:T(8,128)S(1)} %bitcast.21, f32[1024,128]{1,0:T(8,128)S(1)} %bitcast.20, f32[16,128]{1,0:T(8,128)S(1)} %copy-done.5, ...), custom_call_target="tpu_custom_call" | custom-call | flops 10000000000 | bytes 4194304 | tf_op jit(solution)/shard_map/deposit/pallas_call | solution.py:459
  94.6 0.0 copy-start.2
  94.6 0.8 copy-done.2
  95.4 0.0 collective-permute-done.2.left_ref
  95.4 0.6 copy-done.8
  96.0 0.6 copy-done.9
  96.6 2.3 %span.1 = f32[1024,128]{1,0:T(8,128)} custom-call(f32[1024,128]{1,0:T(8,128)} %copy-done.2, f32[1024,128]{1,0:T(8,128)} %bitcast.19, f32[1,1024]{1,0:T(1,128)} %copy-done.8, f32[1,1024]{1,0:T(1,128)} %copy-done.9), custom_call_target="tpu_custom_call" | custom-call | flops 10000000 | bytes 2097152 | tf_op jit(solution)/shard_map/span/pallas_call | solution.py:499
  98.9 21.7 %settle.1 = f32[64,6144]{1,0:T(8,128)} custom-call(f32[32,264,128]{2,1,0:T(8,128)} %all-to-all-done.rows_ref, f32[1,128]{1,0:T(1,128)} %maximum_bitcast_fusion.fw_ref, bf16[256,256]{1,0:T(8,128)(2,1)} %maximum_maximum_fusion.weights_ref), custom_call_target="tpu_custom_call" | custom-call | tf_op jit(solution)/shard_map/settle/pallas_call | solution.py:593
  (19 shorter events, 0.0 us)
Async XLA Ops:
  29.7 11.4 %copy-start = (f32[16,64,128]{2,1,0:T(8,128)S(1)}, f32[16,64,128]{2,1,0:T(8,128)}, u32[]{:S(2)}) copy-start(f32[16,64,128]{2,1,0:T(8,128)} %param.11) | copy-start | bytes 1572868
  29.7 23.2 %copy-start.7 = (f32[64,64]{1,0:T(8,128)S(1)}, f32[64,64]{1,0:T(8,128)}, u32[]{:S(2)}) copy-start(f32[64,64]{1,0:T(8,128)} %param.19) | copy-start | bytes 49156
  29.7 23.4 %copy-start.10 = (f32[64]{0:T(128)S(1)}, f32[64]{0:T(128)}, u32[]{:S(2)}) copy-start(f32[64]{0:T(128)} %param.20) | copy-start | bytes 772
  29.7 24.0 %copy-start.11 = (f32[64]{0:T(128)S(1)}, f32[64]{0:T(128)}, u32[]{:S(2)}) copy-start(f32[64]{0:T(128)} %param.21) | copy-start | bytes 772
  29.7 69.2 %all-to-all-start = ((f32[32,264,128]{2,1,0:T(8,128)}), f32[32,264,128]{2,1,0:T(8,128)}, u32[]{:S(2)}, u32[]{:S(2)}) async-start(f32[32,264,128]{2,1,0:T(8,128)} %get-tuple-element.13.rows_ref.side_ref), calls=%async_computation | async-start | bytes 8650752 | tf_op jit(solution)/shard_map/all_to_all | solution.py:642
  41.1 41.3 %collective-permute-start = (f32[64,128]{1,0:T(8,128)S(1)}, f32[64,128]{1,0:T(8,128)S(1)}, u32[]{:S(2)}, u32[]{:S(2)}) collective-permute-start(f32[64,128]{1,0:T(8,128)S(1)} %get-tuple-element.21), channel_id=1, source_target_pairs={{0,32},{32,64},{64,96},{1,33},{33,65},{65,97},{2,34},{34,66},{66,9... | collective-permute-start | bytes 98312 | tf_op jit(solution)/shard_map/ppermute | solution.py:623
  44.6 37.8 %collective-permute-start.1 = (f32[64,128]{1,0:T(8,128)S(1)}, f32[64,128]{1,0:T(8,128)S(1)}, u32[]{:S(2)}, u32[]{:S(2)}) collective-permute-start(f32[64,128]{1,0:T(8,128)S(1)} %get-tuple-element.20), channel_id=1, source_target_pairs={{32,0},{64,32},{96,64},{33,1},{65,33},{97,65},{34,2},{66,34},{98,6... | collective-permute-start | bytes 98312 | tf_op jit(solution)/shard_map/ppermute | solution.py:624
  47.8 47.6 %collective-permute-start.2 = (f32[1,1024]{1,0:T(1,128)S(1)}, f32[1,1024]{1,0:T(1,128)S(1)}, u32[]{:S(2)}, u32[]{:S(2)}) collective-permute-start(f32[1,1024]{1,0:T(1,128)S(1)} %get-tuple-element.23), channel_id=1, source_target_pairs={{0,1},{1,2},{2,3},{3,4},{4,5},{5,6},{6,7},{7,8},{8,9},{9,10},{10,1... | collective-permute-start | bytes 12296 | tf_op jit(solution)/shard_map/ppermute | solution.py:625
  47.8 47.6 %collective-permute-start.3 = (f32[1,1024]{1,0:T(1,128)S(1)}, f32[1,1024]{1,0:T(1,128)S(1)}, u32[]{:S(2)}, u32[]{:S(2)}) collective-permute-start(f32[1,1024]{1,0:T(1,128)S(1)} %get-tuple-element.22), channel_id=1, source_target_pairs={{1,0},{2,1},{3,2},{4,3},{5,4},{6,5},{7,6},{8,7},{9,8},{10,9},{11,1... | collective-permute-start | bytes 12296 | tf_op jit(solution)/shard_map/ppermute | solution.py:626
  55.2 27.2 %copy-start.1 = (f32[16,64,128]{2,1,0:T(8,128)S(1)}, f32[16,64,128]{2,1,0:T(8,128)}, u32[]{:S(2)}) copy-start(f32[16,64,128]{2,1,0:T(8,128)} %param.13) | copy-start | bytes 1572868
  55.2 27.2 %copy-start.3 = (f32[16,64,128]{2,1,0:T(8,128)S(1)}, f32[16,64,128]{2,1,0:T(8,128)}, u32[]{:S(2)}) copy-start(f32[16,64,128]{2,1,0:T(8,128)} %param.12) | copy-start | bytes 1572868
  55.2 27.2 %copy-start.4 = (f32[32,8,512]{2,1,0:T(8,128)S(1)}, f32[32,8,512]{2,1,0:T(8,128)}, u32[]{:S(2)}) copy-start(f32[32,8,512]{2,1,0:T(8,128)} %get-tuple-element.11.lanes_ref) | copy-start | bytes 1572868
  55.2 27.2 %copy-start.5 = (f32[16,128]{1,0:T(8,128)S(1)}, f32[16,128]{1,0:T(8,128)}, u32[]{:S(2)}) copy-start(f32[16,128]{1,0:T(8,128)} %flux_ref.1) | copy-start | bytes 24580
  82.4 1.0 copy-start.6
  94.6 0.8 copy-start.2
  95.4 0.6 copy-start.8
  96.0 0.6 copy-start.9

commit v8 on v7

--- a/solution.py
+++ b/solution.py
@@ -238,17 +238,15 @@
     table[...] = jnp.concatenate([p[0] for p in parts] + [p[1] for p in parts], axis=1)
     m_rows = GROUP * HALF
     ones8 = jnp.ones((8, 256), BF16)
-    sub128 = iota((128, 128), 0)
     place = iota((m_rows, 128), 1).astype(F32)
 
     def far(g):
-        meta = meta_v[pl.ds(g * GROUP, GROUP)].reshape(m_rows, 128)
+        meta = meta_v[pl.ds(g * GROUP, GROUP)].reshape(m_rows, 128).astype(F32)
         for h in range(2):
             first = 0 if h == 0 else 64
-            col = jnp.where(sub128 == first, one, nil) + jnp.where(sub128 == first + 1, 128.0 * one, nil)
-            row = jnp.where(sub128 == first + 2, one, nil)
-            got = dot(meta, jnp.concatenate([col, row], axis=1).astype(BF16))
-            col, row = got[:, :128], got[:, 128:]
+            col = meta[:, first : first + 1] + 128.0 * meta[:, first + 1 : first + 2]
+            col = jnp.broadcast_to(col, (m_rows, 128))
+            row = jnp.broadcast_to(meta[:, first + 2 : first + 3], (m_rows, 128))
             hot = jnp.concatenate(
                 [jnp.where(row == place + 128.0 * q, one, nil).astype(BF16) for q in range(2)], axis=1
             )
@@ -345,7 +343,7 @@
     return (got[:, :128] + got[:, 128:]) + (add + 0.25 * jnp.tanh(state))
 
 
-HEAT_N = GROUP
+HEAT_N = 8
 
 
 def far_columns(side):
@@ -512,6 +510,7 @@
 def settle_kernel(
     rows_ref, fw_ref, weights_ref, out_ref,
     stage, comb, got, got_sem, side, side_sem, slot_v, slot_s, slot_sem, amount_v, amount_s, amount_sem,
+    out_v, out_sem,
 ):
     fetch_side = pltpu.make_async_copy(rows_ref.at[:, pl.ds(HALF, 8)], side, side_sem)
     fetch_side.start()
@@ -560,20 +559,30 @@
     def _(t):
         amount = amount_s[t, 0]
 
-        @pl.loop(0, (amount + 127) >> 7)
+        def move(r, lanes):
+            row = 4 * t + r
+            for lane in lanes:
+                stage[pl.ds(slot_s[row, lane], 1)] = comb[pl.ds(row * 128 + lane, 1)]
+
+        @pl.loop(0, amount >> 7)
         def _(r):
-            row = 4 * t + r
-            for lane in range(0, 128, 32):
-
-                @pl.when(amount > r * 128 + lane)
-                def _():
-                    at = pl.multiple_of(t * MSG + r * 128 + lane, 32)
-                    for i in range(32):
-                        stage[pl.ds(slot_s[row, lane + i], 1)] = comb[pl.ds(at + i, 1)]
+            move(r, range(128))
+
+        last = amount >> 7
+        for lane in range(0, 128, 32):
+
+            @pl.when((amount & 127) > lane)
+            def _():
+                move(last, range(lane, lane + 32))
 
     weights = weights_ref[...]
     fw = fw_ref[...]
     low_lanes = iota((SETTLE, 128), 1) < 64
+
+    def send(c, h):
+        part = pl.ds(c * SETTLE + h * OWN2, SETTLE)
+        return pltpu.make_async_copy(out_v.at[:, part], out_ref.at[:, part], out_sem.at[2 * c + h])
+
     for c in range(OWN2 // SETTLE):
         at = c * SETTLE
         a = stage[at : at + SETTLE]
@@ -584,8 +593,13 @@
             state = substep(state, add, weights)
         for k in range(SETTLE // 128):
             turned = state[128 * k : 128 * k + 128].T
-            out_ref[:, at + 128 * k : at + 128 * k + 128] = turned[:64]
-            out_ref[:, at + OWN2 + 128 * k : at + OWN2 + 128 * k + 128] = turned[64:]
+            out_v[:, at + 128 * k : at + 128 * k + 128] = turned[:64]
+            out_v[:, at + OWN2 + 128 * k : at + OWN2 + 128 * k + 128] = turned[64:]
+        for h in range(2):
+            send(c, h).start()
+    for c in range(OWN2 // SETTLE):
+        for h in range(2):
+            send(c, h).wait()
 
 
 def settle(rows, fw, weights):
@@ -594,7 +608,7 @@
         settle_kernel,
         out_shape=jax.ShapeDtypeStruct((PTS, OWN), F32),
         in_specs=[pl.BlockSpec(memory_space=pl.ANY), vmem, vmem],
-        out_specs=vmem,
+        out_specs=pl.BlockSpec(memory_space=pl.ANY),
         scratch_shapes=[
             pltpu.VMEM((OWN + 8, 128), F32),
             pltpu.VMEM((NT * MSG, 128), F32),
@@ -608,6 +622,8 @@
             pltpu.VMEM((NT, 128), I32),
             pltpu.SMEM((NT, 128), I32),
             pltpu.SemaphoreType.DMA,
+            pltpu.VMEM((PTS, OWN), F32),
+            pltpu.SemaphoreType.DMA((2 * OWN2 // SETTLE,)),
         ],
         compiler_params=pltpu.CompilerParams(vmem_limit_bytes=ROOM),
         name="settle",

time: 122 us -> 116 us (0.951)
  the two profiles are of different devices: /device:TPU:32 before, /device:TPU:35 now
where the time goes in v8:
time: 116 us; the launch traced here: 115 us
  Pallas kernels  89.4 us (77%)
  starting transfers between devices  15.2 us (13%)
  local copies, waits for them, and re-layouts  3.52 us (3%)
  waiting for transfers between devices  2.95 us (3%)
  other arithmetic  2.04 us (2%)
  between operations  1.62 us (1%)
    pallas_call x1, Pallas kernels, route(): pl.pallas_call(route_kernel, out_shape=(jax.ShapeDtypeStruct((NT, LOAD, 1...  29.4 us
    pallas_call x1, Pallas kernels, home_heat(): pl.pallas_call(heat_kernel, grid=(steps,), out_shape=jax.ShapeDtypeStruct...  25.9 us
    pallas_call x1, Pallas kernels, settle(): pl.pallas_call(settle_kernel, out_shape=jax.ShapeDtypeStruct((PTS, OWN),...  20.6 us
    pallas_call x1, Pallas kernels, deposit(): pl.pallas_call(deposit_kernel, grid=(NT // DEP_N,), out_shape=jax.ShapeDt...  11.2 us
    all_to_all x1, starting transfers between devices, on_device(): got = lax.all_to_all(rows, 'tile', split_axis=0, concat_axis=0, tiled=True)  7.85 us
    ppermute x1, waiting for transfers between devices, edges_of(): right = lax.ppermute(ends[0:1], 'tile', down_s)  2.94 us
    ppermute x1, starting transfers between devices, edges_of(): below = lax.ppermute(cells[-1], 'stream', up_x)  2.81 us
    ppermute x1, starting transfers between devices, edges_of(): above = lax.ppermute(cells[0], 'stream', down_x)  2.47 us
  transfers between devices with their start and end apart: 5, of which 1 were waited for; matrix products, arithmetic and copies ran while one was open for 3% of the time, Pallas kernels for 34%

profile of v8, /device:TPU:35, one launch (start us, length us, event | category | flops | bytes accessed | tf_op | source)
XLA Modules:
  0.0 114.7 jit_solution(15063456571938338970)
XLA Ops:
  1.3 29.4 %route.1 = (f32[32,264,128]{2,1,0:T(8,128)}, f32[32,8,512]{2,1,0:T(8,128)}, f32[8,1024]{1,0:T(8,128)}) custom-call(s32[1]{0:T(128)S(6)} %copy.14.count_ref, s32[128,128]{1,0:T(8,128)} %bitcast.24, s32[128,128]{1,0:T(8,128)} %bitcast.25, f32[1024,128]{1,0:T(8,128)} %bitcast.17, f32[64,16384]{1,0:T(8,128)} %prof_ref.1), custom_call_target="tpu_custom_call" | custom-call | tf_op jit(solution)/shard_map/route/pallas_call | solution.py:288
  30.7 0.0 copy-start
  30.7 0.0 copy-start.7
  30.7 0.0 copy-start.10
  30.7 0.0 copy-start.11
  30.7 7.9 %all-to-all-start = ((f32[32,264,128]{2,1,0:T(8,128)}), f32[32,264,128]{2,1,0:T(8,128)}, u32[]{:S(2)}, u32[]{:S(2)}) async-start(f32[32,264,128]{2,1,0:T(8,128)} %get-tuple-element.13.rows_ref.side_ref), calls=%async_computation | async-start | bytes 8650752 | tf_op jit(solution)/shard_map/all_to_all | solution.py:658
  38.6 2.8 %collective-permute-start = (f32[64,128]{1,0:T(8,128)S(1)}, f32[64,128]{1,0:T(8,128)S(1)}, u32[]{:S(2)}, u32[]{:S(2)}) collective-permute-start(f32[64,128]{1,0:T(8,128)S(1)} %get-tuple-element.21), channel_id=1, source_target_pairs={{0,32},{32,64},{64,96},{1,33},{33,65},{65,97},{2,34},{34,66},{66,9... | collective-permute-start | bytes 98312 | tf_op jit(solution)/shard_map/ppermute | solution.py:639
  41.4 2.5 %collective-permute-start.1 = (f32[64,128]{1,0:T(8,128)S(1)}, f32[64,128]{1,0:T(8,128)S(1)}, u32[]{:S(2)}, u32[]{:S(2)}) collective-permute-start(f32[64,128]{1,0:T(8,128)S(1)} %get-tuple-element.20), channel_id=1, source_target_pairs={{32,0},{64,32},{96,64},{33,1},{65,33},{97,65},{34,2},{66,34},{98,6... | collective-permute-start | bytes 98312 | tf_op jit(solution)/shard_map/ppermute | solution.py:640
  43.9 0.8 fusion.1
  44.8 2.0 %collective-permute-start.2 = (f32[1,1024]{1,0:T(1,128)S(1)}, f32[1,1024]{1,0:T(1,128)S(1)}, u32[]{:S(2)}, u32[]{:S(2)}) collective-permute-start(f32[1,1024]{1,0:T(1,128)S(1)} %get-tuple-element.23), channel_id=1, source_target_pairs={{0,1},{1,2},{2,3},{3,4},{4,5},{5,6},{6,7},{7,8},{8,9},{9,10},{10,1... | collective-permute-start | bytes 12296 | tf_op jit(solution)/shard_map/ppermute | solution.py:641
  46.8 0.0 collective-permute-start.3
  46.8 0.1 copy.13
  46.9 0.1 pad.6.clone
  46.9 0.1 pad.7.clone
  47.0 0.6 maximum_bitcast_fusion.fw_ref
  47.7 0.1 pad_bitcast_fusion.1
  47.7 0.1 reduce-precision_convert_fusion
  47.8 0.7 maximum_maximum_fusion.weights_ref
  48.5 0.7 maximum_multiply_fusion.flux_ref
  49.2 25.9 %home_heat.1.heat_ref = f32[32,8,256]{2,1,0:T(8,128)} custom-call(f32[32,264,128]{2,1,0:T(8,128)} %get-tuple-element.13.rows_ref.side_ref, f32[32,264,128]{2,1,0:T(8,128)} %get-tuple-element.13.rows_ref.side_ref, f32[1,128]{1,0:T(1,128)} %maximum_bitcast_fusion.fw_ref, bf16[256,256]{1,0:T(8,128)(2,1)} %maximum_maximum_fusion.weights_ref, ...), custom_call_target="tpu_custom_call" | custom-call | flops 10000000000 | bytes 4194304 | tf_op jit(solution)/shard_map/home_heat/pallas_call | solution.py:380
  75.1 0.0 collective-permute-done.below_ref
  75.1 0.0 collective-permute-done.1.above_ref
  75.1 0.0 copy-start.6
  75.1 0.9 copy-done.6
  76.1 11.2 %deposit.1.new_ref = f32[1024,128]{1,0:T(8,128)S(1)} custom-call(f32[32,8,512]{2,1,0:T(8,128)S(1)} %copy-done.4, f32[32,8,256]{2,1,0:T(8,128)S(1)} %copy-done.6, f32[1024,128]{1,0:T(8,128)S(1)} %bitcast.18, f32[1024,128]{1,0:T(8,128)S(1)} %bitcast.21, f32[1024,128]{1,0:T(8,128)S(1)} %bitcast.20, f32[16,128]{1,0:T(8,128)S(1)} %copy-done.5, ...), custom_call_target="tpu_custom_call" | custom-call | flops 10000000000 | bytes 4194304 | tf_op jit(solution)/shard_map/deposit/pallas_call | solution.py:457
  87.2 0.0 copy-start.2
  87.2 0.8 copy-done.2
  88.0 2.9 %collective-permute-done.3.right_ref = f32[1,1024]{1,0:T(1,128)S(1)} collective-permute-done((f32[1,1024]{1,0:T(1,128)S(1)}, f32[1,1024]{1,0:T(1,128)S(1)}, u32[]{:S(2)}, u32[]{:S(2)}) %collective-permute-start.3) | collective-permute-done | bytes 4128 | tf_op jit(solution)/shard_map/ppermute | solution.py:642
  91.0 0.6 copy-done.9
  91.6 2.3 %span.1 = f32[1024,128]{1,0:T(8,128)} custom-call(f32[1024,128]{1,0:T(8,128)} %copy-done.2, f32[1024,128]{1,0:T(8,128)} %bitcast.19, f32[1,1024]{1,0:T(1,128)} %copy-done.8, f32[1,1024]{1,0:T(1,128)} %copy-done.9), custom_call_target="tpu_custom_call" | custom-call | flops 10000000 | bytes 2097152 | tf_op jit(solution)/shard_map/span/pallas_call | solution.py:497
  93.9 0.0 all-to-all-done.rows_ref
  93.9 20.6 %settle.1 = f32[64,6144]{1,0:T(8,128)} custom-call(f32[32,264,128]{2,1,0:T(8,128)} %all-to-all-done.rows_ref, f32[1,128]{1,0:T(1,128)} %maximum_bitcast_fusion.fw_ref, bf16[256,256]{1,0:T(8,128)(2,1)} %maximum_maximum_fusion.weights_ref), custom_call_target="tpu_custom_call" | custom-call | tf_op jit(solution)/shard_map/settle/pallas_call | solution.py:607
  (19 shorter events, 0.0 us)
Async XLA Ops:
  30.7 7.9 %copy-start = (f32[16,64,128]{2,1,0:T(8,128)S(1)}, f32[16,64,128]{2,1,0:T(8,128)}, u32[]{:S(2)}) copy-start(f32[16,64,128]{2,1,0:T(8,128)} %param.11) | copy-start | bytes 1572868
  30.7 16.1 %copy-start.7 = (f32[64,64]{1,0:T(8,128)S(1)}, f32[64,64]{1,0:T(8,128)}, u32[]{:S(2)}) copy-start(f32[64,64]{1,0:T(8,128)} %param.19) | copy-start | bytes 49156
  30.7 16.3 %copy-start.10 = (f32[64]{0:T(128)S(1)}, f32[64]{0:T(128)}, u32[]{:S(2)}) copy-start(f32[64]{0:T(128)} %param.20) | copy-start | bytes 772
  30.7 16.9 %copy-start.11 = (f32[64]{0:T(128)S(1)}, f32[64]{0:T(128)}, u32[]{:S(2)}) copy-start(f32[64]{0:T(128)} %param.21) | copy-start | bytes 772
  30.7 63.1 %all-to-all-start = ((f32[32,264,128]{2,1,0:T(8,128)}), f32[32,264,128]{2,1,0:T(8,128)}, u32[]{:S(2)}, u32[]{:S(2)}) async-start(f32[32,264,128]{2,1,0:T(8,128)} %get-tuple-element.13.rows_ref.side_ref), calls=%async_computation | async-start | bytes 8650752 | tf_op jit(solution)/shard_map/all_to_all | solution.py:658
  38.6 36.4 %collective-permute-start = (f32[64,128]{1,0:T(8,128)S(1)}, f32[64,128]{1,0:T(8,128)S(1)}, u32[]{:S(2)}, u32[]{:S(2)}) collective-permute-start(f32[64,128]{1,0:T(8,128)S(1)} %get-tuple-element.21), channel_id=1, source_target_pairs={{0,32},{32,64},{64,96},{1,33},{33,65},{65,97},{2,34},{34,66},{66,9... | collective-permute-start | bytes 98312 | tf_op jit(solution)/shard_map/ppermute | solution.py:639
  41.4 33.6 %collective-permute-start.1 = (f32[64,128]{1,0:T(8,128)S(1)}, f32[64,128]{1,0:T(8,128)S(1)}, u32[]{:S(2)}, u32[]{:S(2)}) collective-permute-start(f32[64,128]{1,0:T(8,128)S(1)} %get-tuple-element.20), channel_id=1, source_target_pairs={{32,0},{64,32},{96,64},{33,1},{65,33},{97,65},{34,2},{66,34},{98,6... | collective-permute-start | bytes 98312 | tf_op jit(solution)/shard_map/ppermute | solution.py:640
  44.8 43.3 %collective-permute-start.2 = (f32[1,1024]{1,0:T(1,128)S(1)}, f32[1,1024]{1,0:T(1,128)S(1)}, u32[]{:S(2)}, u32[]{:S(2)}) collective-permute-start(f32[1,1024]{1,0:T(1,128)S(1)} %get-tuple-element.23), channel_id=1, source_target_pairs={{0,1},{1,2},{2,3},{3,4},{4,5},{5,6},{6,7},{7,8},{8,9},{9,10},{10,1... | collective-permute-start | bytes 12296 | tf_op jit(solution)/shard_map/ppermute | solution.py:641
  46.8 44.2 %collective-permute-start.3 = (f32[1,1024]{1,0:T(1,128)S(1)}, f32[1,1024]{1,0:T(1,128)S(1)}, u32[]{:S(2)}, u32[]{:S(2)}) collective-permute-start(f32[1,1024]{1,0:T(1,128)S(1)} %get-tuple-element.22), channel_id=1, source_target_pairs={{1,0},{2,1},{3,2},{4,3},{5,4},{6,5},{7,6},{8,7},{9,8},{10,9},{11,1... | collective-permute-start | bytes 12296 | tf_op jit(solution)/shard_map/ppermute | solution.py:642
  49.2 25.9 %copy-start.1 = (f32[16,64,128]{2,1,0:T(8,128)S(1)}, f32[16,64,128]{2,1,0:T(8,128)}, u32[]{:S(2)}) copy-start(f32[16,64,128]{2,1,0:T(8,128)} %param.13) | copy-start | bytes 1572868
  49.2 25.9 %copy-start.3 = (f32[16,64,128]{2,1,0:T(8,128)S(1)}, f32[16,64,128]{2,1,0:T(8,128)}, u32[]{:S(2)}) copy-start(f32[16,64,128]{2,1,0:T(8,128)} %param.12) | copy-start | bytes 1572868
  49.2 25.9 %copy-start.4 = (f32[32,8,512]{2,1,0:T(8,128)S(1)}, f32[32,8,512]{2,1,0:T(8,128)}, u32[]{:S(2)}) copy-start(f32[32,8,512]{2,1,0:T(8,128)} %get-tuple-element.11.lanes_ref) | copy-start | bytes 1572868
  49.2 25.9 %copy-start.5 = (f32[16,128]{1,0:T(8,128)S(1)}, f32[16,128]{1,0:T(8,128)}, u32[]{:S(2)}) copy-start(f32[16,128]{1,0:T(8,128)} %flux_ref.1) | copy-start | bytes 24580
  75.1 1.0 copy-start.6
  87.2 0.8 copy-start.2
  88.0 2.9 %copy-start.8 = (f32[1,1024]{1,0:T(1,128)}, f32[1,1024]{1,0:T(1,128)S(1)}, u32[]{:S(2)}) copy-start(f32[1,1024]{1,0:T(1,128)S(1)} %collective-permute-done.2.left_ref) | copy-start | bytes 12292
  91.0 0.6 copy-start.9

commit v9 on v8

--- a/solution.py
+++ b/solution.py
@@ -45,7 +45,7 @@
 
 def route_kernel(
     count_ref, owners_ref, cells_ref, field_ref, prof_ref,
-    rows_ref, lanes_ref, ends_ref,
+    rows_ref, lanes_ref, first_ref, last_ref,
     pos_s, m0_s, m1_s, m2_s, m3_s, m4_s, sorted_a, sorted_b, sorted_c, sorted_d,
     bucket, tab_v, tab_s, sem, prof_v, prof_sem, pack_v, pack_sem, meta_v, table,
 ):
@@ -277,7 +277,9 @@
     pick = pick.astype(BF16)
     f0, f1 = split(field_ref[...])
     f2 = (field_ref[...] - f0.astype(F32) - f1.astype(F32)).astype(BF16)
-    ends_ref[...] = dot_nt(pick, f0) + dot_nt(pick, f1) + dot_nt(pick, f2)
+    ends = dot_nt(pick, f0) + dot_nt(pick, f1) + dot_nt(pick, f2)
+    first_ref[...] = ends[0:1]
+    last_ref[...] = ends[1:2]
     for g in range(NT // GROUP):
         send(g).wait()
 
@@ -290,10 +292,11 @@
         out_shape=(
             jax.ShapeDtypeStruct((NT, LOAD, 128), F32),
             jax.ShapeDtypeStruct((NT, 8, MSG), F32),
-            jax.ShapeDtypeStruct((8, ROWS), F32),
+            jax.ShapeDtypeStruct((1, ROWS), F32),
+            jax.ShapeDtypeStruct((1, ROWS), F32),
         ),
         in_specs=[pl.BlockSpec(memory_space=pltpu.SMEM), vmem, vmem, vmem, anywhere],
-        out_specs=(anywhere, vmem, vmem),
+        out_specs=(anywhere, vmem, vmem, vmem),
         scratch_shapes=[pltpu.VMEM((NBLK, BLK), F32)] * 6
         + [pltpu.VMEM((BLK + 16, 128), F32)] * 4
         + [
@@ -313,28 +316,28 @@
     )(counts, owners.reshape(128, 128), cells.reshape(128, 128), field, profiles)
 
 
+def twice(row):
+    return jnp.concatenate([row, row], axis=1)
+
+
 def step_weights(radial_step):
-    zero = jnp.zeros((PTS, PTS), F32)
-    w = jnp.concatenate(
+    w0, w1 = split(radial_step.T)
+    w0, w1 = w0.astype(F32), w1.astype(F32)
+    nil = jnp.zeros((PTS, PTS), F32)
+    half = jnp.concatenate(
         [
-            jnp.concatenate([radial_step.T, zero], axis=1),
-            jnp.concatenate([zero, radial_step.T], axis=1),
+            jnp.concatenate([w0, nil, w1, nil], axis=1),
+            jnp.concatenate([nil, w0, nil, w1], axis=1),
         ],
         axis=0,
-    )
-    high = lax.reduce_precision(w, 8, 7)
-    w0, w1 = high.astype(BF16), (w - high).astype(BF16)
-    row = jnp.concatenate([w0, w1], axis=1)
-    return jnp.concatenate([row, row], axis=0)
+    ).astype(BF16)
+    return jnp.concatenate([half, half], axis=0)
 
 
 def flux_rows(flux_weights):
-    zero = jnp.zeros((PTS,), F32)
-    f = jnp.stack(
-        [jnp.concatenate([flux_weights, zero]), jnp.concatenate([zero, flux_weights])]
-        + [jnp.zeros((128,), F32)] * 6
-    )
-    return f / SUB
+    row, low = iota((8, 128), 0), iota((8, 128), 1) < 64
+    mine = ((row == 0) & low) | ((row == 1) & jnp.logical_not(low))
+    return jnp.where(mine, twice(flux_weights) / SUB, 0.0)
 
 
 def substep(state, add, weights):
@@ -355,46 +358,57 @@
     return lax.dot_general(terms, pick, (((0,), (0,)), ((), ())), preferred_element_type=F32)
 
 
-def heat_kernel(rows_ref, side_ref, fw_ref, weights_ref, flux_ref, heat_ref):
+def heat_kernel(rows_ref, side_ref, radial_ref, fw_ref, flux_ref, heat_ref, weights_ref):
+    @pl.when(pl.program_id(0) == 0)
+    def _():
+        weights_ref[...] = step_weights(radial_ref[...])
+
     weights = weights_ref[...]
+    fw = twice(fw_ref[...])
     state = rows_ref[...].reshape(HEAT_N * HALF, 128)
     low_lanes = iota((HALF, 128), 1) < 64
     adds = []
     for i in range(HEAT_N):
         far = far_columns(side_ref[i])
-        adds.append(fw_ref[...] * jnp.where(low_lanes, far[:HALF], far[HALF:]))
+        adds.append(fw * jnp.where(low_lanes, far[:HALF], far[HALF:]))
     add = jnp.concatenate(adds, axis=0)
     total = jnp.zeros_like(state)
     for _ in range(SUB):
         state = substep(state, add, weights)
         total = total + state
     t0, t1 = split(total)
-    f0, f1 = split(flux_ref[...])
+    f0, f1 = split(flux_rows(flux_ref[...]))
     heat = dot_nt(f0, t0) + dot_nt(f0, t1) + dot_nt(f1, t0)
     for i in range(HEAT_N):
         heat_ref[i] = heat[:, HALF * i : HALF * i + HALF]
 
 
-def home_heat(rows, fw, weights, flux):
+def home_heat(rows, radial_step, far_weights, flux_weights):
     steps = NT // HEAT_N
     return pl.pallas_call(
         heat_kernel,
         grid=(steps,),
-        out_shape=jax.ShapeDtypeStruct((steps * HEAT_N, 8, HALF), F32),
+        out_shape=(
+            jax.ShapeDtypeStruct((NT, 8, HALF), F32),
+            jax.ShapeDtypeStruct((256, 256), BF16),
+        ),
         in_specs=[
             pl.BlockSpec((HEAT_N, HALF, 128), lambda d: (d, 0, 0)),
             pl.BlockSpec((HEAT_N, 8, 128), lambda d: (d, HALF // 8, 0)),
-            pl.BlockSpec((1, 128), lambda d: (0, 0)),
+            pl.BlockSpec((PTS, PTS), lambda d: (0, 0)),
+            pl.BlockSpec((1, PTS), lambda d: (0, 0)),
+            pl.BlockSpec((1, PTS), lambda d: (0, 0)),
+        ],
+        out_specs=(
+            pl.BlockSpec((HEAT_N, 8, HALF), lambda d: (d, 0, 0)),
             pl.BlockSpec((256, 256), lambda d: (0, 0)),
-            pl.BlockSpec((8, 128), lambda d: (0, 0)),
-        ],
-        out_specs=pl.BlockSpec((HEAT_N, 8, HALF), lambda d: (d, 0, 0)),
+        ),
         compiler_params=pltpu.CompilerParams(vmem_limit_bytes=ROOM),
         cost_estimate=pl.CostEstimate(
             flops=25 * 10**8 * steps, bytes_accessed=steps << 20, transcendentals=steps << 21
         ),
         name="home_heat",
-    )(rows, rows, fw, weights, flux)
+    )(rows, rows, radial_step, far_weights[None], flux_weights[None])
 
 
 DEP_N = GROUP
@@ -470,17 +484,16 @@
         ],
         out_specs=field,
         scratch_shapes=[pltpu.VMEM((ROWS, 256), F32)],
-        compiler_params=pltpu.CompilerParams(vmem_limit_bytes=40 * 2**20),
+        compiler_params=pltpu.CompilerParams(vmem_limit_bytes=ROOM),
         cost_estimate=pl.CostEstimate(flops=10**10, bytes_accessed=4 << 20, transcendentals=0),
         name="deposit",
     )(lanes, heat, cells, velocity, diffusivity, wall_flux, below, above)
 
 
-def span_kernel(new_ref, dif_ref, left_ref, right_ref, out_ref):
+def span_term(ends):
     row8, lane = iota((8, ROWS), 0), iota((8, 128), 1)
     terms = jnp.zeros((8, ROWS), F32)
-    for i, ref in enumerate((left_ref, right_ref)):
-        rest = ref[...]
+    for i, rest in enumerate(ends):
         for k in range(3):
             high = rest.astype(BF16).astype(F32)
             terms = jnp.where(row8 == 3 * i + k, high, terms)
@@ -488,27 +501,16 @@
     row = iota((8, 128), 0)
     first, last = (row < 3) & (lane == 0), (row >= 3) & (row < 6) & (lane == 127)
     pick = jnp.where(first | last, 1.0, 0.0).astype(BF16)
-    ends = lax.dot_general(terms.astype(BF16), pick, (((0,), (0,)), ((), ())), preferred_element_type=F32)
-    out_ref[...] = new_ref[...] + dif_ref[...] * ends
-
-
-def add_span(new, diffusivity, left, right):
-    vmem = pl.BlockSpec(memory_space=pltpu.VMEM)
-    return pl.pallas_call(
-        span_kernel,
-        out_shape=jax.ShapeDtypeStruct((ROWS, 128), F32),
-        in_specs=[vmem] * 4,
-        out_specs=vmem,
-        cost_estimate=pl.CostEstimate(flops=10**7, bytes_accessed=2 << 20, transcendentals=0),
-        name="span",
-    )(new, diffusivity, left, right)
+    return lax.dot_general(
+        terms.astype(BF16), pick, (((0,), (0,)), ((), ())), preferred_element_type=F32
+    )
 
 
 SETTLE = 1024
 
 
 def settle_kernel(
-    rows_ref, fw_ref, weights_ref, out_ref,
+    rows_ref, fw_ref, weights_ref, new_ref, dif_ref, left_ref, right_ref, out_ref, field_ref,
     stage, comb, got, got_sem, side, side_sem, slot_v, slot_s, slot_sem, amount_v, amount_s, amount_sem,
     out_v, out_sem,
 ):
@@ -521,6 +523,7 @@
 
     for g in range(NT // GROUP):
         fetch(g).start()
+    field_ref[...] = new_ref[...] + dif_ref[...] * span_term((left_ref[...], right_ref[...]))
     fetch_side.wait()
     for t in range(NT):
         slot_v[4 * t : 4 * t + 4] = side[t, 0:4].astype(I32)
@@ -576,7 +579,7 @@
                 move(last, range(lane, lane + 32))
 
     weights = weights_ref[...]
-    fw = fw_ref[...]
+    fw = twice(fw_ref[...])
     low_lanes = iota((SETTLE, 128), 1) < 64
 
     def send(c, h):
@@ -602,13 +605,13 @@
             send(c, h).wait()
 
 
-def settle(rows, fw, weights):
+def settle(rows, far_weights, weights, new, diffusivity, left, right):
     vmem = pl.BlockSpec(memory_space=pltpu.VMEM)
     return pl.pallas_call(
         settle_kernel,
-        out_shape=jax.ShapeDtypeStruct((PTS, OWN), F32),
-        in_specs=[pl.BlockSpec(memory_space=pl.ANY), vmem, vmem],
-        out_specs=pl.BlockSpec(memory_space=pl.ANY),
+        out_shape=(jax.ShapeDtypeStruct((PTS, OWN), F32), jax.ShapeDtypeStruct((ROWS, 128), F32)),
+        in_specs=[pl.BlockSpec(memory_space=pl.ANY)] + [vmem] * 6,
+        out_specs=(pl.BlockSpec(memory_space=pl.ANY), vmem),
         scratch_shapes=[
             pltpu.VMEM((OWN + 8, 128), F32),
             pltpu.VMEM((NT * MSG, 128), F32),
@@ -627,10 +630,10 @@
         ],
         compiler_params=pltpu.CompilerParams(vmem_limit_bytes=ROOM),
         name="settle",
-    )(rows, fw, weights)
-
-
-def edges_of(cells, ends):
+    )(rows, far_weights[None], weights, new, diffusivity, left, right)
+
+
+def edges_of(cells, first, last):
     n_x, n_s = lax.axis_size("stream"), lax.axis_size("tile")
     up_x = [(i, i + 1) for i in range(n_x - 1)]
     down_x = [(i + 1, i) for i in range(n_x - 1)]
@@ -638,8 +641,8 @@
     down_s = [((i + 1) % n_s, i) for i in range(n_s)]
     below = lax.ppermute(cells[-1], "stream", up_x)
     above = lax.ppermute(cells[0], "stream", down_x)
-    left = lax.ppermute(ends[1:2], "tile", up_s)
-    right = lax.ppermute(ends[0:1], "tile", down_s)
+    left = lax.ppermute(last, "tile", up_s)
+    right = lax.ppermute(first, "tile", down_s)
     return below, above, left, right
 
 
@@ -648,21 +651,18 @@
     radial_step, far_weights, flux_weights,
 ):
     table = enthalpy.reshape(ROWS, 128)
-    rows, lanes, ends = route(counts, owners, cells, table, profiles)
+    rows, lanes, first, last = route(counts, owners, cells, table, profiles)
     rows, radial_step, far_weights, flux_weights = lax.optimization_barrier(
         (rows, radial_step, far_weights, flux_weights)
     )
-    weights = step_weights(radial_step)
-    fw = jnp.concatenate([far_weights, far_weights])[None, :]
-    flux = flux_rows(flux_weights)
     got = lax.all_to_all(rows, "tile", split_axis=0, concat_axis=0, tiled=True)
-    layers, ends = lax.optimization_barrier((enthalpy, ends))
-    heat = home_heat(rows, fw, weights, flux)
-    below, above, left, right = edges_of(layers, ends)
+    layers, first, last = lax.optimization_barrier((enthalpy, first, last))
+    heat, weights = home_heat(rows, radial_step, far_weights, flux_weights)
+    below, above, left, right = edges_of(layers, first, last)
     spread = diffusivity.reshape(ROWS, 128)
     new = deposit(lanes, heat, table, velocity.reshape(ROWS, 128), spread, wall_flux, below, above)
-    new_enthalpy = add_span(new, spread, left, right).reshape(enthalpy.shape)
-    new_profiles = settle(got, fw, weights)
+    new_profiles, field = settle(got, far_weights, weights, new, spread, left, right)
+    new_enthalpy = field.reshape(enthalpy.shape)
     return new_enthalpy, new_profiles
 
 

time: 116 us -> 116 us (level)
  starting transfers between devices: 15.2 us -> 18.2 us
  other arithmetic: 2.04 us -> 0 us
  local copies, waits for them, and re-layouts: 3.52 us -> 1.97 us
  Pallas kernels: 89.4 us -> 88.1 us
    pallas_call x1, Pallas kernels: 29.4 us -> 26.3 us  [route(): pl.pallas_call(route_kernel, out_shape=(jax.ShapeDtypeStruct((NT, LOAD, 1...]
    all_to_all x1, starting transfers between devices: 7.85 us -> 10.8 us  [on_device(): got = lax.all_to_all(rows, 'tile', split_axis=0, concat_axis=0, tiled=True)]
    pallas_call x1, Pallas kernels: 11.2 us -> 13.7 us  [deposit(): pl.pallas_call(deposit_kernel, grid=(NT // DEP_N,), out_shape=jax.ShapeDt...]
    unnamed x24 -> x12, local copies, waits for them, and re-layouts: 2.37 us -> 1.19 us
    pallas_call x3 -> x2, Pallas kernels: 48.8 us -> 48.1 us  [the longest x1 26 us: home_heat(): pl.pallas_call(heat_kernel, grid=(steps,), out_shape=(jax.ShapeDtypeStruc...]
  transfers between devices with their start and end apart: 5 -> 5, of which waited for: 1 -> 1; matrix products, arithmetic and copies ran while one was open for 3% -> 1% of each run, Pallas kernels for 34% -> 35%
where the time goes in v9:
time: 116 us; the launch traced here: 114 us
  Pallas kernels  88.1 us (76%)
  starting transfers between devices  18.2 us (16%)
  waiting for transfers between devices  3.88 us (3%)
  local copies, waits for them, and re-layouts  1.97 us (2%)
  between operations  1.55 us (1%)
    pallas_call x1, Pallas kernels, route(): pl.pallas_call(route_kernel, out_shape=(jax.ShapeDtypeStruct((NT, LOAD, 1...  26.3 us
    pallas_call x1, Pallas kernels, home_heat(): pl.pallas_call(heat_kernel, grid=(steps,), out_shape=(jax.ShapeDtypeStruc...  26 us
    pallas_call x1, Pallas kernels, settle(): pl.pallas_call(settle_kernel, out_shape=(jax.ShapeDtypeStruct((PTS, OWN),...  22 us
    pallas_call x1, Pallas kernels, deposit(): pl.pallas_call(deposit_kernel, grid=(NT // DEP_N,), out_shape=jax.ShapeDt...  13.7 us
    all_to_all x1, starting transfers between devices, on_device(): got = lax.all_to_all(rows, 'tile', split_axis=0, concat_axis=0, tiled=True)  10.8 us
    ppermute x1, waiting for transfers between devices, edges_of(): right = lax.ppermute(first, 'tile', down_s)  3.87 us
    ppermute x1, starting transfers between devices, edges_of(): below = lax.ppermute(cells[-1], 'stream', up_x)  3.23 us
  transfers between devices with their start and end apart: 5, of which 1 were waited for; matrix products, arithmetic and copies ran while one was open for 1% of the time, Pallas kernels for 35%

profile of v9, /device:TPU:35, one launch (start us, length us, event | category | flops | bytes accessed | tf_op | source)
XLA Modules:
  0.0 113.6 jit_solution(4313017375340427002)
XLA Ops:
  1.3 26.3 %route.1 = (f32[32,264,128]{2,1,0:T(8,128)}, f32[32,8,512]{2,1,0:T(8,128)}, f32[1,1024]{1,0:T(1,128)}, f32[1,1024]{1,0:T(1,128)}) custom-call(s32[1]{0:T(128)S(6)} %copy.13.count_ref, s32[128,128]{1,0:T(8,128)} %bitcast.16, s32[128,128]{1,0:T(8,128)} %bitcast.17, f32[1024,128]{1,0:T(8,128)} %bitcast.12, f32[64,16384]{1,0:T(8,128)} %prof_ref.1), custom_call_target="tpu_custom_call" | custom-call | tf_op jit(solution)/shard_map/route/pallas_call | solution.py:290
  27.6 0.0 copy-start.5
  27.6 0.0 copy-start.4
  27.6 10.8 %all-to-all-start = ((f32[32,264,128]{2,1,0:T(8,128)}), f32[32,264,128]{2,1,0:T(8,128)}, u32[]{:S(2)}, u32[]{:S(2)}) async-start(f32[32,264,128]{2,1,0:T(8,128)} %get-tuple-element.18.rows_ref.side_ref), calls=%async_computation | async-start | bytes 8650752 | tf_op jit(solution)/shard_map/all_to_all | solution.py:658
  38.5 0.8 slice_bitcast_fusion
  39.2 3.2 %collective-permute-start = (f32[64,128]{1,0:T(8,128)S(1)}, f32[64,128]{1,0:T(8,128)S(1)}, u32[]{:S(2)}, u32[]{:S(2)}) collective-permute-start(f32[64,128]{1,0:T(8,128)S(1)} %get-tuple-element.33), channel_id=1, source_target_pairs={{0,32},{32,64},{64,96},{1,33},{33,65},{65,97},{2,34},{34,66},{66,9... | collective-permute-start | bytes 98312 | tf_op jit(solution)/shard_map/ppermute | solution.py:642
  42.5 2.0 %collective-permute-start.1 = (f32[64,128]{1,0:T(8,128)S(1)}, f32[64,128]{1,0:T(8,128)S(1)}, u32[]{:S(2)}, u32[]{:S(2)}) collective-permute-start(f32[64,128]{1,0:T(8,128)S(1)} %get-tuple-element.32), channel_id=1, source_target_pairs={{32,0},{64,32},{96,64},{33,1},{65,33},{97,65},{34,2},{66,34},{98,6... | collective-permute-start | bytes 98312 | tf_op jit(solution)/shard_map/ppermute | solution.py:643
  44.5 0.0 copy-done.5
  44.5 2.1 %collective-permute-start.2 = (f32[1,1024]{1,0:T(1,128)S(1)}, f32[1,1024]{1,0:T(1,128)S(1)}, u32[]{:S(2)}, u32[]{:S(2)}) collective-permute-start(f32[1,1024]{1,0:T(1,128)S(1)} %copy-done.5), channel_id=1, source_target_pairs={{0,1},{1,2},{2,3},{3,4},{4,5},{5,6},{6,7},{7,8},{8,9},{9,10},{10,1... | collective-permute-start | bytes 12296 | tf_op jit(solution)/shard_map/ppermute | solution.py:644
  46.6 0.0 copy-done.4
  46.6 0.0 collective-permute-start.3
  46.6 26.0 %home_heat.1 = (f32[32,8,256]{2,1,0:T(8,128)}, bf16[256,256]{1,0:T(8,128)(2,1)}) custom-call(f32[32,264,128]{2,1,0:T(8,128)} %get-tuple-element.18.rows_ref.side_ref, f32[32,264,128]{2,1,0:T(8,128)} %get-tuple-element.18.rows_ref.side_ref, f32[64,64]{1,0:T(8,128)} %radial_ref, f32[1,64]{1,0:T(1,128)} %bitcast.18, f32[1,64]{1,0:T(1,128)} %bitcast.22), custom_call_target="tpu_custom_call" | custom-call | flops 10000000000 | bytes 4194304 | tf_op jit(solution)/shard_map/home_heat/pallas_call | solution.py:388
  72.6 0.0 collective-permute-done.below_ref
  72.6 0.0 copy-start.2
  72.6 0.0 collective-permute-done.1.above_ref
  72.7 0.0 copy-start.3
  72.7 0.6 copy-done.2
  73.2 0.0 copy-done.3
  73.3 13.7 %deposit.1.new_ref = f32[1024,128]{1,0:T(8,128)} custom-call(f32[32,8,512]{2,1,0:T(8,128)} %get-tuple-element.23.lanes_ref, f32[32,8,256]{2,1,0:T(8,128)} %get-tuple-element.24.heat_ref, f32[1024,128]{1,0:T(8,128)} %bitcast.13, f32[1024,128]{1,0:T(8,128)} %bitcast.20, f32[1024,128]{1,0:T(8,128)} %bitcast.14, f32[16,128]{1,0:T(8,128)} %flux_ref.1, ...), custom_call_target="tpu_custom_call" | custom-call | flops 10000000000 | bytes 4194304 | tf_op jit(solution)/shard_map/deposit/pallas_call | solution.py:471
  87.0 0.0 collective-permute-done.2.left_ref
  87.0 0.0 copy-start
  87.0 3.9 %collective-permute-done.3.right_ref = f32[1,1024]{1,0:T(1,128)S(1)} collective-permute-done((f32[1,1024]{1,0:T(1,128)S(1)}, f32[1,1024]{1,0:T(1,128)S(1)}, u32[]{:S(2)}, u32[]{:S(2)}) %collective-permute-start.3) | collective-permute-done | bytes 4128 | tf_op jit(solution)/shard_map/ppermute | solution.py:645
  90.8 0.0 copy-start.1
  90.8 0.0 all-to-all-done.rows_ref
  90.8 0.0 copy-done
  90.8 0.6 copy-done.1
  91.4 22.0 %settle.1 = (f32[64,6144]{1,0:T(8,128)}, f32[1024,128]{1,0:T(8,128)}) custom-call(f32[32,264,128]{2,1,0:T(8,128)} %all-to-all-done.rows_ref, f32[1,64]{1,0:T(1,128)} %bitcast.19, bf16[256,256]{1,0:T(8,128)(2,1)} %get-tuple-element.22.weights_ref, f32[1024,128]{1,0:T(8,128)} %deposit.1.new_ref, f32[1024,128]{1,0:T(8,128)} %bitcast.15, f32[1,1024]{1,0:T(1,128)} %copy-done, ...), custom_call_target="tpu_custom_call" | custom-call | tf_op jit(solution)/shard_map/settle/pallas_call | solution.py:610
Async XLA Ops:
  27.6 16.9 %copy-start.5 = (f32[1,1024]{1,0:T(1,128)S(1)}, f32[1,1024]{1,0:T(1,128)}, u32[]{:S(2)}) copy-start(f32[1,1024]{1,0:T(1,128)} %get-tuple-element.28) | copy-start | bytes 12292
  27.6 19.0 %copy-start.4 = (f32[1,1024]{1,0:T(1,128)S(1)}, f32[1,1024]{1,0:T(1,128)}, u32[]{:S(2)}) copy-start(f32[1,1024]{1,0:T(1,128)} %get-tuple-element.29) | copy-start | bytes 12292
  27.6 63.2 %all-to-all-start = ((f32[32,264,128]{2,1,0:T(8,128)}), f32[32,264,128]{2,1,0:T(8,128)}, u32[]{:S(2)}, u32[]{:S(2)}) async-start(f32[32,264,128]{2,1,0:T(8,128)} %get-tuple-element.18.rows_ref.side_ref), calls=%async_computation | async-start | bytes 8650752 | tf_op jit(solution)/shard_map/all_to_all | solution.py:658
  39.2 33.4 %collective-permute-start = (f32[64,128]{1,0:T(8,128)S(1)}, f32[64,128]{1,0:T(8,128)S(1)}, u32[]{:S(2)}, u32[]{:S(2)}) collective-permute-start(f32[64,128]{1,0:T(8,128)S(1)} %get-tuple-element.33), channel_id=1, source_target_pairs={{0,32},{32,64},{64,96},{1,33},{33,65},{65,97},{2,34},{34,66},{66,9... | collective-permute-start | bytes 98312 | tf_op jit(solution)/shard_map/ppermute | solution.py:642
  42.5 30.2 %collective-permute-start.1 = (f32[64,128]{1,0:T(8,128)S(1)}, f32[64,128]{1,0:T(8,128)S(1)}, u32[]{:S(2)}, u32[]{:S(2)}) collective-permute-start(f32[64,128]{1,0:T(8,128)S(1)} %get-tuple-element.32), channel_id=1, source_target_pairs={{32,0},{64,32},{96,64},{33,1},{65,33},{97,65},{34,2},{66,34},{98,6... | collective-permute-start | bytes 98312 | tf_op jit(solution)/shard_map/ppermute | solution.py:643
  44.5 42.4 %collective-permute-start.2 = (f32[1,1024]{1,0:T(1,128)S(1)}, f32[1,1024]{1,0:T(1,128)S(1)}, u32[]{:S(2)}, u32[]{:S(2)}) collective-permute-start(f32[1,1024]{1,0:T(1,128)S(1)} %copy-done.5), channel_id=1, source_target_pairs={{0,1},{1,2},{2,3},{3,4},{4,5},{5,6},{6,7},{7,8},{8,9},{9,10},{10,1... | collective-permute-start | bytes 12296 | tf_op jit(solution)/shard_map/ppermute | solution.py:644
  46.6 44.2 %collective-permute-start.3 = (f32[1,1024]{1,0:T(1,128)S(1)}, f32[1,1024]{1,0:T(1,128)S(1)}, u32[]{:S(2)}, u32[]{:S(2)}) collective-permute-start(f32[1,1024]{1,0:T(1,128)S(1)} %copy-done.4), channel_id=1, source_target_pairs={{1,0},{2,1},{3,2},{4,3},{5,4},{6,5},{7,6},{8,7},{9,8},{10,9},{11,1... | collective-permute-start | bytes 12296 | tf_op jit(solution)/shard_map/ppermute | solution.py:645
  72.6 0.6 copy-start.2
  72.7 0.6 copy-start.3
  87.0 3.9 %copy-start = (f32[1,1024]{1,0:T(1,128)}, f32[1,1024]{1,0:T(1,128)S(1)}, u32[]{:S(2)}) copy-start(f32[1,1024]{1,0:T(1,128)S(1)} %collective-permute-done.2.left_ref) | copy-start | bytes 12292
  90.8 0.6 copy-start.1

commit v10 on v9

--- a/solution.py
+++ b/solution.py
@@ -484,7 +484,7 @@
         ],
         out_specs=field,
         scratch_shapes=[pltpu.VMEM((ROWS, 256), F32)],
-        compiler_params=pltpu.CompilerParams(vmem_limit_bytes=ROOM),
+        compiler_params=pltpu.CompilerParams(vmem_limit_bytes=40 * 2**20),
         cost_estimate=pl.CostEstimate(flops=10**10, bytes_accessed=4 << 20, transcendentals=0),
         name="deposit",
     )(lanes, heat, cells, velocity, diffusivity, wall_flux, below, above)
@@ -543,7 +543,7 @@
     for g in range(NT // GROUP):
         fetch(g).wait()
 
-    @pl.loop(0, NT // GROUP, unroll=2)
+    @pl.loop(0, NT // GROUP, unroll=4)
     def _(g):
         for k in range(GROUP):
             t = GROUP * g + k

time: 116 us -> 115 us (level)
  Pallas kernels: 88.1 us -> 85 us
  waiting for transfers between devices: 3.88 us -> 5.73 us
    pallas_call x1, Pallas kernels: 13.7 us -> 11.2 us  [deposit(): pl.pallas_call(deposit_kernel, grid=(NT // DEP_N,), out_shape=jax.ShapeDt...]
    ppermute x1, waiting for transfers between devices: 3.87 us -> 5.72 us  [edges_of(): right = lax.ppermute(first, 'tile', down_s)]
    unnamed x12 -> x22, local copies, waits for them, and re-layouts: 1.19 us -> 2.39 us
  transfers between devices with their start and end apart: 5 -> 5, of which waited for: 1 -> 1; matrix products, arithmetic and copies ran while one was open for 1% -> 0% of each run, Pallas kernels for 35% -> 33%
where the time goes in v10:
time: 115 us; the launch traced here: 113 us
  Pallas kernels  85 us (74%)
  starting transfers between devices  18.5 us (16%)
  waiting for transfers between devices  5.73 us (5%)
  local copies, waits for them, and re-layouts  2.4 us (2%)
  between operations  1.63 us (1%)
    pallas_call x1, Pallas kernels, home_heat(): pl.pallas_call(heat_kernel, grid=(steps,), out_shape=(jax.ShapeDtypeStruc...  26.2 us
    pallas_call x1, Pallas kernels, route(): pl.pallas_call(route_kernel, out_shape=(jax.ShapeDtypeStruct((NT, LOAD, 1...  25.9 us
    pallas_call x1, Pallas kernels, settle(): pl.pallas_call(settle_kernel, out_shape=(jax.ShapeDtypeStruct((PTS, OWN),...  21.7 us
    pallas_call x1, Pallas kernels, deposit(): pl.pallas_call(deposit_kernel, grid=(NT // DEP_N,), out_shape=jax.ShapeDt...  11.2 us
    all_to_all x1, starting transfers between devices, on_device(): got = lax.all_to_all(rows, 'tile', split_axis=0, concat_axis=0, tiled=True)  11.1 us
    ppermute x1, waiting for transfers between devices, edges_of(): right = lax.ppermute(first, 'tile', down_s)  5.72 us
    ppermute x1, starting transfers between devices, edges_of(): above = lax.ppermute(cells[0], 'stream', down_x)  2.83 us
    ppermute x1, starting transfers between devices, edges_of(): below = lax.ppermute(cells[-1], 'stream', up_x)  2.45 us
  transfers between devices with their start and end apart: 5, of which 1 were waited for; matrix products, arithmetic and copies ran while one was open for 0% of the time, Pallas kernels for 33%

profile of v10, /device:TPU:35, one launch (start us, length us, event | category | flops | bytes accessed | tf_op | source)
XLA Modules:
  0.0 113.2 jit_solution(15524149917702453194)
XLA Ops:
  1.3 25.9 %route.1 = (f32[32,264,128]{2,1,0:T(8,128)}, f32[32,8,512]{2,1,0:T(8,128)}, f32[1,1024]{1,0:T(1,128)}, f32[1,1024]{1,0:T(1,128)}) custom-call(s32[1]{0:T(128)S(6)} %copy.13.count_ref, s32[128,128]{1,0:T(8,128)} %bitcast.17, s32[128,128]{1,0:T(8,128)} %bitcast.18, f32[1024,128]{1,0:T(8,128)} %bitcast.12, f32[64,16384]{1,0:T(8,128)} %prof_ref.1), custom_call_target="tpu_custom_call" | custom-call | tf_op jit(solution)/shard_map/route/pallas_call | solution.py:290
  27.2 0.0 copy-start
  27.2 0.0 copy-start.10
  27.3 0.0 copy-start.9
  27.3 11.1 %all-to-all-start = ((f32[32,264,128]{2,1,0:T(8,128)}), f32[32,264,128]{2,1,0:T(8,128)}, u32[]{:S(2)}, u32[]{:S(2)}) async-start(f32[32,264,128]{2,1,0:T(8,128)} %get-tuple-element.18.rows_ref.side_ref), calls=%async_computation | async-start | bytes 8650752 | tf_op jit(solution)/shard_map/all_to_all | solution.py:658
  38.4 0.0 copy-done
  38.4 2.5 %collective-permute-start = (f32[64,128]{1,0:T(8,128)S(1)}, f32[64,128]{1,0:T(8,128)S(1)}, u32[]{:S(2)}, u32[]{:S(2)}) collective-permute-start(f32[64,128]{1,0:T(8,128)S(1)} %get-tuple-element.33), channel_id=1, source_target_pairs={{0,32},{32,64},{64,96},{1,33},{33,65},{65,97},{2,34},{34,66},{66,9... | collective-permute-start | bytes 98312 | tf_op jit(solution)/shard_map/ppermute | solution.py:642
  40.9 2.8 %collective-permute-start.1 = (f32[64,128]{1,0:T(8,128)S(1)}, f32[64,128]{1,0:T(8,128)S(1)}, u32[]{:S(2)}, u32[]{:S(2)}) collective-permute-start(f32[64,128]{1,0:T(8,128)S(1)} %get-tuple-element.32), channel_id=1, source_target_pairs={{32,0},{64,32},{96,64},{33,1},{65,33},{97,65},{34,2},{66,34},{98,6... | collective-permute-start | bytes 98312 | tf_op jit(solution)/shard_map/ppermute | solution.py:643
  43.7 0.0 copy-done.10
  43.7 2.1 %collective-permute-start.2 = (f32[1,1024]{1,0:T(1,128)S(1)}, f32[1,1024]{1,0:T(1,128)S(1)}, u32[]{:S(2)}, u32[]{:S(2)}) collective-permute-start(f32[1,1024]{1,0:T(1,128)S(1)} %copy-done.10), channel_id=1, source_target_pairs={{0,1},{1,2},{2,3},{3,4},{4,5},{5,6},{6,7},{7,8},{8,9},{9,10},{10,1... | collective-permute-start | bytes 12296 | tf_op jit(solution)/shard_map/ppermute | solution.py:644
  45.8 0.0 copy-done.9
  45.8 0.0 collective-permute-start.3
  45.8 0.0 copy-start.3
  45.8 0.0 copy-start.4
  45.8 0.0 copy-start.5
  45.9 26.2 %home_heat.1 = (f32[32,8,256]{2,1,0:T(8,128)}, bf16[256,256]{1,0:T(8,128)(2,1)}) custom-call(f32[32,264,128]{2,1,0:T(8,128)} %get-tuple-element.18.rows_ref.side_ref, f32[32,264,128]{2,1,0:T(8,128)} %get-tuple-element.18.rows_ref.side_ref, f32[64,64]{1,0:T(8,128)} %radial_ref, f32[1,64]{1,0:T(1,128)} %bitcast.19, f32[1,64]{1,0:T(1,128)} %bitcast.22), custom_call_target="tpu_custom_call" | custom-call | flops 10000000000 | bytes 4194304 | tf_op jit(solution)/shard_map/home_heat/pallas_call | solution.py:388
  72.0 0.0 collective-permute-done.below_ref
  72.0 0.0 collective-permute-done.1.above_ref
  72.0 0.0 copy-done.1
  72.0 0.0 copy-done.3
  72.0 0.0 copy-done.4
  72.1 0.0 copy-done.5
  72.1 0.0 copy-start.6
  72.1 0.9 copy-done.6
  73.0 11.2 %deposit.1.new_ref = f32[1024,128]{1,0:T(8,128)S(1)} custom-call(f32[32,8,512]{2,1,0:T(8,128)S(1)} %copy-done.4, f32[32,8,256]{2,1,0:T(8,128)S(1)} %copy-done.6, f32[1024,128]{1,0:T(8,128)S(1)} %bitcast.13, f32[1024,128]{1,0:T(8,128)S(1)} %bitcast.16, f32[1024,128]{1,0:T(8,128)S(1)} %bitcast.15, f32[16,128]{1,0:T(8,128)S(1)} %copy-done.5, ...), custom_call_target="tpu_custom_call" | custom-call | flops 10000000000 | bytes 4194304 | tf_op jit(solution)/shard_map/deposit/pallas_call | solution.py:471
  84.2 0.0 copy-start.2
  84.2 0.8 copy-done.2
  85.1 0.0 collective-permute-done.2.left_ref
  85.1 5.7 %collective-permute-done.3.right_ref = f32[1,1024]{1,0:T(1,128)S(1)} collective-permute-done((f32[1,1024]{1,0:T(1,128)S(1)}, f32[1,1024]{1,0:T(1,128)S(1)}, u32[]{:S(2)}, u32[]{:S(2)}) %collective-permute-start.3) | collective-permute-done | bytes 4128 | tf_op jit(solution)/shard_map/ppermute | solution.py:645
  90.8 0.0 all-to-all-done.rows_ref
  90.8 0.6 copy-done.8
  91.4 21.7 %settle.1 = (f32[64,6144]{1,0:T(8,128)}, f32[1024,128]{1,0:T(8,128)}) custom-call(f32[32,264,128]{2,1,0:T(8,128)} %all-to-all-done.rows_ref, f32[1,64]{1,0:T(1,128)} %bitcast.20, bf16[256,256]{1,0:T(8,128)(2,1)} %get-tuple-element.22.weights_ref, f32[1024,128]{1,0:T(8,128)} %copy-done.2, f32[1024,128]{1,0:T(8,128)} %bitcast.14, f32[1,1024]{1,0:T(1,128)} %copy-done.7, ...), custom_call_target="tpu_custom_call" | custom-call | tf_op jit(solution)/shard_map/settle/pallas_call | solution.py:610
  (5 shorter events, 0.0 us)
Async XLA Ops:
  27.2 11.2 %copy-start = (f32[16,64,128]{2,1,0:T(8,128)S(1)}, f32[16,64,128]{2,1,0:T(8,128)}, u32[]{:S(2)}) copy-start(f32[16,64,128]{2,1,0:T(8,128)} %param.11) | copy-start | bytes 1572868
  27.2 16.5 %copy-start.10 = (f32[1,1024]{1,0:T(1,128)S(1)}, f32[1,1024]{1,0:T(1,128)}, u32[]{:S(2)}) copy-start(f32[1,1024]{1,0:T(1,128)} %get-tuple-element.28) | copy-start | bytes 12292
  27.3 18.6 %copy-start.9 = (f32[1,1024]{1,0:T(1,128)S(1)}, f32[1,1024]{1,0:T(1,128)}, u32[]{:S(2)}) copy-start(f32[1,1024]{1,0:T(1,128)} %get-tuple-element.29) | copy-start | bytes 12292
  27.3 63.5 %all-to-all-start = ((f32[32,264,128]{2,1,0:T(8,128)}), f32[32,264,128]{2,1,0:T(8,128)}, u32[]{:S(2)}, u32[]{:S(2)}) async-start(f32[32,264,128]{2,1,0:T(8,128)} %get-tuple-element.18.rows_ref.side_ref), calls=%async_computation | async-start | bytes 8650752 | tf_op jit(solution)/shard_map/all_to_all | solution.py:658
  38.4 33.6 %collective-permute-start = (f32[64,128]{1,0:T(8,128)S(1)}, f32[64,128]{1,0:T(8,128)S(1)}, u32[]{:S(2)}, u32[]{:S(2)}) collective-permute-start(f32[64,128]{1,0:T(8,128)S(1)} %get-tuple-element.33), channel_id=1, source_target_pairs={{0,32},{32,64},{64,96},{1,33},{33,65},{65,97},{2,34},{34,66},{66,9... | collective-permute-start | bytes 98312 | tf_op jit(solution)/shard_map/ppermute | solution.py:642
  40.9 31.1 %collective-permute-start.1 = (f32[64,128]{1,0:T(8,128)S(1)}, f32[64,128]{1,0:T(8,128)S(1)}, u32[]{:S(2)}, u32[]{:S(2)}) collective-permute-start(f32[64,128]{1,0:T(8,128)S(1)} %get-tuple-element.32), channel_id=1, source_target_pairs={{32,0},{64,32},{96,64},{33,1},{65,33},{97,65},{34,2},{66,34},{98,6... | collective-permute-start | bytes 98312 | tf_op jit(solution)/shard_map/ppermute | solution.py:643
  43.7 41.3 %collective-permute-start.2 = (f32[1,1024]{1,0:T(1,128)S(1)}, f32[1,1024]{1,0:T(1,128)S(1)}, u32[]{:S(2)}, u32[]{:S(2)}) collective-permute-start(f32[1,1024]{1,0:T(1,128)S(1)} %copy-done.10), channel_id=1, source_target_pairs={{0,1},{1,2},{2,3},{3,4},{4,5},{5,6},{6,7},{7,8},{8,9},{9,10},{10,1... | collective-permute-start | bytes 12296 | tf_op jit(solution)/shard_map/ppermute | solution.py:644
  45.8 45.0 %collective-permute-start.3 = (f32[1,1024]{1,0:T(1,128)S(1)}, f32[1,1024]{1,0:T(1,128)S(1)}, u32[]{:S(2)}, u32[]{:S(2)}) collective-permute-start(f32[1,1024]{1,0:T(1,128)S(1)} %copy-done.9), channel_id=1, source_target_pairs={{1,0},{2,1},{3,2},{4,3},{5,4},{6,5},{7,6},{8,7},{9,8},{10,9},{11,1... | collective-permute-start | bytes 12296 | tf_op jit(solution)/shard_map/ppermute | solution.py:645
  45.8 26.2 %copy-start.1 = (f32[16,64,128]{2,1,0:T(8,128)S(1)}, f32[16,64,128]{2,1,0:T(8,128)}, u32[]{:S(2)}) copy-start(f32[16,64,128]{2,1,0:T(8,128)} %param.13) | copy-start | bytes 1572868
  45.8 26.2 %copy-start.3 = (f32[16,64,128]{2,1,0:T(8,128)S(1)}, f32[16,64,128]{2,1,0:T(8,128)}, u32[]{:S(2)}) copy-start(f32[16,64,128]{2,1,0:T(8,128)} %param.12) | copy-start | bytes 1572868
  45.8 26.2 %copy-start.4 = (f32[32,8,512]{2,1,0:T(8,128)S(1)}, f32[32,8,512]{2,1,0:T(8,128)}, u32[]{:S(2)}) copy-start(f32[32,8,512]{2,1,0:T(8,128)} %get-tuple-element.23.lanes_ref) | copy-start | bytes 1572868
  45.8 26.2 %copy-start.5 = (f32[16,128]{1,0:T(8,128)S(1)}, f32[16,128]{1,0:T(8,128)}, u32[]{:S(2)}) copy-start(f32[16,128]{1,0:T(8,128)} %flux_ref.1) | copy-start | bytes 24580
  72.1 1.0 copy-start.6
  84.2 0.8 copy-start.2
  85.1 5.7 %copy-start.7 = (f32[1,1024]{1,0:T(1,128)}, f32[1,1024]{1,0:T(1,128)S(1)}, u32[]{:S(2)}) copy-start(f32[1,1024]{1,0:T(1,128)S(1)} %collective-permute-done.2.left_ref) | copy-start | bytes 12292
  90.8 0.6 copy-start.8

commit v11 on v10

--- a/solution.py
+++ b/solution.py
@@ -506,7 +506,7 @@
     )
 
 
-SETTLE = 1024
+SETTLE = 1536
 
 
 def settle_kernel(

time: 115 us -> 116 us (level)
  the two profiles are of different devices: /device:TPU:35 before, /device:TPU:96 now
where the time goes in v11:
time: 116 us; the launch traced here: 115 us
  Pallas kernels  84.7 us (73%)
  starting transfers between devices  22.1 us (19%)
  waiting for transfers between devices  4.91 us (4%)
  local copies, waits for them, and re-layouts  1.82 us (2%)
  between operations  1.63 us (1%)
    pallas_call x1, Pallas kernels, home_heat(): pl.pallas_call(heat_kernel, grid=(steps,), out_shape=(jax.ShapeDtypeStruc...  26.2 us
    pallas_call x1, Pallas kernels, route(): pl.pallas_call(route_kernel, out_shape=(jax.ShapeDtypeStruct((NT, LOAD, 1...  25.6 us
    pallas_call x1, Pallas kernels, settle(): pl.pallas_call(settle_kernel, out_shape=(jax.ShapeDtypeStruct((PTS, OWN),...  21.8 us
    pallas_call x1, Pallas kernels, deposit(): pl.pallas_call(deposit_kernel, grid=(NT // DEP_N,), out_shape=jax.ShapeDt...  11.2 us
    all_to_all x1, starting transfers between devices, on_device(): got = lax.all_to_all(rows, 'tile', split_axis=0, concat_axis=0, tiled=True)  11.1 us
    ppermute x1, starting transfers between devices, edges_of(): right = lax.ppermute(first, 'tile', down_s)  5.05 us
    all_to_all x1, waiting for transfers between devices, on_device(): got = lax.all_to_all(rows, 'tile', split_axis=0, concat_axis=0, tiled=True)  4.9 us
    ppermute x1, starting transfers between devices, edges_of(): above = lax.ppermute(cells[0], 'stream', down_x)  4.55 us
  transfers between devices with their start and end apart: 5, of which 1 were waited for; matrix products, arithmetic and copies ran while one was open for 0% of the time, Pallas kernels for 32%

profile of v11, /device:TPU:96, one launch (start us, length us, event | category | flops | bytes accessed | tf_op | source)
XLA Modules:
  0.0 115.1 jit_solution(13257528487699732704)
XLA Ops:
  1.3 25.6 %route.1 = (f32[32,264,128]{2,1,0:T(8,128)}, f32[32,8,512]{2,1,0:T(8,128)}, f32[1,1024]{1,0:T(1,128)}, f32[1,1024]{1,0:T(1,128)}) custom-call(s32[1]{0:T(128)S(6)} %copy.13.count_ref, s32[128,128]{1,0:T(8,128)} %bitcast.17, s32[128,128]{1,0:T(8,128)} %bitcast.18, f32[1024,128]{1,0:T(8,128)} %bitcast.12, f32[64,16384]{1,0:T(8,128)} %prof_ref.1), custom_call_target="tpu_custom_call" | custom-call | tf_op jit(solution)/shard_map/route/pallas_call | solution.py:290
  26.9 0.0 copy-start
  26.9 0.0 copy-start.10
  26.9 0.0 copy-start.9
  26.9 11.1 %all-to-all-start = ((f32[32,264,128]{2,1,0:T(8,128)}), f32[32,264,128]{2,1,0:T(8,128)}, u32[]{:S(2)}, u32[]{:S(2)}) async-start(f32[32,264,128]{2,1,0:T(8,128)} %get-tuple-element.18.rows_ref.side_ref), calls=%async_computation | async-start | bytes 8650752 | tf_op jit(solution)/shard_map/all_to_all | solution.py:658
  38.0 0.0 copy-done
  38.1 1.3 %collective-permute-start = (f32[64,128]{1,0:T(8,128)S(1)}, f32[64,128]{1,0:T(8,128)S(1)}, u32[]{:S(2)}, u32[]{:S(2)}) collective-permute-start(f32[64,128]{1,0:T(8,128)S(1)} %get-tuple-element.33), channel_id=1, source_target_pairs={{0,32},{32,64},{64,96},{1,33},{33,65},{65,97},{2,34},{34,66},{66,9... | collective-permute-start | bytes 98312 | tf_op jit(solution)/shard_map/ppermute | solution.py:642
  39.4 4.5 %collective-permute-start.1 = (f32[64,128]{1,0:T(8,128)S(1)}, f32[64,128]{1,0:T(8,128)S(1)}, u32[]{:S(2)}, u32[]{:S(2)}) collective-permute-start(f32[64,128]{1,0:T(8,128)S(1)} %get-tuple-element.32), channel_id=1, source_target_pairs={{32,0},{64,32},{96,64},{33,1},{65,33},{97,65},{34,2},{66,34},{98,6... | collective-permute-start | bytes 98312 | tf_op jit(solution)/shard_map/ppermute | solution.py:643
  43.9 0.0 copy-done.10
  43.9 0.1 collective-permute-start.2
  44.0 0.0 copy-done.9
  44.0 5.0 %collective-permute-start.3 = (f32[1,1024]{1,0:T(1,128)S(1)}, f32[1,1024]{1,0:T(1,128)S(1)}, u32[]{:S(2)}, u32[]{:S(2)}) collective-permute-start(f32[1,1024]{1,0:T(1,128)S(1)} %copy-done.9), channel_id=1, source_target_pairs={{1,0},{2,1},{3,2},{4,3},{5,4},{6,5},{7,6},{8,7},{9,8},{10,9},{11,1... | collective-permute-start | bytes 12296 | tf_op jit(solution)/shard_map/ppermute | solution.py:645
  49.1 0.0 copy-start.1
  49.1 26.2 %home_heat.1 = (f32[32,8,256]{2,1,0:T(8,128)}, bf16[256,256]{1,0:T(8,128)(2,1)}) custom-call(f32[32,264,128]{2,1,0:T(8,128)} %get-tuple-element.18.rows_ref.side_ref, f32[32,264,128]{2,1,0:T(8,128)} %get-tuple-element.18.rows_ref.side_ref, f32[64,64]{1,0:T(8,128)} %radial_ref, f32[1,64]{1,0:T(1,128)} %bitcast.19, f32[1,64]{1,0:T(1,128)} %bitcast.22), custom_call_target="tpu_custom_call" | custom-call | flops 10000000000 | bytes 4194304 | tf_op jit(solution)/shard_map/home_heat/pallas_call | solution.py:388
  75.2 0.0 collective-permute-done.below_ref
  75.2 0.0 collective-permute-done.1.above_ref
  75.2 0.0 copy-done.1
  75.3 0.0 copy-done.3
  75.3 0.0 copy-done.4
  75.3 0.0 copy-done.5
  75.3 0.0 copy-start.6
  75.3 0.9 copy-done.6
  76.2 11.2 %deposit.1.new_ref = f32[1024,128]{1,0:T(8,128)S(1)} custom-call(f32[32,8,512]{2,1,0:T(8,128)S(1)} %copy-done.4, f32[32,8,256]{2,1,0:T(8,128)S(1)} %copy-done.6, f32[1024,128]{1,0:T(8,128)S(1)} %bitcast.13, f32[1024,128]{1,0:T(8,128)S(1)} %bitcast.16, f32[1024,128]{1,0:T(8,128)S(1)} %bitcast.15, f32[16,128]{1,0:T(8,128)S(1)} %copy-done.5, ...), custom_call_target="tpu_custom_call" | custom-call | flops 10000000000 | bytes 4194304 | tf_op jit(solution)/shard_map/deposit/pallas_call | solution.py:471
  87.4 0.0 copy-start.2
  87.5 0.8 copy-done.2
  88.3 0.0 collective-permute-done.2.left_ref
  88.3 0.0 collective-permute-done.3.right_ref
  88.3 0.0 copy-start.8
  88.3 4.9 %all-to-all-done.rows_ref = f32[32,264,128]{2,1,0:T(8,128)} async-done(((f32[32,264,128]{2,1,0:T(8,128)}), f32[32,264,128]{2,1,0:T(8,128)}, u32[]{:S(2)}, u32[]{:S(2)}) %all-to-all-start) | async-done | bytes 4325408 | tf_op jit(solution)/shard_map/all_to_all | solution.py:658
  93.2 0.0 copy-done.7
  93.2 0.0 copy-done.8
  93.2 21.8 %settle.1 = (f32[64,6144]{1,0:T(8,128)}, f32[1024,128]{1,0:T(8,128)}) custom-call(f32[32,264,128]{2,1,0:T(8,128)} %all-to-all-done.rows_ref, f32[1,64]{1,0:T(1,128)} %bitcast.20, bf16[256,256]{1,0:T(8,128)(2,1)} %get-tuple-element.22.weights_ref, f32[1024,128]{1,0:T(8,128)} %copy-done.2, f32[1024,128]{1,0:T(8,128)} %bitcast.14, f32[1,1024]{1,0:T(1,128)} %copy-done.7, ...), custom_call_target="tpu_custom_call" | custom-call | tf_op jit(solution)/shard_map/settle/pallas_call | solution.py:610
  (5 shorter events, 0.0 us)
Async XLA Ops:
  26.9 11.2 %copy-start = (f32[16,64,128]{2,1,0:T(8,128)S(1)}, f32[16,64,128]{2,1,0:T(8,128)}, u32[]{:S(2)}) copy-start(f32[16,64,128]{2,1,0:T(8,128)} %param.11) | copy-start | bytes 1572868
  26.9 17.0 %copy-start.10 = (f32[1,1024]{1,0:T(1,128)S(1)}, f32[1,1024]{1,0:T(1,128)}, u32[]{:S(2)}) copy-start(f32[1,1024]{1,0:T(1,128)} %get-tuple-element.28) | copy-start | bytes 12292
  26.9 17.1 %copy-start.9 = (f32[1,1024]{1,0:T(1,128)S(1)}, f32[1,1024]{1,0:T(1,128)}, u32[]{:S(2)}) copy-start(f32[1,1024]{1,0:T(1,128)} %get-tuple-element.29) | copy-start | bytes 12292
  26.9 66.3 %all-to-all-start = ((f32[32,264,128]{2,1,0:T(8,128)}), f32[32,264,128]{2,1,0:T(8,128)}, u32[]{:S(2)}, u32[]{:S(2)}) async-start(f32[32,264,128]{2,1,0:T(8,128)} %get-tuple-element.18.rows_ref.side_ref), calls=%async_computation | async-start | bytes 8650752 | tf_op jit(solution)/shard_map/all_to_all | solution.py:658
  38.1 37.2 %collective-permute-start = (f32[64,128]{1,0:T(8,128)S(1)}, f32[64,128]{1,0:T(8,128)S(1)}, u32[]{:S(2)}, u32[]{:S(2)}) collective-permute-start(f32[64,128]{1,0:T(8,128)S(1)} %get-tuple-element.33), channel_id=1, source_target_pairs={{0,32},{32,64},{64,96},{1,33},{33,65},{65,97},{2,34},{34,66},{66,9... | collective-permute-start | bytes 98312 | tf_op jit(solution)/shard_map/ppermute | solution.py:642
  39.4 35.9 %collective-permute-start.1 = (f32[64,128]{1,0:T(8,128)S(1)}, f32[64,128]{1,0:T(8,128)S(1)}, u32[]{:S(2)}, u32[]{:S(2)}) collective-permute-start(f32[64,128]{1,0:T(8,128)S(1)} %get-tuple-element.32), channel_id=1, source_target_pairs={{32,0},{64,32},{96,64},{33,1},{65,33},{97,65},{34,2},{66,34},{98,6... | collective-permute-start | bytes 98312 | tf_op jit(solution)/shard_map/ppermute | solution.py:643
  43.9 44.3 %collective-permute-start.2 = (f32[1,1024]{1,0:T(1,128)S(1)}, f32[1,1024]{1,0:T(1,128)S(1)}, u32[]{:S(2)}, u32[]{:S(2)}) collective-permute-start(f32[1,1024]{1,0:T(1,128)S(1)} %copy-done.10), channel_id=1, source_target_pairs={{0,1},{1,2},{2,3},{3,4},{4,5},{5,6},{6,7},{7,8},{8,9},{9,10},{10,1... | collective-permute-start | bytes 12296 | tf_op jit(solution)/shard_map/ppermute | solution.py:644
  44.0 44.3 %collective-permute-start.3 = (f32[1,1024]{1,0:T(1,128)S(1)}, f32[1,1024]{1,0:T(1,128)S(1)}, u32[]{:S(2)}, u32[]{:S(2)}) collective-permute-start(f32[1,1024]{1,0:T(1,128)S(1)} %copy-done.9), channel_id=1, source_target_pairs={{1,0},{2,1},{3,2},{4,3},{5,4},{6,5},{7,6},{8,7},{9,8},{10,9},{11,1... | collective-permute-start | bytes 12296 | tf_op jit(solution)/shard_map/ppermute | solution.py:645
  49.1 26.2 %copy-start.1 = (f32[16,64,128]{2,1,0:T(8,128)S(1)}, f32[16,64,128]{2,1,0:T(8,128)}, u32[]{:S(2)}) copy-start(f32[16,64,128]{2,1,0:T(8,128)} %param.13) | copy-start | bytes 1572868
  49.1 26.2 %copy-start.3 = (f32[16,64,128]{2,1,0:T(8,128)S(1)}, f32[16,64,128]{2,1,0:T(8,128)}, u32[]{:S(2)}) copy-start(f32[16,64,128]{2,1,0:T(8,128)} %param.12) | copy-start | bytes 1572868
  49.1 26.2 %copy-start.4 = (f32[32,8,512]{2,1,0:T(8,128)S(1)}, f32[32,8,512]{2,1,0:T(8,128)}, u32[]{:S(2)}) copy-start(f32[32,8,512]{2,1,0:T(8,128)} %get-tuple-element.23.lanes_ref) | copy-start | bytes 1572868
  49.1 26.2 %copy-start.5 = (f32[16,128]{1,0:T(8,128)S(1)}, f32[16,128]{1,0:T(8,128)}, u32[]{:S(2)}) copy-start(f32[16,128]{1,0:T(8,128)} %flux_ref.1) | copy-start | bytes 24580
  75.3 1.0 copy-start.6
  87.4 0.8 copy-start.2
  88.3 4.9 %copy-start.7 = (f32[1,1024]{1,0:T(1,128)}, f32[1,1024]{1,0:T(1,128)S(1)}, u32[]{:S(2)}) copy-start(f32[1,1024]{1,0:T(1,128)S(1)} %collective-permute-done.2.left_ref) | copy-start | bytes 12292
  88.3 4.9 %copy-start.8 = (f32[1,1024]{1,0:T(1,128)}, f32[1,1024]{1,0:T(1,128)S(1)}, u32[]{:S(2)}) copy-start(f32[1,1024]{1,0:T(1,128)S(1)} %collective-permute-done.3.right_ref) | copy-start | bytes 12292
